TPU v7x, 128 devices: a whole 4x4x4 slice. The times are simulated.
128 devices in a mesh: tx: 8 (over z, core), ty: 16 (over x, y).
Axes of the slice: x: 4, y: 4, z: 4, core: 2. Of those that a mesh axis runs over, the one named last changes fastest.
Arguments:
- voxels: bfloat16 [524288, 128], P(('tx', 'ty')), may hold values from 0 to 9
- owner_tile: int32 [524288, 1], P(('tx', 'ty')), may hold values from 0 to 127; in each aligned block of 4096 rows (0 to 4095, 4096 to 8191, ...) at most 64 rows name the same one
- rim_blocks: int32 [128, 4, 16], P(('tx', 'ty')), may hold values from 0 to 127
- kernel_map: int32 [128, 27, 8192], P(('tx', 'ty')), may hold values from -1 to 12287, as said below
- weights: bfloat16 [27, 128, 128], replicated, may hold values from -0.109375 to 0.109375
- norm_gain: float32 [128], replicated, may hold values from 0.1 to 1.9
- shift_bias: float32 [128], replicated, may hold values from -3 to 3
Outputs:
- normalized: bfloat16 [1048576, 128], P(('tx', 'ty'))
Inputs may be any that keep to these rules, and one draw needn't show every extreme that they name: `owner_tile`: at most 64 of one device's 4096 rows name one tile, and in every draw some device's rows name some tile exactly 64 times. `kernel_map`: for each tile, offset and aligned block of 64 output slots, all entries other than -1 lie in one block of the extended rows. The middle offset maps every slot to itself.
All inputs are finite; a program needn't handle non-finite values.
Results may differ from a plain program's by a relative error of at most 0.0004.
Values may be sent and summed in bfloat16 or wider, within the bound.
No kernel may reach another device: no remote copies, remote signals or barrier semaphores. Data moves between devices by JAX's collectives and lax.ppermute only.
A program may use at most 64 MiB of HBM per device.

v0:
```python
import jax
import jax.numpy as jnp
from jax import lax
from jax.sharding import PartitionSpec as P

BLOCK = 64


def from_behind(value, axis, steps):
    count = lax.axis_size(axis)
    leading, last = (max(0, -steps), min(count, count - steps))
    return lax.ppermute(value, axis, [(source, source + steps) for source in range(leading, last)])


def along_rows(payload, stride):
    return from_behind(payload, "tx", stride)


def along_cols(payload, stride):
    return from_behind(payload, "ty", stride)


def shards(voxels, owner_tile, rim_blocks, kernel_map, weights, norm_gain, shift_bias):
    devices = lax.axis_size(("tx", "ty"))
    src_count = voxels.shape[0]
    channels = voxels.shape[1]
    tile_rows = kernel_map.shape[2]
    pair_rows = tile_rows // devices
    target = owner_tile[:, 0]
    member = (target[:, None] == jnp.arange(devices, dtype=jnp.int32)[None, :]).astype(jnp.bfloat16)
    run_len = min(512, src_count)
    run_count = src_count // run_len
    member_runs = member.reshape(run_count, run_len, devices)
    lower_ones = (jnp.arange(run_len)[:, None] >= jnp.arange(run_len)[None, :]).astype(jnp.bfloat16)
    inside = jnp.einsum("ij,bjd->bid", lower_ones, member_runs, preferred_element_type=jnp.float32)
    run_totals = inside[:, -1, :]
    before = jnp.cumsum(run_totals, axis=0) - run_totals
    running = (inside + before[:, None, :]).reshape(src_count, devices)
    member_wide = member.astype(jnp.float32)
    placed = jnp.sum((running - 1.0) * member_wide, axis=1).astype(jnp.int32)
    address = target * pair_rows + placed
    filled = jnp.sum(member_wide, axis=0).astype(jnp.bfloat16)
    slot_len = min(512, tile_rows)

    def place_slots(first):
        slots = first * slot_len + jnp.arange(slot_len, dtype=jnp.int32)
        chooser = (slots[:, None] == address[None, :]).astype(jnp.bfloat16)
        return jnp.dot(chooser, voxels, preferred_element_type=jnp.float32).astype(jnp.bfloat16)

    outgoing = lax.map(place_slots, jnp.arange(tile_rows // slot_len, dtype=jnp.int32)).reshape(
        tile_rows, channels
    )
    arrival, received = (
        lax.all_to_all(
            outgoing.reshape(devices, pair_rows, channels),
            ("tx", "ty"),
            split_axis=0,
            concat_axis=0,
            tiled=True,
        ),
        lax.all_to_all(
            filled.reshape(devices, 1), ("tx", "ty"), split_axis=0, concat_axis=0, tiled=True
        ),
    )
    arrival = arrival.reshape(tile_rows, channels)
    occupied = jnp.arange(pair_rows, dtype=jnp.float32)[None, :] < received.astype(jnp.float32)
    occupied = occupied.astype(jnp.float32).reshape(tile_rows)
    blocked = arrival.reshape(tile_rows // BLOCK, BLOCK, channels)
    picked = blocked[rim_blocks[0]]
    lower_x = along_rows(picked[0], 1)
    upper_x = along_rows(picked[1], -1)
    lower_y = along_cols(picked[2], 1)
    upper_y = along_cols(picked[3], -1)
    margin = jnp.concatenate((lower_x, upper_x, lower_y, upper_y), axis=0).reshape(-1, channels)
    extended = jnp.concatenate((arrival, margin), axis=0)
    ext_blocks = extended.reshape(-1, BLOCK, channels)
    offsets = kernel_map.shape[1]
    out_blocks = tile_rows // BLOCK
    block_map = kernel_map[0].reshape(offsets, out_blocks, BLOCK)
    source_block = jnp.maximum(jnp.max(block_map, axis=2) // BLOCK, 0)
    local_row = block_map - source_block[:, :, None] * BLOCK
    window = min(512, tile_rows)
    per_window = window // BLOCK
    windows = tile_rows // window
    source_groups = source_block.reshape(offsets, windows, per_window).transpose(1, 0, 2)
    local_groups = local_row.reshape(offsets, windows, per_window, BLOCK).transpose(1, 0, 2, 3)
    valid_groups = (
        (block_map >= 0).reshape(offsets, windows, per_window, BLOCK).transpose(1, 0, 2, 3)
    )
    positions = jnp.arange(BLOCK, dtype=jnp.int32)

    def convolve(bundle):
        sources, locals_here, valid_here = bundle
        fetched = ext_blocks[sources]
        selector = ((locals_here[..., None] == positions) & valid_here[..., None]).astype(
            jnp.bfloat16
        )
        chosen = jnp.einsum(
            "kbrj,kbjc->kbrc", selector, fetched, preferred_element_type=jnp.float32
        ).astype(jnp.bfloat16)
        return jnp.einsum("kbrc,kco->bro", chosen, weights, preferred_element_type=jnp.float32)

    response = (
        lax.map(convolve, (source_groups, local_groups, valid_groups)).reshape(tile_rows, -1)
        * occupied[:, None]
    )
    population = jnp.float32(voxels.shape[0] * devices)
    average = lax.psum(jnp.sum(response, axis=0), ("tx", "ty")) / population
    centred = (response - average) * occupied[:, None]
    variance = lax.psum(jnp.sum(centred * centred, axis=0), ("tx", "ty")) / population
    scaled = norm_gain * (response - average) / jnp.sqrt(variance + 1e-05) + shift_bias
    return (jnp.maximum(scaled, 0.0) * occupied[:, None]).astype(jnp.bfloat16)


def solution(mesh):
    return jax.shard_map(
        shards,
        mesh=mesh,
        in_specs=(
            P(("tx", "ty"), None),
            P(("tx", "ty"), None),
            P(("tx", "ty"), None, None),
            P(("tx", "ty"), None, None),
            P(),
            P(),
            P(),
        ),
        out_specs=P(("tx", "ty"), None),
        check_vma=False,
    )
```

profile of v0, /device:TPU:1, one launch (start us, length us, event | category | flops | bytes accessed | tf_op | source)
XLA Modules:
  0.0 477.9 jit_solution(10910480477086179535)
XLA Ops:
  0.0 2.6 fusion.57
  3.3 11.5 %all-to-all-start.1 = ((bf16[128,1,1]{2,1,0:T(2,128)(2,1)}), bf16[128,1,1]{2,1,0:T(2,128)(2,1)S(1)}, u32[]{:S(2)}, u32[]{:S(2)}) async-start(bf16[128,1,1]{2,1,0:T(2,128)(2,1)} %copy.37), calls=%async_computation.1 | async-start | bytes 131072 | tf_op jit(solution)/shard_map/all_to_all | solution.py:61
  18.7 51.1 %while.21 = (s32[]{:T(128)}, bf16[16,512,128]{2,1,0:T(8,128)(2,1)}, s32[16]{0:T(128)S(1)}, s32[4096]{0:T(1024)S(1)}, bf16[4096,128]{1,0:T(8,128)(2,1)S(1)}, /*index=5*/s32[]{:T(128)}, s32[1]{0:T(128)}) while((s32[]{:T(128)}, bf16[16,512,128]{2,1,0:T(8,128)(2,1)}, s32[16]{0:T(128)S(1)}, s32[4096]{0:T(1024)S(1)}, ...), condition=%wide.region_4.5_spmd, body=%wide.region_3.4_spmd.sunk | while | flops 539034112 | bytes 1200745 | solution.py:50
  69.7 10.2 %all-to-all-start = ((bf16[128,64,128]{2,1,0:T(8,128)(2,1)}), bf16[128,64,128]{2,1,0:T(8,128)(2,1)}, u32[]{:S(2)}, u32[]{:S(2)}) async-start(bf16[128,64,128]{2,1,0:T(8,128)(2,1)} %bitcast.9), calls=%async_computation | async-start | bytes 4194304 | tf_op jit(solution)/shard_map/all_to_all | solution.py:54
  90.9 18.5 %all-to-all-done = bf16[128,64,128]{2,1,0:T(8,128)(2,1)} async-done(((bf16[128,64,128]{2,1,0:T(8,128)(2,1)}), bf16[128,64,128]{2,1,0:T(8,128)(2,1)}, u32[]{:S(2)}, u32[]{:S(2)}) %all-to-all-start) | async-done | bytes 2097184 | tf_op jit(solution)/shard_map/all_to_all | solution.py:54
  109.4 2.3 gather_fusion.1
  111.8 3.4 collective-permute-start
  117.1 2.6 collective-permute-start.2
  124.6 4.1 collective-permute-done.3
  128.9 7.4 %pad_maximum_fusion = bf16[12288,128]{1,0:T(8,128)(2,1)S(1)} fusion(bf16[4096,128]{1,0:T(8,128)(2,1)S(1)} %bitcast.107, bf16[8192,128]{1,0:T(8,128)(2,1)} %bitcast.10), kind=kLoop, calls=%fused_computation.39 | loop fusion | flops 6291456 | bytes 6291456 | tf_op jit(solution)/shard_map/concatenate | solution.py:75
  136.3 200.1 %while.22 = (s32[]{:T(128)}, f32[16,8,64,128]{3,2,1,0:T(8,128)}, s32[16,27,8,64]{3,2,0,1:T(8,128)}, pred[16,27,8,64]{3,2,0,1:T(8,128)(4,1)}, s32[16,27,8]{1,2,0:...) while((s32[]{:T(128)}, f32[16,8,64,128]{3,2,1,0:T(8,128)}, ...), condition=%wide.region_6.7_spmd.clone, body=%wide.region_5.6_spmd.clone.sunk | while | flops 683017856 | bytes 12122657 | solution.py:104
  136.5 2.9 gather_fusion
  141.1 7.7 %fusion.87 = f32[16,8,64,128]{3,2,1,0:T(8,128)} fusion(f32[16,8,64,128]{3,2,1,0:T(8,128)} %get-tuple-element.261, s32[]{:T(128)} %get-tuple-element.260, bf16[27,8,64,128]{3,2,1,0:T(8,128)(2,1)} %bitcast.106, s32[27,8,64]{2,0,1:T(8,128)S(1)} %bitcast.108, pred[27,8,64]{2,0,1:T(8,128)(4,1)S(1)} %bitcast.109, bf16[27,128,128]{2,1,0:T(8,128)(2,1)} %get-tuple-element.274), kind=kOutput, calls=%fused_computation.20.clone.1 | convolution fusion | flops 683016192 | bytes 4755456 | tf_op jit(solution)/shard_map/while/body/eval_jaxpr/kbrc,kco->bro/dot_general | solution.py:101
  149.0 2.9 gather_fusion
  153.6 7.7 %fusion.87 = f32[16,8,64,128]{3,2,1,0:T(8,128)} fusion(f32[16,8,64,128]{3,2,1,0:T(8,128)} %get-tuple-element.261, s32[]{:T(128)} %get-tuple-element.260, bf16[27,8,64,128]{3,2,1,0:T(8,128)(2,1)} %bitcast.106, s32[27,8,64]{2,0,1:T(8,128)S(1)} %bitcast.108, pred[27,8,64]{2,0,1:T(8,128)(4,1)S(1)} %bitcast.109, bf16[27,128,128]{2,1,0:T(8,128)(2,1)} %get-tuple-element.274), kind=kOutput, calls=%fused_computation.20.clone.1 | convolution fusion | flops 683016192 | bytes 4755456 | tf_op jit(solution)/shard_map/while/body/eval_jaxpr/kbrc,kco->bro/dot_general | solution.py:101
  161.5 2.9 gather_fusion
  166.1 7.7 %fusion.87 = f32[16,8,64,128]{3,2,1,0:T(8,128)} fusion(f32[16,8,64,128]{3,2,1,0:T(8,128)} %get-tuple-element.261, s32[]{:T(128)} %get-tuple-element.260, bf16[27,8,64,128]{3,2,1,0:T(8,128)(2,1)} %bitcast.106, s32[27,8,64]{2,0,1:T(8,128)S(1)} %bitcast.108, pred[27,8,64]{2,0,1:T(8,128)(4,1)S(1)} %bitcast.109, bf16[27,128,128]{2,1,0:T(8,128)(2,1)} %get-tuple-element.274), kind=kOutput, calls=%fused_computation.20.clone.1 | convolution fusion | flops 683016192 | bytes 4755456 | tf_op jit(solution)/shard_map/while/body/eval_jaxpr/kbrc,kco->bro/dot_general | solution.py:101
  174.0 2.9 gather_fusion
  178.5 7.7 %fusion.87 = f32[16,8,64,128]{3,2,1,0:T(8,128)} fusion(f32[16,8,64,128]{3,2,1,0:T(8,128)} %get-tuple-element.261, s32[]{:T(128)} %get-tuple-element.260, bf16[27,8,64,128]{3,2,1,0:T(8,128)(2,1)} %bitcast.106, s32[27,8,64]{2,0,1:T(8,128)S(1)} %bitcast.108, pred[27,8,64]{2,0,1:T(8,128)(4,1)S(1)} %bitcast.109, bf16[27,128,128]{2,1,0:T(8,128)(2,1)} %get-tuple-element.274), kind=kOutput, calls=%fused_computation.20.clone.1 | convolution fusion | flops 683016192 | bytes 4755456 | tf_op jit(solution)/shard_map/while/body/eval_jaxpr/kbrc,kco->bro/dot_general | solution.py:101
  186.5 2.9 gather_fusion
  191.1 7.7 %fusion.87 = f32[16,8,64,128]{3,2,1,0:T(8,128)} fusion(f32[16,8,64,128]{3,2,1,0:T(8,128)} %get-tuple-element.261, s32[]{:T(128)} %get-tuple-element.260, bf16[27,8,64,128]{3,2,1,0:T(8,128)(2,1)} %bitcast.106, s32[27,8,64]{2,0,1:T(8,128)S(1)} %bitcast.108, pred[27,8,64]{2,0,1:T(8,128)(4,1)S(1)} %bitcast.109, bf16[27,128,128]{2,1,0:T(8,128)(2,1)} %get-tuple-element.274), kind=kOutput, calls=%fused_computation.20.clone.1 | convolution fusion | flops 683016192 | bytes 4755456 | tf_op jit(solution)/shard_map/while/body/eval_jaxpr/kbrc,kco->bro/dot_general | solution.py:101
  199.0 2.9 gather_fusion
  203.6 7.7 %fusion.87 = f32[16,8,64,128]{3,2,1,0:T(8,128)} fusion(f32[16,8,64,128]{3,2,1,0:T(8,128)} %get-tuple-element.261, s32[]{:T(128)} %get-tuple-element.260, bf16[27,8,64,128]{3,2,1,0:T(8,128)(2,1)} %bitcast.106, s32[27,8,64]{2,0,1:T(8,128)S(1)} %bitcast.108, pred[27,8,64]{2,0,1:T(8,128)(4,1)S(1)} %bitcast.109, bf16[27,128,128]{2,1,0:T(8,128)(2,1)} %get-tuple-element.274), kind=kOutput, calls=%fused_computation.20.clone.1 | convolution fusion | flops 683016192 | bytes 4755456 | tf_op jit(solution)/shard_map/while/body/eval_jaxpr/kbrc,kco->bro/dot_general | solution.py:101
  211.5 2.9 gather_fusion
  216.1 7.7 %fusion.87 = f32[16,8,64,128]{3,2,1,0:T(8,128)} fusion(f32[16,8,64,128]{3,2,1,0:T(8,128)} %get-tuple-element.261, s32[]{:T(128)} %get-tuple-element.260, bf16[27,8,64,128]{3,2,1,0:T(8,128)(2,1)} %bitcast.106, s32[27,8,64]{2,0,1:T(8,128)S(1)} %bitcast.108, pred[27,8,64]{2,0,1:T(8,128)(4,1)S(1)} %bitcast.109, bf16[27,128,128]{2,1,0:T(8,128)(2,1)} %get-tuple-element.274), kind=kOutput, calls=%fused_computation.20.clone.1 | convolution fusion | flops 683016192 | bytes 4755456 | tf_op jit(solution)/shard_map/while/body/eval_jaxpr/kbrc,kco->bro/dot_general | solution.py:101
  224.0 2.9 gather_fusion
  228.6 7.7 %fusion.87 = f32[16,8,64,128]{3,2,1,0:T(8,128)} fusion(f32[16,8,64,128]{3,2,1,0:T(8,128)} %get-tuple-element.261, s32[]{:T(128)} %get-tuple-element.260, bf16[27,8,64,128]{3,2,1,0:T(8,128)(2,1)} %bitcast.106, s32[27,8,64]{2,0,1:T(8,128)S(1)} %bitcast.108, pred[27,8,64]{2,0,1:T(8,128)(4,1)S(1)} %bitcast.109, bf16[27,128,128]{2,1,0:T(8,128)(2,1)} %get-tuple-element.274), kind=kOutput, calls=%fused_computation.20.clone.1 | convolution fusion | flops 683016192 | bytes 4755456 | tf_op jit(solution)/shard_map/while/body/eval_jaxpr/kbrc,kco->bro/dot_general | solution.py:101
  236.5 2.9 gather_fusion
  241.1 7.7 %fusion.87 = f32[16,8,64,128]{3,2,1,0:T(8,128)} fusion(f32[16,8,64,128]{3,2,1,0:T(8,128)} %get-tuple-element.261, s32[]{:T(128)} %get-tuple-element.260, bf16[27,8,64,128]{3,2,1,0:T(8,128)(2,1)} %bitcast.106, s32[27,8,64]{2,0,1:T(8,128)S(1)} %bitcast.108, pred[27,8,64]{2,0,1:T(8,128)(4,1)S(1)} %bitcast.109, bf16[27,128,128]{2,1,0:T(8,128)(2,1)} %get-tuple-element.274), kind=kOutput, calls=%fused_computation.20.clone.1 | convolution fusion | flops 683016192 | bytes 4755456 | tf_op jit(solution)/shard_map/while/body/eval_jaxpr/kbrc,kco->bro/dot_general | solution.py:101
  249.0 2.9 gather_fusion
  253.6 7.7 %fusion.87 = f32[16,8,64,128]{3,2,1,0:T(8,128)} fusion(f32[16,8,64,128]{3,2,1,0:T(8,128)} %get-tuple-element.261, s32[]{:T(128)} %get-tuple-element.260, bf16[27,8,64,128]{3,2,1,0:T(8,128)(2,1)} %bitcast.106, s32[27,8,64]{2,0,1:T(8,128)S(1)} %bitcast.108, pred[27,8,64]{2,0,1:T(8,128)(4,1)S(1)} %bitcast.109, bf16[27,128,128]{2,1,0:T(8,128)(2,1)} %get-tuple-element.274), kind=kOutput, calls=%fused_computation.20.clone.1 | convolution fusion | flops 683016192 | bytes 4755456 | tf_op jit(solution)/shard_map/while/body/eval_jaxpr/kbrc,kco->bro/dot_general | solution.py:101
  261.5 2.9 gather_fusion
  266.1 7.7 %fusion.87 = f32[16,8,64,128]{3,2,1,0:T(8,128)} fusion(f32[16,8,64,128]{3,2,1,0:T(8,128)} %get-tuple-element.261, s32[]{:T(128)} %get-tuple-element.260, bf16[27,8,64,128]{3,2,1,0:T(8,128)(2,1)} %bitcast.106, s32[27,8,64]{2,0,1:T(8,128)S(1)} %bitcast.108, pred[27,8,64]{2,0,1:T(8,128)(4,1)S(1)} %bitcast.109, bf16[27,128,128]{2,1,0:T(8,128)(2,1)} %get-tuple-element.274), kind=kOutput, calls=%fused_computation.20.clone.1 | convolution fusion | flops 683016192 | bytes 4755456 | tf_op jit(solution)/shard_map/while/body/eval_jaxpr/kbrc,kco->bro/dot_general | solution.py:101
  274.0 2.9 gather_fusion
  278.6 7.7 %fusion.87 = f32[16,8,64,128]{3,2,1,0:T(8,128)} fusion(f32[16,8,64,128]{3,2,1,0:T(8,128)} %get-tuple-element.261, s32[]{:T(128)} %get-tuple-element.260, bf16[27,8,64,128]{3,2,1,0:T(8,128)(2,1)} %bitcast.106, s32[27,8,64]{2,0,1:T(8,128)S(1)} %bitcast.108, pred[27,8,64]{2,0,1:T(8,128)(4,1)S(1)} %bitcast.109, bf16[27,128,128]{2,1,0:T(8,128)(2,1)} %get-tuple-element.274), kind=kOutput, calls=%fused_computation.20.clone.1 | convolution fusion | flops 683016192 | bytes 4755456 | tf_op jit(solution)/shard_map/while/body/eval_jaxpr/kbrc,kco->bro/dot_general | solution.py:101
  286.5 2.9 gather_fusion
  291.1 7.7 %fusion.87 = f32[16,8,64,128]{3,2,1,0:T(8,128)} fusion(f32[16,8,64,128]{3,2,1,0:T(8,128)} %get-tuple-element.261, s32[]{:T(128)} %get-tuple-element.260, bf16[27,8,64,128]{3,2,1,0:T(8,128)(2,1)} %bitcast.106, s32[27,8,64]{2,0,1:T(8,128)S(1)} %bitcast.108, pred[27,8,64]{2,0,1:T(8,128)(4,1)S(1)} %bitcast.109, bf16[27,128,128]{2,1,0:T(8,128)(2,1)} %get-tuple-element.274), kind=kOutput, calls=%fused_computation.20.clone.1 | convolution fusion | flops 683016192 | bytes 4755456 | tf_op jit(solution)/shard_map/while/body/eval_jaxpr/kbrc,kco->bro/dot_general | solution.py:101
  299.0 2.9 gather_fusion
  303.6 7.7 %fusion.87 = f32[16,8,64,128]{3,2,1,0:T(8,128)} fusion(f32[16,8,64,128]{3,2,1,0:T(8,128)} %get-tuple-element.261, s32[]{:T(128)} %get-tuple-element.260, bf16[27,8,64,128]{3,2,1,0:T(8,128)(2,1)} %bitcast.106, s32[27,8,64]{2,0,1:T(8,128)S(1)} %bitcast.108, pred[27,8,64]{2,0,1:T(8,128)(4,1)S(1)} %bitcast.109, bf16[27,128,128]{2,1,0:T(8,128)(2,1)} %get-tuple-element.274), kind=kOutput, calls=%fused_computation.20.clone.1 | convolution fusion | flops 683016192 | bytes 4755456 | tf_op jit(solution)/shard_map/while/body/eval_jaxpr/kbrc,kco->bro/dot_general | solution.py:101
  311.5 2.9 gather_fusion
  316.1 7.7 %fusion.87 = f32[16,8,64,128]{3,2,1,0:T(8,128)} fusion(f32[16,8,64,128]{3,2,1,0:T(8,128)} %get-tuple-element.261, s32[]{:T(128)} %get-tuple-element.260, bf16[27,8,64,128]{3,2,1,0:T(8,128)(2,1)} %bitcast.106, s32[27,8,64]{2,0,1:T(8,128)S(1)} %bitcast.108, pred[27,8,64]{2,0,1:T(8,128)(4,1)S(1)} %bitcast.109, bf16[27,128,128]{2,1,0:T(8,128)(2,1)} %get-tuple-element.274), kind=kOutput, calls=%fused_computation.20.clone.1 | convolution fusion | flops 683016192 | bytes 4755456 | tf_op jit(solution)/shard_map/while/body/eval_jaxpr/kbrc,kco->bro/dot_general | solution.py:101
  324.0 2.9 gather_fusion
  328.6 7.7 %fusion.87 = f32[16,8,64,128]{3,2,1,0:T(8,128)} fusion(f32[16,8,64,128]{3,2,1,0:T(8,128)} %get-tuple-element.261, s32[]{:T(128)} %get-tuple-element.260, bf16[27,8,64,128]{3,2,1,0:T(8,128)(2,1)} %bitcast.106, s32[27,8,64]{2,0,1:T(8,128)S(1)} %bitcast.108, pred[27,8,64]{2,0,1:T(8,128)(4,1)S(1)} %bitcast.109, bf16[27,128,128]{2,1,0:T(8,128)(2,1)} %get-tuple-element.274), kind=kOutput, calls=%fused_computation.20.clone.1 | convolution fusion | flops 683016192 | bytes 4755456 | tf_op jit(solution)/shard_map/while/body/eval_jaxpr/kbrc,kco->bro/dot_general | solution.py:101
  336.3 2.9 multiply_reduce_fusion.1
  339.2 66.1 %psum.14 = f32[128]{0:T(128)S(1)} all-reduce(f32[128]{0:T(128)S(1)} %multiply_reduce_fusion.1), channel_id=1, replica_groups=mesh['tx'=8,'ty'=16] {'tx','ty'}, use_global_device_ids=true, to_apply=%region_9.10 | all-reduce | flops 128 | bytes 1024 | tf_op jit(solution)/shard_map/psum | solution.py:108
  405.3 2.8 multiply_reduce_fusion
  408.2 63.6 %psum.15 = f32[128]{0:T(128)S(1)} all-reduce(f32[128]{0:T(128)S(1)} %multiply_reduce_fusion), channel_id=1, replica_groups=mesh['tx'=8,'ty'=16] {'tx','ty'}, use_global_device_ids=true, to_apply=%region_11.12 | all-reduce | flops 128 | bytes 1024 | tf_op jit(solution)/shard_map/psum | solution.py:110
  471.8 6.1 %fusion.52 = bf16[8192,128]{1,0:T(8,128)(2,1)} fusion(f32[16,8,64,128]{3,2,1,0:T(8,128)} %get-tuple-element.75, f32[128]{0:T(128)S(1)} %copy-done.3, f32[128]{0:T(128)S(1)} %add_sqrt_fusion, f32[128]{0:T(128)S(1)} %broadcast_multiply_fusion.1, f32[8192]{0:T(1024)S(1)} %reshape.199, f32[128]{0:T(128)S(1)} %copy-done.4), kind=kLoop, calls=%fused_computation.37 | loop fusion | flops 8388608 | bytes 6326272 | tf_op jit(solution)/shard_map/convert_element_type | solution.py:112
  (244 shorter events, 93.7 us)
Async XLA Ops:
  0.0 18.6 %copy-start.1 = (s32[4096,1]{0,1:T(1,128)S(1)}, s32[4096,1]{0,1:T(1,128)}, u32[]{:S(2)}) copy-start(s32[4096,1]{0,1:T(1,128)} %param.12) | copy-start | bytes 49156
  0.0 18.6 %copy-start.5 = (bf16[4096,128]{1,0:T(8,128)(2,1)S(1)}, bf16[4096,128]{1,0:T(8,128)(2,1)}, u32[]{:S(2)}) copy-start(bf16[4096,128]{1,0:T(8,128)(2,1)} %param.11) | copy-start | bytes 3145732
  3.3 66.4 %all-to-all-start.1 = ((bf16[128,1,1]{2,1,0:T(2,128)(2,1)}), bf16[128,1,1]{2,1,0:T(2,128)(2,1)S(1)}, u32[]{:S(2)}, u32[]{:S(2)}) async-start(bf16[128,1,1]{2,1,0:T(2,128)(2,1)} %copy.37), calls=%async_computation.1 | async-start | bytes 131072 | tf_op jit(solution)/shard_map/all_to_all | solution.py:61
  69.7 10.2 %copy-start = (s32[1,27,8192]{2,0,1:T(1,128)S(1)}, s32[1,27,8192]{2,0,1:T(1,128)}, u32[]{:S(2)}) copy-start(s32[1,27,8192]{2,0,1:T(1,128)} %param.14) | copy-start | bytes 2654212
  69.7 39.6 %all-to-all-start = ((bf16[128,64,128]{2,1,0:T(8,128)(2,1)}), bf16[128,64,128]{2,1,0:T(8,128)(2,1)}, u32[]{:S(2)}, u32[]{:S(2)}) async-start(bf16[128,64,128]{2,1,0:T(8,128)(2,1)} %bitcast.9), calls=%async_computation | async-start | bytes 4194304 | tf_op jit(solution)/shard_map/all_to_all | solution.py:54
  80.0 4.8 %copy-start.2 = (s32[1,4,16]{2,1,0:T(4,128)S(1)}, s32[1,4,16]{2,1,0:T(4,128)}, u32[]{:S(2)}) copy-start(s32[1,4,16]{2,1,0:T(4,128)} %param.13) | copy-start | bytes 772
  111.8 9.8 %collective-permute-start = (bf16[16,64,128]{2,1,0:T(8,128)(2,1)S(1)}, bf16[16,64,128]{2,1,0:T(8,128)(2,1)S(1)}, u32[]{:S(2)}, u32[]{:S(2)}) collective-permute-start(bf16[16,64,128]{2,1,0:T(8,128)(2,1)S(1)} %get-tuple-element.151), channel_id=1, source_target_pairs={{0,16},{16,32},{32,48},{48,64},{64,80},{80,96},{96,112},{1,17},{17... | collective-permute-start | bytes 786440 | tf_op jit(solution)/shard_map/ppermute | solution.py:12
  115.2 7.7 %collective-permute-start.1 = (bf16[16,64,128]{2,1,0:T(8,128)(2,1)S(1)}, bf16[16,64,128]{2,1,0:T(8,128)(2,1)S(1)}, u32[]{:S(2)}, u32[]{:S(2)}) collective-permute-start(bf16[16,64,128]{2,1,0:T(8,128)(2,1)S(1)} %get-tuple-element.153), channel_id=1, source_target_pairs={{16,0},{32,16},{48,32},{64,48},{80,64},{96,80},{112,96},{17,1},{33... | collective-permute-start | bytes 786440 | tf_op jit(solution)/shard_map/ppermute | solution.py:12
  117.1 7.5 %collective-permute-start.2 = (bf16[16,64,128]{2,1,0:T(8,128)(2,1)S(1)}, bf16[16,64,128]{2,1,0:T(8,128)(2,1)S(1)}, u32[]{:S(2)}, u32[]{:S(2)}) collective-permute-start(bf16[16,64,128]{2,1,0:T(8,128)(2,1)S(1)} %get-tuple-element.152), channel_id=1, source_target_pairs={{0,1},{1,2},{2,3},{3,4},{4,5},{5,6},{6,7},{7,8},{8,9},{9,10},{10,1... | collective-permute-start | bytes 786440 | tf_op jit(solution)/shard_map/ppermute | solution.py:12
  119.7 9.0 %collective-permute-start.3 = (bf16[16,64,128]{2,1,0:T(8,128)(2,1)S(1)}, bf16[16,64,128]{2,1,0:T(8,128)(2,1)S(1)}, u32[]{:S(2)}, u32[]{:S(2)}) collective-permute-start(bf16[16,64,128]{2,1,0:T(8,128)(2,1)S(1)} %get-tuple-element.154), channel_id=1, source_target_pairs={{1,0},{2,1},{3,2},{4,3},{5,4},{6,5},{7,6},{8,7},{9,8},{10,9},{11,1... | collective-permute-start | bytes 786440 | tf_op jit(solution)/shard_map/ppermute | solution.py:12
  336.3 135.4 %copy-start.3 = (f32[128]{0:T(128)S(1)}, f32[128]{0:T(128)}, u32[]{:S(2)}) copy-start(f32[128]{0:T(128)} %param.17) | copy-start | bytes 1540
  336.3 135.4 %copy-start.4 = (f32[128]{0:T(128)S(1)}, f32[128]{0:T(128)}, u32[]{:S(2)}) copy-start(f32[128]{0:T(128)} %param.16) | copy-start | bytes 1540
where the time goes:
time: 480 us; the launch traced here: 478 us
  matrix products  156 us (32%)
  blocking collectives  130 us (27%)
  local copies, waits for them, and re-layouts  92.5 us (19%)
  other arithmetic  32.7 us (7%)
  starting transfers between devices  31.1 us (6%)
  waiting for transfers between devices  25.6 us (5%)
  loops' own time  10.5 us (2%)
    dot_general x16, matrix products, convolve(): jnp.einsum('kbrc,kco->bro', chosen, weights, preferred_element_type=jnp.f...  123 us
    psum x1, blocking collectives, shards(): average = lax.psum(jnp.sum(response, axis=0), ('tx', 'ty')) / population  66.1 us
    psum x1, blocking collectives, shards(): lax.psum(jnp.sum(centred * centred, axis=0), ('tx', 'ty')) / population  63.6 us
    gather x16, local copies, waits for them, and re-layouts, convolve(): fetched = ext_blocks[sources]  46 us
    dot_general x16, matrix products, place_slots(): jnp.dot(chooser, voxels, preferred_element_type=jnp.float32)  31.4 us
    dynamic_slice x96, local copies, waits for them, and re-layouts, shards(): lax.map(convolve, (source_groups, local_groups, valid_groups))  28.7 us
    all_to_all x1, waiting for transfers between devices, shards(): lax.all_to_all(outgoing.reshape(devices, pair_rows, channels), ('tx', 'ty...  18.5 us
    all_to_all x1, starting transfers between devices, shards(): lax.all_to_all(filled.reshape(devices, 1), ('tx', 'ty'), split_axis=0, co...  11.5 us
  transfers between devices with their start and end apart: 6, of which 4 were waited for; matrix products, arithmetic and copies ran while one was open for 12% of the time, Pallas kernels for 0%

commit v1 on v0

v1 whole, which is shorter than its diff:
```python
import functools

import jax
import jax.numpy as jnp
from jax import lax
from jax.experimental import pallas as pl
from jax.experimental.pallas import tpu as pltpu
from jax.sharding import PartitionSpec as P

AXES = ("tx", "ty")
LANES = 128
BF16, F32, I32 = jnp.bfloat16, jnp.float32, jnp.int32
EMPTY = -1.0
MIB = 1 << 20


def from_behind(value, axis, steps):
    count = lax.axis_size(axis)
    leading, last = (max(0, -steps), min(count, count - steps))
    return lax.ppermute(value, axis, [(source, source + steps) for source in range(leading, last)])


def place_kernel(pair_rows, owner, voxels, out, addr_v, addr_s, wide, slots, sem):
    runs, run_len = owner.shape
    tiles = out.shape[0] // pair_rows
    earlier = lax.broadcasted_iota(I32, (run_len, run_len), 0)
    later = lax.broadcasted_iota(I32, (run_len, run_len), 1)
    upto = (earlier <= later).astype(BF16)
    tile_ids = lax.broadcasted_iota(I32, (tiles, run_len), 0)
    before = jnp.zeros((tiles, 1), F32)
    for run in range(runs):
        target = owner[run : run + 1, :]
        member = tile_ids == target
        inside = jnp.dot(member.astype(BF16), upto, preferred_element_type=F32) + before
        rank = jnp.sum(jnp.where(member, inside, 0.0), axis=0, keepdims=True)
        addr_v[run : run + 1, :] = target * pair_rows + rank.astype(I32) - 1
        before = inside[:, run_len - 1 : run_len]
    copy = pltpu.make_async_copy(addr_v, addr_s, sem)
    copy.start()
    chunk = 256

    @pl.loop(0, voxels.shape[0] // chunk)
    def _(i):
        rows = pl.ds(pl.multiple_of(i * chunk, chunk), chunk)
        wide[rows, :] = voxels[rows, :].astype(F32)

    @pl.loop(0, out.shape[0] // chunk)
    def _(i):
        rows = pl.ds(pl.multiple_of(i * chunk, chunk), chunk)
        slots[rows, :] = jnp.full((chunk, slots.shape[1]), EMPTY, F32)

    copy.wait()
    unroll = 16
    for run in range(runs):

        @pl.loop(0, run_len // unroll)
        def _(i):
            for u in range(unroll):
                place = addr_s[run, i * unroll + u]
                slots[pl.ds(place, 1), :] = wide[pl.ds(run * run_len + i * unroll + u, 1), :]

    @pl.loop(0, out.shape[0] // chunk)
    def _(i):
        rows = pl.ds(pl.multiple_of(i * chunk, chunk), chunk)
        out[rows, :] = slots[rows, :].astype(BF16)


def place(voxels, owner, tile_rows, pair_rows):
    rows, channels = voxels.shape
    runs = 8
    return pl.pallas_call(
        functools.partial(place_kernel, pair_rows),
        out_shape=jax.ShapeDtypeStruct((tile_rows, channels), BF16),
        scratch_shapes=[
            pltpu.VMEM((runs, rows // runs), I32),
            pltpu.SMEM((runs, rows // runs), I32),
            pltpu.VMEM((rows, channels), F32),
            pltpu.VMEM((tile_rows, channels), F32),
            pltpu.SemaphoreType.DMA,
        ],
        compiler_params=pltpu.CompilerParams(vmem_limit_bytes=32 * MIB),
        name="place",
    )(owner.reshape(runs, rows // runs), voxels)


def pick_kernel(block, listed, arrival, *rest):
    outs, sems = rest[:-1], rest[-1]
    count = outs[0].shape[0] // block
    copies = []
    for d, out in enumerate(outs):
        for i in range(count):
            source = pl.multiple_of(listed[d, i] * block, block)
            copies.append(
                pltpu.make_async_copy(
                    arrival.at[pl.ds(source, block), :],
                    out.at[pl.ds(i * block, block), :],
                    sems.at[d * count + i],
                )
            )
    for copy in copies:
        copy.start()
    for copy in copies:
        copy.wait()


def pick(arrival, listed, block):
    directions, count = listed.shape
    shape = jax.ShapeDtypeStruct((count * block, arrival.shape[1]), arrival.dtype)
    return pl.pallas_call(
        functools.partial(pick_kernel, block),
        in_specs=[
            pl.BlockSpec(memory_space=pltpu.SMEM),
            pl.BlockSpec(memory_space=pl.ANY),
        ],
        out_specs=[pl.BlockSpec(memory_space=pl.ANY)] * directions,
        out_shape=[shape] * directions,
        scratch_shapes=[pltpu.SemaphoreType.DMA((directions * count,))],
        name="pick_rims",
    )(listed, arrival)


def conv_kernel(block, source, kmap, arrival, rim0, rim1, rim2, rim3, weights_t, resp, occ, stats, xt, g):
    step = pl.program_id(0)
    offsets, window = kmap.shape
    channels = arrival.shape[1]
    lane = lax.broadcasted_iota(I32, (channels, LANES), 1)
    right = lane >= block
    lane_row = lax.broadcasted_iota(I32, (1, LANES), 1)
    half = jnp.where(lane_row >= block, block, 0)
    rows = lax.broadcasted_iota(I32, (LANES, LANES), 0)

    @pl.when(step == 0)
    def _():
        first = 0
        for number, part in enumerate((arrival, rim0, rim1, rim2, rim3)):
            pairs = part.shape[0] // LANES

            def turn(p, carry, part=part, first=first, number=number):
                at = pl.multiple_of(p * LANES, LANES)
                turned = part[pl.ds(at, LANES), :].astype(F32).T
                if number == 0:
                    occ[:, pl.ds(at, LANES)] = (turned[0:1, :] >= 0.0).astype(F32)
                turned = jnp.maximum(turned, 0.0)
                xt[first + 2 * p] = turned.astype(BF16)
                xt[first + 2 * p + 1] = pltpu.roll(turned, block, 1).astype(BF16)
                return carry

            lax.fori_loop(0, pairs, turn, 0, unroll=2)
            first += 2 * pairs

    blocks = window // block
    for k in range(offsets):
        for p in range(window // LANES):
            listed = kmap[k : k + 1, p * LANES : (p + 1) * LANES]
            left_block = source[k, blocks * step + 2 * p]
            right_block = source[k, blocks * step + 2 * p + 1]
            pair = jnp.where(right, xt[right_block ^ 1], xt[left_block])
            local = jnp.where(listed < 0, -1, (listed & (block - 1)) + half)
            chooser = (rows == local).astype(BF16)
            chosen = jnp.dot(pair, chooser, preferred_element_type=F32).astype(BF16)
            g[k * channels : (k + 1) * channels, p * LANES : (p + 1) * LANES] = chosen
    here = pl.ds(pl.multiple_of(step * window, window), window)
    resp[:, here] = jnp.dot(weights_t[...], g[...], preferred_element_type=F32) * occ[:, here]

    @pl.when(step == pl.num_programs(0) - 1)
    def _():
        count = resp.shape[1] // LANES

        def add(p, carry):
            total, number = carry
            at = pl.ds(pl.multiple_of(p * LANES, LANES), LANES)
            return total + resp[:, at], number + occ[:, at]

        zero = jnp.zeros((channels, LANES), F32)
        total, number = lax.fori_loop(0, count, add, (zero, jnp.zeros((1, LANES), F32)), unroll=4)
        total = jnp.sum(total, axis=1, keepdims=True)
        number = jnp.sum(number, axis=1, keepdims=True)
        mean = total / jnp.maximum(number, 1.0)

        def spread(p, squares):
            at = pl.ds(pl.multiple_of(p * LANES, LANES), LANES)
            centred = (resp[:, at] - mean) * occ[:, at]
            return squares + centred * centred

        squares = lax.fori_loop(0, count, spread, zero, unroll=4)
        squares = jnp.sum(squares, axis=1, keepdims=True)
        columns = jnp.where(lane == 0, total, jnp.where(lane == 1, squares, jnp.broadcast_to(number, (channels, LANES))))
        stats[...] = columns.T[: stats.shape[0], :]


def convolve(source, kmap, arrival, rims, weights_t, block):
    offsets, tile_rows = kmap.shape
    channels = arrival.shape[1]
    window = min(1024, tile_rows)
    ext_blocks = (tile_rows + sum(rim.shape[0] for rim in rims)) // block
    whole = pl.BlockSpec(memory_space=pltpu.VMEM)
    return pl.pallas_call(
        functools.partial(conv_kernel, block),
        grid=(tile_rows // window,),
        in_specs=[
            pl.BlockSpec(memory_space=pltpu.SMEM),
            pl.BlockSpec((offsets, window), lambda q: (0, q)),
            *[whole] * 6,
        ],
        out_specs=[whole, whole, whole],
        out_shape=[
            jax.ShapeDtypeStruct((channels, tile_rows), F32),
            jax.ShapeDtypeStruct((1, tile_rows), F32),
            jax.ShapeDtypeStruct((4, channels), F32),
        ],
        scratch_shapes=[
            pltpu.VMEM((ext_blocks, channels, LANES), BF16),
            pltpu.VMEM((offsets * channels, window), BF16),
        ],
        compiler_params=pltpu.CompilerParams(vmem_limit_bytes=56 * MIB),
        name="convolve",
    )(source, kmap, arrival, *rims, weights_t)


def finish_kernel(population, stats, gain, bias, resp, occ, out, affine):
    @pl.when(pl.program_id(0) == 0)
    def _():
        total, squares, number = stats[:, 0, :], stats[:, 1, :], stats[:, 2, :]
        average = jnp.sum(total, axis=0, keepdims=True) / population
        apart = total / jnp.maximum(number, 1.0) - average
        spread = jnp.sum(squares + number * apart * apart, axis=0, keepdims=True)
        scale = gain[...] / jnp.sqrt(spread / population + 1e-05)
        row = lax.broadcasted_iota(I32, affine.shape, 0)
        rows = jnp.where(row == 0, average, jnp.where(row == 1, scale, bias[...]))
        affine[...] = rows.T

    average, scale, shift = affine[:, 0:1], affine[:, 1:2], affine[:, 2:3]
    for p in range(resp.shape[1] // LANES):
        at = slice(p * LANES, (p + 1) * LANES)
        value = jnp.maximum((resp[:, at] - average) * scale + shift, 0.0) * occ[:, at]
        out[at, :] = value.T.astype(BF16)


def finish(stats, gain, bias, resp, occ, population):
    channels, tile_rows = resp.shape
    window = min(1024, tile_rows)
    return pl.pallas_call(
        functools.partial(finish_kernel, population),
        grid=(tile_rows // window,),
        in_specs=[
            pl.BlockSpec(memory_space=pltpu.VMEM),
            pl.BlockSpec(memory_space=pltpu.VMEM),
            pl.BlockSpec(memory_space=pltpu.VMEM),
            pl.BlockSpec((channels, window), lambda q: (0, q)),
            pl.BlockSpec((1, window), lambda q: (0, q)),
        ],
        out_specs=pl.BlockSpec((window, channels), lambda q: (q, 0)),
        out_shape=jax.ShapeDtypeStruct((tile_rows, channels), BF16),
        scratch_shapes=[pltpu.VMEM((channels, LANES), F32)],
        compiler_params=pltpu.CompilerParams(vmem_limit_bytes=32 * MIB),
        name="finish",
    )(stats, gain.reshape(1, channels), bias.reshape(1, channels), resp, occ)


def shards(voxels, owner_tile, rim_blocks, kernel_map, weights, norm_gain, shift_bias):
    devices = lax.axis_size(AXES)
    offsets, tile_rows = kernel_map.shape[1:]
    pair_rows = tile_rows // devices
    block = pair_rows
    channels = voxels.shape[1]

    def swap(value):
        return lax.all_to_all(value, AXES, split_axis=0, concat_axis=0, tiled=True)

    outgoing = place(voxels, owner_tile[:, 0], tile_rows, pair_rows)
    arrival = swap(outgoing.reshape(devices, pair_rows, channels)).reshape(tile_rows, channels)
    kmap = kernel_map[0]
    source = jnp.maximum(jnp.max(kmap.reshape(offsets, tile_rows // block, block), axis=2), 0) // block
    weights_t = weights.transpose(2, 0, 1).reshape(weights.shape[2], offsets * channels)
    picked = pick(arrival, rim_blocks[0], block)
    rims = (
        from_behind(picked[0], "tx", 1),
        from_behind(picked[1], "tx", -1),
        from_behind(picked[2], "ty", 1),
        from_behind(picked[3], "ty", -1),
    )
    resp, occ, stats = convolve(source, kmap, arrival, rims, weights_t, block)
    gathered = swap(jnp.broadcast_to(stats[None], (devices, *stats.shape)))
    return finish(gathered, norm_gain, shift_bias, resp, occ, float(voxels.shape[0] * devices))


def solution(mesh):
    return jax.shard_map(
        shards,
        mesh=mesh,
        in_specs=(
            P(AXES, None),
            P(AXES, None),
            P(AXES, None, None),
            P(AXES, None, None),
            P(),
            P(),
            P(),
        ),
        out_specs=P(AXES, None),
        check_vma=False,
    )
```

time: 480 us -> 181 us (0.38)
  matrix products: 156 us -> 0 us
  Pallas kernels: 0 us -> 94.8 us
  local copies, waits for them, and re-layouts: 92.5 us -> 9.31 us
  blocking collectives: 130 us -> 60.8 us
  other arithmetic: 32.7 us -> 4.73 us
  waiting for transfers between devices: 25.6 us -> 0.75 us
  starting transfers between devices: 31.1 us -> 10 us
  loops' own time: 10.5 us -> 0 us
    dot_general x33 -> x0, matrix products: 156 us -> none  [the longest x16 123 us: convolve(): jnp.einsum('kbrc,kco->bro', chosen, weights, preferred_element_type=jnp.f...]
    psum x2 -> x0, blocking collectives: 130 us -> none  [the longest x1 66.1 us: shards(): average = lax.psum(jnp.sum(response, axis=0), ('tx', 'ty')) / population]
    pallas_call x0 -> x4, Pallas kernels: none -> 94.8 us  [the longest x1 44.2 us: convolve(): pl.pallas_call(functools.partial(conv_kernel, block), grid=(tile_rows //...]
    all_to_all x0 -> x2, blocking collectives: none -> 60.8 us  [swap(): return lax.all_to_all(value, AXES, split_axis=0, concat_axis=0, tiled=True)]
    gather x17 -> x0, local copies, waits for them, and re-layouts: 48.4 us -> none  [the longest x16 46 us: convolve(): fetched = ext_blocks[sources]]
    dynamic_slice x112 -> x0, local copies, waits for them, and re-layouts: 38.2 us -> none  [the longest x96 28.7 us: shards(): lax.map(convolve, (source_groups, local_groups, valid_groups))]
    all_to_all x2 -> x0, starting transfers between devices: 21.7 us -> none  [the longest x1 11.5 us: shards(): lax.all_to_all(filled.reshape(devices, 1), ('tx', 'ty'), split_axis=0, co...]
    all_to_all x2 -> x0, waiting for transfers between devices: 18.5 us -> none  [the longest x1 18.5 us: shards(): lax.all_to_all(outgoing.reshape(devices, pair_rows, channels), ('tx', 'ty...]
  transfers between devices with their start and end apart: 6 -> 4, of which waited for: 4 -> 1; matrix products, arithmetic and copies ran while one was open for 12% -> 4% of each run, Pallas kernels for 0% -> 0%
where the time goes in v1:
time: 181 us; the launch traced here: 180 us
  Pallas kernels  94.8 us (52%)
  blocking collectives  60.8 us (34%)
  starting transfers between devices  10 us (6%)
  local copies, waits for them, and re-layouts  9.31 us (5%)
  other arithmetic  4.73 us (3%)
    all_to_all x2, blocking collectives, swap(): return lax.all_to_all(value, AXES, split_axis=0, concat_axis=0, tiled=True)  60.8 us
    pallas_call x1, Pallas kernels, convolve(): pl.pallas_call(functools.partial(conv_kernel, block), grid=(tile_rows //...  44.2 us
    pallas_call x1, Pallas kernels, pick(): pl.pallas_call(functools.partial(pick_kernel, block), in_specs=[pl.BlockS...  34.3 us
    pallas_call x1, Pallas kernels, place(): pl.pallas_call(functools.partial(place_kernel, pair_rows), out_shape=jax....  11.6 us
    ppermute x4, starting transfers between devices, from_behind(): lax.ppermute(value, axis, [(source, source + steps) for source in range(l...  10 us
    unnamed x20, local copies, waits for them, and re-layouts  6.24 us
    pallas_call x1, Pallas kernels, finish(): pl.pallas_call(functools.partial(finish_kernel, population), grid=(tile_r...  4.7 us
  transfers between devices with their start and end apart: 4, of which 1 were waited for; matrix products, arithmetic and copies ran while one was open for 4% of the time, Pallas kernels for 0%

profile of v1, /device:TPU:1, one launch (start us, length us, event | category | flops | bytes accessed | tf_op | source)
XLA Modules:
  0.0 180.5 jit_solution(4122513158480914487)
XLA Ops:
  0.0 0.5 broadcast.12
  0.5 1.4 reduce.4
  1.9 0.0 copy-start.1
  1.9 1.2 copy-done.1
  3.2 11.6 %place.1 = bf16[8192,128]{1,0:T(8,128)(2,1)S(1)} custom-call(s32[8,512]{1,0:T(8,128)S(1)} %reshape_squeeze.7.owner, bf16[4096,128]{1,0:T(8,128)(2,1)S(1)} %copy-done.1), custom_call_target="tpu_custom_call" | custom-call | tf_op jit(solution)/shard_map/place/pallas_call | solution.py:71
  14.8 41.2 %all_to_all.10 = bf16[128,64,128]{2,1,0:T(8,128)(2,1)} all-to-all(bf16[128,64,128]{2,1,0:T(8,128)(2,1)S(1)} %bitcast.12), channel_id=1, replica_groups=mesh['tx'=8,'ty'=16] {'tx','ty'}, dimensions={0} | all-to-all | bytes 4194304 | tf_op jit(solution)/shard_map/all_to_all | solution.py:268
  56.0 0.0 copy-start.5
  56.0 34.3 %pick_rims.1 = (bf16[1024,128]{1,0:T(8,128)(2,1)}, bf16[1024,128]{1,0:T(8,128)(2,1)}, bf16[1024,128]{1,0:T(8,128)(2,1)}, bf16[1024,128]{1,0:T(8,128)(2,1)}) custom-call(s32[4,16]{1,0:T(4,128)} %bitcast.19, bf16[8192,128]{1,0:T(8,128)(2,1)} %bitcast.15), custom_call_target="tpu_custom_call" | custom-call | tf_op jit(solution)/shard_map/pick_rims/pallas_call | solution.py:109
  90.3 0.0 copy-start.6
  90.3 3.5 %collective-permute-start = (bf16[1024,128]{1,0:T(8,128)(2,1)}, bf16[1024,128]{1,0:T(8,128)(2,1)S(1)}, u32[]{:S(2)}, u32[]{:S(2)}) collective-permute-start(bf16[1024,128]{1,0:T(8,128)(2,1)} %get-tuple-element.12), channel_id=1, source_target_pairs={{0,16},{16,32},{32,48},{48,64},{64,80},{80,96},{96,112},{1,17},{17... | collective-permute-start | bytes 786440 | tf_op jit(solution)/shard_map/ppermute | solution.py:20
  93.8 1.9 %collective-permute-start.1 = (bf16[1024,128]{1,0:T(8,128)(2,1)}, bf16[1024,128]{1,0:T(8,128)(2,1)S(1)}, u32[]{:S(2)}, u32[]{:S(2)}) collective-permute-start(bf16[1024,128]{1,0:T(8,128)(2,1)} %get-tuple-element.13), channel_id=1, source_target_pairs={{16,0},{32,16},{48,32},{64,48},{80,64},{96,80},{112,96},{17,1},{33... | collective-permute-start | bytes 786440 | tf_op jit(solution)/shard_map/ppermute | solution.py:20
  95.7 3.3 %collective-permute-start.2 = (bf16[1024,128]{1,0:T(8,128)(2,1)}, bf16[1024,128]{1,0:T(8,128)(2,1)}, u32[]{:S(2)}, u32[]{:S(2)}) collective-permute-start(bf16[1024,128]{1,0:T(8,128)(2,1)} %get-tuple-element.14), channel_id=1, source_target_pairs={{0,1},{1,2},{2,3},{3,4},{4,5},{5,6},{6,7},{7,8},{8,9},{9,10},{10,1... | collective-permute-start | bytes 786440 | tf_op jit(solution)/shard_map/ppermute | solution.py:20
  99.0 1.3 collective-permute-start.3
  100.3 0.0 copy-done.5
  100.3 1.5 copy.12
  101.8 2.2 %reduce = s32[27,8192]{1,0:T(8,128)S(1)} reduce(s32[1,27,8192]{2,0,1:T(1,128)S(1)} %copy-done.5, s32[]{:T(128)} %constant.16.clone.1), dimensions={0}, to_apply=%param.10.reduce_sub_computation | reduce | bytes 1769476 | tf_op args[3]
  104.0 0.0 copy-done.6
  104.0 1.7 copy.9.weights_t
  105.7 0.7 reshape_squeeze.6
  106.4 0.5 reduce_max.9
  106.9 0.6 add_select_fusion.source
  107.6 0.0 collective-permute-done.rim0
  107.6 0.0 copy-start.7
  107.6 0.0 collective-permute-done.1.rim1
  107.6 0.0 copy-start.8
  107.6 0.0 collective-permute-done.2.rim2
  107.6 0.7 collective-permute-done.3.rim3
  108.3 0.0 copy-done.7
  108.3 0.0 copy-done.8
  108.4 0.0 copy-start.3
  108.4 0.0 copy-start.4
  108.4 44.2 %convolve.1 = (f32[128,8192]{1,0:T(8,128)}, f32[1,8192]{1,0:T(1,128)}, f32[4,128]{1,0:T(4,128)}) custom-call(s32[27,128]{1,0:T(8,128)} %add_select_fusion.source, s32[27,8192]{1,0:T(8,128)} %bitcast.17, bf16[8192,128]{1,0:T(8,128)(2,1)} %bitcast.16, bf16[1024,128]{1,0:T(8,128)(2,1)} %copy-done.7, bf16[1024,128]{1,0:T(8,128)(2,1)} %copy-done.8, ...), custom_call_target="tpu_custom_call" | custom-call | tf_op jit(solution)/shard_map/convolve/pallas_call | solution.py:197
  152.6 0.7 broadcast_in_dim.2
  153.3 19.6 %all_to_all.11.stats = f32[128,4,128]{2,1,0:T(4,128)S(1)} all-to-all(f32[128,4,128]{2,1,0:T(4,128)S(1)} %broadcast_in_dim.2), channel_id=1, replica_groups=mesh['tx'=8,'ty'=16] {'tx','ty'}, dimensions={0} | all-to-all | bytes 524288 | tf_op jit(solution)/shard_map/all_to_all | solution.py:268
  172.8 0.0 copy-done.3
  172.8 0.0 copy-done.4
  172.8 0.0 copy-start
  172.8 2.2 %copy-done = f32[128,8192]{1,0:T(8,128)S(1)} copy-done((f32[128,8192]{1,0:T(8,128)S(1)}, f32[128,8192]{1,0:T(8,128)}, u32[]{:S(2)}) %copy-start) | copy-done | bytes 4194328
  175.0 0.0 copy-start.2
  175.0 0.8 copy-done.2
  175.8 4.7 %finish.1 = bf16[8192,128]{1,0:T(8,128)(2,1)} custom-call(f32[128,4,128]{2,1,0:T(4,128)S(1)} %all_to_all.11.stats, f32[1,128]{1,0:T(1,128)S(1)} %bitcast.13, f32[1,128]{1,0:T(1,128)S(1)} %bitcast.14, f32[128,8192]{1,0:T(8,128)S(1)} %copy-done, f32[1,8192]{1,0:T(1,128)S(1)} %copy-done.2), custom_call_target="tpu_custom_call" | custom-call | tf_op jit(solution)/shard_map/finish/pallas_call | solution.py:242
  (1 shorter events, 0.0 us)
Async XLA Ops:
  1.9 1.2 copy-start.1
  56.0 44.4 %copy-start.5 = (s32[1,27,8192]{2,0,1:T(1,128)S(1)}, s32[1,27,8192]{2,0,1:T(1,128)}, u32[]{:S(2)}) copy-start(s32[1,27,8192]{2,0,1:T(1,128)} %param.10) | copy-start | bytes 2654212
  90.3 13.7 %copy-start.6 = (bf16[27,128,128]{2,1,0:T(8,128)(2,1)S(1)}, bf16[27,128,128]{2,1,0:T(8,128)(2,1)}, u32[]{:S(2)}) copy-start(bf16[27,128,128]{2,1,0:T(8,128)(2,1)} %param.11) | copy-start | bytes 2654212
  90.3 17.3 %collective-permute-start = (bf16[1024,128]{1,0:T(8,128)(2,1)}, bf16[1024,128]{1,0:T(8,128)(2,1)S(1)}, u32[]{:S(2)}, u32[]{:S(2)}) collective-permute-start(bf16[1024,128]{1,0:T(8,128)(2,1)} %get-tuple-element.12), channel_id=1, source_target_pairs={{0,16},{16,32},{32,48},{48,64},{64,80},{80,96},{96,112},{1,17},{17... | collective-permute-start | bytes 786440 | tf_op jit(solution)/shard_map/ppermute | solution.py:20
  93.8 13.8 %collective-permute-start.1 = (bf16[1024,128]{1,0:T(8,128)(2,1)}, bf16[1024,128]{1,0:T(8,128)(2,1)S(1)}, u32[]{:S(2)}, u32[]{:S(2)}) collective-permute-start(bf16[1024,128]{1,0:T(8,128)(2,1)} %get-tuple-element.13), channel_id=1, source_target_pairs={{16,0},{32,16},{48,32},{64,48},{80,64},{96,80},{112,96},{17,1},{33... | collective-permute-start | bytes 786440 | tf_op jit(solution)/shard_map/ppermute | solution.py:20
  95.7 11.9 %collective-permute-start.2 = (bf16[1024,128]{1,0:T(8,128)(2,1)}, bf16[1024,128]{1,0:T(8,128)(2,1)}, u32[]{:S(2)}, u32[]{:S(2)}) collective-permute-start(bf16[1024,128]{1,0:T(8,128)(2,1)} %get-tuple-element.14), channel_id=1, source_target_pairs={{0,1},{1,2},{2,3},{3,4},{4,5},{5,6},{6,7},{7,8},{8,9},{9,10},{10,1... | collective-permute-start | bytes 786440 | tf_op jit(solution)/shard_map/ppermute | solution.py:20
  99.0 9.3 %collective-permute-start.3 = (bf16[1024,128]{1,0:T(8,128)(2,1)}, bf16[1024,128]{1,0:T(8,128)(2,1)}, u32[]{:S(2)}, u32[]{:S(2)}) collective-permute-start(bf16[1024,128]{1,0:T(8,128)(2,1)} %get-tuple-element.15), channel_id=1, source_target_pairs={{1,0},{2,1},{3,2},{4,3},{5,4},{6,5},{7,6},{8,7},{9,8},{10,9},{11,1... | collective-permute-start | bytes 786440 | tf_op jit(solution)/shard_map/ppermute | solution.py:20
  107.6 0.8 copy-start.7
  107.6 0.8 copy-start.8
  108.4 64.5 %copy-start.3 = (f32[128]{0:T(128)S(1)}, f32[128]{0:T(128)}, u32[]{:S(2)}) copy-start(f32[128]{0:T(128)} %param.12) | copy-start | bytes 1540
  108.4 64.5 %copy-start.4 = (f32[128]{0:T(128)S(1)}, f32[128]{0:T(128)}, u32[]{:S(2)}) copy-start(f32[128]{0:T(128)} %param.13) | copy-start | bytes 1540
  172.8 2.2 %copy-start = (f32[128,8192]{1,0:T(8,128)S(1)}, f32[128,8192]{1,0:T(8,128)}, u32[]{:S(2)}) copy-start(f32[128,8192]{1,0:T(8,128)} %get-tuple-element.17.resp) | copy-start | bytes 12582916
  175.0 0.8 copy-start.2

commit v2 on v1

--- a/solution.py
+++ b/solution.py
@@ -83,24 +83,12 @@
     )(owner.reshape(runs, rows // runs), voxels)
 
 
-def pick_kernel(block, listed, arrival, *rest):
-    outs, sems = rest[:-1], rest[-1]
+def pick_kernel(block, listed, arrival, *outs):
     count = outs[0].shape[0] // block
-    copies = []
     for d, out in enumerate(outs):
         for i in range(count):
-            source = pl.multiple_of(listed[d, i] * block, block)
-            copies.append(
-                pltpu.make_async_copy(
-                    arrival.at[pl.ds(source, block), :],
-                    out.at[pl.ds(i * block, block), :],
-                    sems.at[d * count + i],
-                )
-            )
-    for copy in copies:
-        copy.start()
-    for copy in copies:
-        copy.wait()
+            at = pl.multiple_of(listed[d, i] * block, block)
+            out[i * block : (i + 1) * block, :] = arrival[pl.ds(at, block), :]
 
 
 def pick(arrival, listed, block):
@@ -110,13 +98,36 @@
         functools.partial(pick_kernel, block),
         in_specs=[
             pl.BlockSpec(memory_space=pltpu.SMEM),
-            pl.BlockSpec(memory_space=pl.ANY),
-        ],
-        out_specs=[pl.BlockSpec(memory_space=pl.ANY)] * directions,
+            pl.BlockSpec(memory_space=pltpu.VMEM),
+        ],
+        out_specs=[pl.BlockSpec(memory_space=pltpu.VMEM)] * directions,
         out_shape=[shape] * directions,
-        scratch_shapes=[pltpu.SemaphoreType.DMA((directions * count,))],
+        compiler_params=pltpu.CompilerParams(vmem_limit_bytes=16 * MIB),
         name="pick_rims",
     )(listed, arrival)
+
+
+def source_kernel(block, kmap, out):
+    offsets, tile_rows = kmap.shape
+    lane = lax.broadcasted_iota(I32, (offsets, LANES), 1)
+    right = lane >= block
+    found = jnp.zeros((offsets, LANES), I32)
+    for p in range(tile_rows // LANES):
+        listed = kmap[:, p * LANES : (p + 1) * LANES]
+        for half, mine in enumerate((jnp.logical_not(right), right)):
+            top = jnp.max(jnp.where(mine, listed, 0), axis=1, keepdims=True)
+            found = jnp.where(lane == 2 * p + half, top, found)
+    out[...] = found // block
+
+
+def source_blocks(kmap, block):
+    offsets, tile_rows = kmap.shape
+    return pl.pallas_call(
+        functools.partial(source_kernel, block),
+        out_shape=jax.ShapeDtypeStruct((offsets, tile_rows // block), I32),
+        compiler_params=pltpu.CompilerParams(vmem_limit_bytes=16 * MIB),
+        name="source_blocks",
+    )(kmap)
 
 
 def conv_kernel(block, source, kmap, arrival, rim0, rim1, rim2, rim3, weights_t, resp, occ, stats, xt, g):
@@ -131,21 +142,25 @@
 
     @pl.when(step == 0)
     def _():
+        same = (rows == lane).astype(BF16)
         first = 0
         for number, part in enumerate((arrival, rim0, rim1, rim2, rim3)):
             pairs = part.shape[0] // LANES
 
             def turn(p, carry, part=part, first=first, number=number):
                 at = pl.multiple_of(p * LANES, LANES)
-                turned = part[pl.ds(at, LANES), :].astype(F32).T
+                straight = part[pl.ds(at, LANES), :]
+                swapped = jnp.concatenate((straight[block:], straight[:block]), axis=0)
+                both = jnp.concatenate((straight, swapped), axis=0)
+                turned = lax.dot_general(same, both, (((1,), (1,)), ((), ())), preferred_element_type=F32)
                 if number == 0:
-                    occ[:, pl.ds(at, LANES)] = (turned[0:1, :] >= 0.0).astype(F32)
-                turned = jnp.maximum(turned, 0.0)
-                xt[first + 2 * p] = turned.astype(BF16)
-                xt[first + 2 * p + 1] = pltpu.roll(turned, block, 1).astype(BF16)
+                    occ[:, pl.ds(at, LANES)] = (turned[0:1, :LANES] >= 0.0).astype(F32)
+                turned = jnp.maximum(turned, 0.0).astype(BF16)
+                xt[first + 2 * p] = turned[:, :LANES]
+                xt[first + 2 * p + 1] = turned[:, LANES:]
                 return carry
 
-            lax.fori_loop(0, pairs, turn, 0, unroll=2)
+            lax.fori_loop(0, pairs, turn, 0, unroll=4)
             first += 2 * pairs
 
     blocks = window // block
@@ -270,7 +285,7 @@
     outgoing = place(voxels, owner_tile[:, 0], tile_rows, pair_rows)
     arrival = swap(outgoing.reshape(devices, pair_rows, channels)).reshape(tile_rows, channels)
     kmap = kernel_map[0]
-    source = jnp.maximum(jnp.max(kmap.reshape(offsets, tile_rows // block, block), axis=2), 0) // block
+    source = source_blocks(kmap, block)
     weights_t = weights.transpose(2, 0, 1).reshape(weights.shape[2], offsets * channels)
     picked = pick(arrival, rim_blocks[0], block)
     rims = (

time: 181 us -> 144 us (0.80)
  Pallas kernels: 94.8 us -> 59.7 us
  other arithmetic: 4.73 us -> 1.4 us
    pallas_call x1, Pallas kernels: 34.3 us -> 0.65 us  [pick(): pl.pallas_call(functools.partial(pick_kernel, block), in_specs=[pl.BlockS...]
    pallas_call x1, Pallas kernels: 44.2 us -> 41.4 us  [convolve(): pl.pallas_call(functools.partial(conv_kernel, block), grid=(tile_rows //...]
    unnamed x2 -> x1, other arithmetic: 3.57 us -> 1.4 us
    unnamed x20 -> x22, local copies, waits for them, and re-layouts: 6.24 us -> 6.99 us
  transfers between devices with their start and end apart: 4 -> 4, of which waited for: 1 -> 1; matrix products, arithmetic and copies ran while one was open for 4% -> 3% of each run, Pallas kernels for 0% -> 1%
where the time goes in v2:
time: 144 us
  blocking collectives  60.7 us (42%)
  Pallas kernels  59.7 us (41%)
  local copies, waits for them, and re-layouts  9.96 us (7%)
  starting transfers between devices  9.89 us (7%)
  waiting for transfers between devices  1.86 us (1%)
    all_to_all x2, blocking collectives, swap(): return lax.all_to_all(value, AXES, split_axis=0, concat_axis=0, tiled=True)  60.7 us
    pallas_call x1, Pallas kernels, convolve(): pl.pallas_call(functools.partial(conv_kernel, block), grid=(tile_rows //...  41.4 us
    pallas_call x1, Pallas kernels, place(): pl.pallas_call(functools.partial(place_kernel, pair_rows), out_shape=jax....  11.6 us
    ppermute x4, starting transfers between devices, from_behind(): lax.ppermute(value, axis, [(source, source + steps) for source in range(l...  9.89 us
    unnamed x22, local copies, waits for them, and re-layouts  6.99 us
    pallas_call x1, Pallas kernels, finish(): pl.pallas_call(functools.partial(finish_kernel, population), grid=(tile_r...  4.7 us
  transfers between devices with their start and end apart: 4, of which 1 were waited for; matrix products, arithmetic and copies ran while one was open for 3% of the time, Pallas kernels for 1%

profile of v2, /device:TPU:1, one launch (start us, length us, event | category | flops | bytes accessed | tf_op | source)
XLA Modules:
  0.0 143.6 jit_solution(17180921213142793439)
XLA Ops:
  0.0 0.5 broadcast.4
  0.5 1.4 reduce.3
  1.9 0.0 copy-start.3
  1.9 1.2 copy-done.3
  3.2 11.6 %place.1 = bf16[8192,128]{1,0:T(8,128)(2,1)S(1)} custom-call(s32[8,512]{1,0:T(8,128)S(1)} %reshape_squeeze.3.owner, bf16[4096,128]{1,0:T(8,128)(2,1)S(1)} %copy-done.3), custom_call_target="tpu_custom_call" | custom-call | tf_op jit(solution)/shard_map/place/pallas_call | solution.py:71
  14.8 0.0 copy-start.6
  14.8 41.1 %all_to_all.10 = bf16[128,64,128]{2,1,0:T(8,128)(2,1)S(1)} all-to-all(bf16[128,64,128]{2,1,0:T(8,128)(2,1)S(1)} %bitcast.16), channel_id=1, replica_groups=mesh['tx'=8,'ty'=16] {'tx','ty'}, dimensions={0} | all-to-all | bytes 4194304 | tf_op jit(solution)/shard_map/all_to_all | solution.py:283
  55.9 0.0 copy-start
  55.9 0.0 copy-done.6
  55.9 0.7 pick_rims.1
  56.5 3.4 %collective-permute-start = (bf16[1024,128]{1,0:T(8,128)(2,1)S(1)}, bf16[1024,128]{1,0:T(8,128)(2,1)S(1)}, u32[]{:S(2)}, u32[]{:S(2)}) collective-permute-start(bf16[1024,128]{1,0:T(8,128)(2,1)S(1)} %get-tuple-element.12), channel_id=1, source_target_pairs={{0,16},{16,32},{32,48},{48,64},{64,80},{80,96},{96,112},{1,17},{17... | collective-permute-start | bytes 786440 | tf_op jit(solution)/shard_map/ppermute | solution.py:20
  59.9 1.9 %collective-permute-start.1 = (bf16[1024,128]{1,0:T(8,128)(2,1)S(1)}, bf16[1024,128]{1,0:T(8,128)(2,1)}, u32[]{:S(2)}, u32[]{:S(2)}) collective-permute-start(bf16[1024,128]{1,0:T(8,128)(2,1)S(1)} %get-tuple-element.13), channel_id=1, source_target_pairs={{16,0},{32,16},{48,32},{64,48},{80,64},{96,80},{112,96},{17,1},{33... | collective-permute-start | bytes 786440 | tf_op jit(solution)/shard_map/ppermute | solution.py:20
  61.8 3.3 %collective-permute-start.2 = (bf16[1024,128]{1,0:T(8,128)(2,1)S(1)}, bf16[1024,128]{1,0:T(8,128)(2,1)}, u32[]{:S(2)}, u32[]{:S(2)}) collective-permute-start(bf16[1024,128]{1,0:T(8,128)(2,1)S(1)} %get-tuple-element.14), channel_id=1, source_target_pairs={{0,1},{1,2},{2,3},{3,4},{4,5},{5,6},{6,7},{7,8},{8,9},{9,10},{10,1... | collective-permute-start | bytes 786440 | tf_op jit(solution)/shard_map/ppermute | solution.py:20
  65.2 1.3 collective-permute-start.3
  66.5 2.3 %copy.9.weights_t = bf16[128,3456]{1,0:T(8,128)(2,1)} copy(bf16[128,3456]{0,1:T(8,128)(2,1)} %bitcast.20) | data formatting | bytes 1769472 | tf_op jit(solution)/shard_map/reshape | solution.py:289
  68.7 1.7 %copy.12 = s32[1,27,8192]{2,1,0:T(8,128)S(1)} copy(s32[1,27,8192]{2,0,1:T(1,128)} %param.10) | data formatting | bytes 1769472
  70.4 0.0 copy-done
  70.4 0.0 copy-start.1
  70.4 1.3 source_blocks.1.source
  71.8 0.0 copy-start.4
  71.8 0.6 copy-done.4
  72.4 0.0 copy-start.7
  72.4 0.0 copy-start.8
  72.4 0.0 collective-permute-done.rim0
  72.4 0.0 copy-start.9
  72.4 0.0 collective-permute-done.1.rim1
  72.4 0.0 collective-permute-done.2.rim2
  72.4 1.9 %collective-permute-done.3.rim3 = bf16[1024,128]{1,0:T(8,128)(2,1)} collective-permute-done((bf16[1024,128]{1,0:T(8,128)(2,1)S(1)}, bf16[1024,128]{1,0:T(8,128)(2,1)}, u32[]{:S(2)}, u32[]{:S(2)}) %collective-permute-start.3) | collective-permute-done | bytes 262176 | tf_op jit(solution)/shard_map/ppermute | solution.py:20
  74.3 0.0 copy-done.1
  74.3 0.0 copy-done.9
  74.3 41.4 %convolve.1 = (f32[128,8192]{1,0:T(8,128)}, f32[1,8192]{1,0:T(1,128)}, f32[4,128]{1,0:T(4,128)}) custom-call(s32[27,128]{1,0:T(8,128)} %copy-done.4, s32[27,8192]{1,0:T(8,128)} %bitcast.15, bf16[8192,128]{1,0:T(8,128)(2,1)} %bitcast.13, bf16[1024,128]{1,0:T(8,128)(2,1)} %copy-done.9, bf16[1024,128]{1,0:T(8,128)(2,1)} %collective-permute-done.1.rim1, ...), custom_call_target="tpu_custom_call" | custom-call | tf_op jit(solution)/shard_map/convolve/pallas_call | solution.py:212
  115.6 0.7 broadcast_in_dim.2
  116.3 19.6 %all_to_all.11.stats = f32[128,4,128]{2,1,0:T(4,128)S(1)} all-to-all(f32[128,4,128]{2,1,0:T(4,128)S(1)} %broadcast_in_dim.2), channel_id=1, replica_groups=mesh['tx'=8,'ty'=16] {'tx','ty'}, dimensions={0} | all-to-all | bytes 524288 | tf_op jit(solution)/shard_map/all_to_all | solution.py:283
  135.9 0.0 copy-done.7
  135.9 0.0 copy-done.8
  135.9 0.0 copy-start.2
  135.9 2.2 %copy-done.2 = f32[128,8192]{1,0:T(8,128)S(1)} copy-done((f32[128,8192]{1,0:T(8,128)S(1)}, f32[128,8192]{1,0:T(8,128)}, u32[]{:S(2)}) %copy-start.2) | copy-done | bytes 4194328
  138.1 0.0 copy-start.5
  138.1 0.8 copy-done.5
  138.9 4.7 %finish.1 = bf16[8192,128]{1,0:T(8,128)(2,1)} custom-call(f32[128,4,128]{2,1,0:T(4,128)S(1)} %all_to_all.11.stats, f32[1,128]{1,0:T(1,128)S(1)} %bitcast.18, f32[1,128]{1,0:T(1,128)S(1)} %bitcast.19, f32[128,8192]{1,0:T(8,128)S(1)} %copy-done.2, f32[1,8192]{1,0:T(1,128)S(1)} %copy-done.5), custom_call_target="tpu_custom_call" | custom-call | tf_op jit(solution)/shard_map/finish/pallas_call | solution.py:257
  (1 shorter events, 0.0 us)
Async XLA Ops:
  1.9 1.2 copy-start.3
  14.8 41.1 %copy-start.6 = (s32[1,4,16]{2,1,0:T(4,128)S(1)}, s32[1,4,16]{2,1,0:T(4,128)}, u32[]{:S(2)}) copy-start(s32[1,4,16]{2,1,0:T(4,128)} %param.9) | copy-start | bytes 772
  55.9 14.5 %copy-start = (bf16[128,64,128]{2,1,0:T(8,128)(2,1)}, bf16[128,64,128]{2,1,0:T(8,128)(2,1)S(1)}, u32[]{:S(2)}) copy-start(bf16[128,64,128]{2,1,0:T(8,128)(2,1)S(1)} %all_to_all.10) | copy-start | bytes 6291460
  56.5 15.8 %collective-permute-start = (bf16[1024,128]{1,0:T(8,128)(2,1)S(1)}, bf16[1024,128]{1,0:T(8,128)(2,1)S(1)}, u32[]{:S(2)}, u32[]{:S(2)}) collective-permute-start(bf16[1024,128]{1,0:T(8,128)(2,1)S(1)} %get-tuple-element.12), channel_id=1, source_target_pairs={{0,16},{16,32},{32,48},{48,64},{64,80},{80,96},{96,112},{1,17},{17... | collective-permute-start | bytes 786440 | tf_op jit(solution)/shard_map/ppermute | solution.py:20
  59.9 12.5 %collective-permute-start.1 = (bf16[1024,128]{1,0:T(8,128)(2,1)S(1)}, bf16[1024,128]{1,0:T(8,128)(2,1)}, u32[]{:S(2)}, u32[]{:S(2)}) collective-permute-start(bf16[1024,128]{1,0:T(8,128)(2,1)S(1)} %get-tuple-element.13), channel_id=1, source_target_pairs={{16,0},{32,16},{48,32},{64,48},{80,64},{96,80},{112,96},{17,1},{33... | collective-permute-start | bytes 786440 | tf_op jit(solution)/shard_map/ppermute | solution.py:20
  61.8 10.6 %collective-permute-start.2 = (bf16[1024,128]{1,0:T(8,128)(2,1)S(1)}, bf16[1024,128]{1,0:T(8,128)(2,1)}, u32[]{:S(2)}, u32[]{:S(2)}) collective-permute-start(bf16[1024,128]{1,0:T(8,128)(2,1)S(1)} %get-tuple-element.14), channel_id=1, source_target_pairs={{0,1},{1,2},{2,3},{3,4},{4,5},{5,6},{6,7},{7,8},{8,9},{9,10},{10,1... | collective-permute-start | bytes 786440 | tf_op jit(solution)/shard_map/ppermute | solution.py:20
  65.2 9.1 %collective-permute-start.3 = (bf16[1024,128]{1,0:T(8,128)(2,1)S(1)}, bf16[1024,128]{1,0:T(8,128)(2,1)}, u32[]{:S(2)}, u32[]{:S(2)}) collective-permute-start(bf16[1024,128]{1,0:T(8,128)(2,1)S(1)} %get-tuple-element.15), channel_id=1, source_target_pairs={{1,0},{2,1},{3,2},{4,3},{5,4},{6,5},{7,6},{8,7},{9,8},{10,9},{11,1... | collective-permute-start | bytes 786440 | tf_op jit(solution)/shard_map/ppermute | solution.py:20
  70.4 3.8 %copy-start.1 = (s32[1,27,8192]{2,1,0:T(8,128)}, s32[1,27,8192]{2,1,0:T(8,128)S(1)}, u32[]{:S(2)}) copy-start(s32[1,27,8192]{2,1,0:T(8,128)S(1)} %copy.12) | copy-start | bytes 2654212
  71.8 0.6 copy-start.4
  72.4 63.6 %copy-start.7 = (f32[128]{0:T(128)S(1)}, f32[128]{0:T(128)}, u32[]{:S(2)}) copy-start(f32[128]{0:T(128)} %param.12) | copy-start | bytes 1540
  72.4 63.6 %copy-start.8 = (f32[128]{0:T(128)S(1)}, f32[128]{0:T(128)}, u32[]{:S(2)}) copy-start(f32[128]{0:T(128)} %param.13) | copy-start | bytes 1540
  72.4 1.9 %copy-start.9 = (bf16[1024,128]{1,0:T(8,128)(2,1)}, bf16[1024,128]{1,0:T(8,128)(2,1)S(1)}, u32[]{:S(2)}) copy-start(bf16[1024,128]{1,0:T(8,128)(2,1)S(1)} %collective-permute-done.rim0) | copy-start | bytes 786436
  135.9 2.2 %copy-start.2 = (f32[128,8192]{1,0:T(8,128)S(1)}, f32[128,8192]{1,0:T(8,128)}, u32[]{:S(2)}) copy-start(f32[128,8192]{1,0:T(8,128)} %get-tuple-element.17.resp) | copy-start | bytes 12582916
  138.1 0.8 copy-start.5

commit v3 on v2

--- a/solution.py
+++ b/solution.py
@@ -108,12 +108,12 @@
 
 
 def source_kernel(block, kmap, out):
-    offsets, tile_rows = kmap.shape
+    offsets, tile_rows = kmap.shape[0], kmap.shape[2]
     lane = lax.broadcasted_iota(I32, (offsets, LANES), 1)
     right = lane >= block
     found = jnp.zeros((offsets, LANES), I32)
     for p in range(tile_rows // LANES):
-        listed = kmap[:, p * LANES : (p + 1) * LANES]
+        listed = kmap[:, 0, p * LANES : (p + 1) * LANES]
         for half, mine in enumerate((jnp.logical_not(right), right)):
             top = jnp.max(jnp.where(mine, listed, 0), axis=1, keepdims=True)
             found = jnp.where(lane == 2 * p + half, top, found)
@@ -121,7 +121,7 @@
 
 
 def source_blocks(kmap, block):
-    offsets, tile_rows = kmap.shape
+    offsets, _, tile_rows = kmap.shape
     return pl.pallas_call(
         functools.partial(source_kernel, block),
         out_shape=jax.ShapeDtypeStruct((offsets, tile_rows // block), I32),
@@ -130,106 +130,159 @@
     )(kmap)
 
 
-def conv_kernel(block, source, kmap, arrival, rim0, rim1, rim2, rim3, weights_t, resp, occ, stats, xt, g):
-    step = pl.program_id(0)
-    offsets, window = kmap.shape
+def same_of(channels):
+    row = lax.broadcasted_iota(I32, (channels, channels), 0)
+    lane = lax.broadcasted_iota(I32, (channels, channels), 1)
+    return (row == lane).astype(BF16)
+
+
+def turned(same, rows):
+    return lax.dot_general(same, rows, (((1,), (1,)), ((), ())), preferred_element_type=F32)
+
+
+def turn_pair(same, part, p, block):
+    straight = part[pl.ds(pl.multiple_of(p * LANES, LANES), LANES), :]
+    swapped = jnp.concatenate((straight[block:], straight[:block]), axis=0)
+    return turned(same, jnp.concatenate((straight, swapped), axis=0))
+
+
+def turn_kernel(block, arrival, weights, xt, occ, weights_t):
     channels = arrival.shape[1]
+    same = same_of(channels)
+
+    def turn(p, carry):
+        both = turn_pair(same, arrival, p, block)
+        occ[:, pl.ds(pl.multiple_of(p * LANES, LANES), LANES)] = (both[0:1, :LANES] >= 0.0).astype(F32)
+        both = jnp.maximum(both, 0.0).astype(BF16)
+        xt[2 * p] = both[:, :LANES]
+        xt[2 * p + 1] = both[:, LANES:]
+        return carry
+
+    lax.fori_loop(0, arrival.shape[0] // LANES, turn, 0, unroll=8)
+    for k in range(weights.shape[0]):
+        weights_t[:, k * channels : (k + 1) * channels] = turned(same, weights[k]).astype(BF16)
+
+
+def turn_local(arrival, weights, block):
+    tile_rows, channels = arrival.shape
+    offsets = weights.shape[0]
+    return pl.pallas_call(
+        functools.partial(turn_kernel, block),
+        out_shape=[
+            jax.ShapeDtypeStruct((tile_rows // block, channels, LANES), BF16),
+            jax.ShapeDtypeStruct((1, tile_rows), F32),
+            jax.ShapeDtypeStruct((weights.shape[2], offsets * channels), BF16),
+        ],
+        compiler_params=pltpu.CompilerParams(vmem_limit_bytes=16 * MIB),
+        name="turn_local",
+    )(arrival, weights)
+
+
+def conv_kernel(block, window, source, kmap, xt_local, rim0, rim1, rim2, rim3, weights_t, occ, resp, stats, xt, g):
+    offsets, tile_rows = kmap.shape[0], kmap.shape[2]
+    channels = xt_local.shape[1]
+    same = same_of(channels)
     lane = lax.broadcasted_iota(I32, (channels, LANES), 1)
     right = lane >= block
-    lane_row = lax.broadcasted_iota(I32, (1, LANES), 1)
-    half = jnp.where(lane_row >= block, block, 0)
-    rows = lax.broadcasted_iota(I32, (LANES, LANES), 0)
-
-    @pl.when(step == 0)
-    def _():
-        same = (rows == lane).astype(BF16)
-        first = 0
-        for number, part in enumerate((arrival, rim0, rim1, rim2, rim3)):
-            pairs = part.shape[0] // LANES
-
-            def turn(p, carry, part=part, first=first, number=number):
-                at = pl.multiple_of(p * LANES, LANES)
-                straight = part[pl.ds(at, LANES), :]
-                swapped = jnp.concatenate((straight[block:], straight[:block]), axis=0)
-                both = jnp.concatenate((straight, swapped), axis=0)
-                turned = lax.dot_general(same, both, (((1,), (1,)), ((), ())), preferred_element_type=F32)
-                if number == 0:
-                    occ[:, pl.ds(at, LANES)] = (turned[0:1, :LANES] >= 0.0).astype(F32)
-                turned = jnp.maximum(turned, 0.0).astype(BF16)
-                xt[first + 2 * p] = turned[:, :LANES]
-                xt[first + 2 * p + 1] = turned[:, LANES:]
-                return carry
-
-            lax.fori_loop(0, pairs, turn, 0, unroll=4)
-            first += 2 * pairs
+    half = jnp.where(lax.broadcasted_iota(I32, (1, LANES), 1) >= block, block, 0)
+    rows16 = lax.broadcasted_iota(I32, (LANES, LANES), 0).astype(jnp.int16)
+    none = jnp.zeros((LANES, LANES), BF16)
+
+    def keep(i, carry):
+        xt[i] = xt_local[i]
+        return carry
+
+    first = xt_local.shape[0]
+    lax.fori_loop(0, first, keep, 0, unroll=8)
+    for part in (rim0, rim1, rim2, rim3):
+        pairs = part.shape[0] // LANES
+
+        def turn(p, carry, part=part, first=first):
+            both = jnp.maximum(turn_pair(same, part, p, block), 0.0).astype(BF16)
+            xt[first + 2 * p] = both[:, :LANES]
+            xt[first + 2 * p + 1] = both[:, LANES:]
+            return carry
+
+        lax.fori_loop(0, pairs, turn, 0, unroll=8)
+        first += 2 * pairs
 
     blocks = window // block
-    for k in range(offsets):
-        for p in range(window // LANES):
-            listed = kmap[k : k + 1, p * LANES : (p + 1) * LANES]
+
+    def convolve_window(step, total):
+        def pair_of(k, p):
             left_block = source[k, blocks * step + 2 * p]
             right_block = source[k, blocks * step + 2 * p + 1]
-            pair = jnp.where(right, xt[right_block ^ 1], xt[left_block])
+            return jnp.where(right, xt[right_block ^ 1], xt[left_block])
+
+        def chooser_of(k, p):
+            at = pl.ds(pl.multiple_of(step * window, window) + p * LANES, LANES)
+            listed = kmap[k, :, at]
             local = jnp.where(listed < 0, -1, (listed & (block - 1)) + half)
-            chooser = (rows == local).astype(BF16)
-            chosen = jnp.dot(pair, chooser, preferred_element_type=F32).astype(BF16)
-            g[k * channels : (k + 1) * channels, p * LANES : (p + 1) * LANES] = chosen
-    here = pl.ds(pl.multiple_of(step * window, window), window)
-    resp[:, here] = jnp.dot(weights_t[...], g[...], preferred_element_type=F32) * occ[:, here]
-
-    @pl.when(step == pl.num_programs(0) - 1)
-    def _():
-        count = resp.shape[1] // LANES
-
-        def add(p, carry):
-            total, number = carry
-            at = pl.ds(pl.multiple_of(p * LANES, LANES), LANES)
-            return total + resp[:, at], number + occ[:, at]
-
-        zero = jnp.zeros((channels, LANES), F32)
-        total, number = lax.fori_loop(0, count, add, (zero, jnp.zeros((1, LANES), F32)), unroll=4)
-        total = jnp.sum(total, axis=1, keepdims=True)
-        number = jnp.sum(number, axis=1, keepdims=True)
-        mean = total / jnp.maximum(number, 1.0)
-
-        def spread(p, squares):
-            at = pl.ds(pl.multiple_of(p * LANES, LANES), LANES)
-            centred = (resp[:, at] - mean) * occ[:, at]
-            return squares + centred * centred
-
-        squares = lax.fori_loop(0, count, spread, zero, unroll=4)
-        squares = jnp.sum(squares, axis=1, keepdims=True)
-        columns = jnp.where(lane == 0, total, jnp.where(lane == 1, squares, jnp.broadcast_to(number, (channels, LANES))))
-        stats[...] = columns.T[: stats.shape[0], :]
-
-
-def convolve(source, kmap, arrival, rims, weights_t, block):
-    offsets, tile_rows = kmap.shape
-    channels = arrival.shape[1]
+            local = jnp.broadcast_to(local, (LANES, LANES)).astype(jnp.int16)
+            return jnp.where(rows16 == local, jnp.ones((), BF16), jnp.zeros((), BF16))
+
+        for k in range(offsets):
+            for p in range(0, window // LANES, 2):
+                to = slice(k * channels, (k + 1) * channels)
+                if k == offsets // 2:
+                    for q in (p, p + 1):
+                        g[to, q * LANES : (q + 1) * LANES] = xt[blocks * step + 2 * q]
+                    continue
+                pairs = jnp.concatenate((pair_of(k, p), pair_of(k, p + 1)), axis=1)
+                chooser = jnp.concatenate(
+                    (
+                        jnp.concatenate((chooser_of(k, p), none), axis=1),
+                        jnp.concatenate((none, chooser_of(k, p + 1)), axis=1),
+                    ),
+                    axis=0,
+                )
+                chosen = jnp.dot(pairs, chooser, preferred_element_type=F32).astype(BF16)
+                g[to, p * LANES : (p + 2) * LANES] = chosen
+        here = pl.ds(pl.multiple_of(step * window, window), window)
+        value = jnp.dot(weights_t[...], g[...], preferred_element_type=F32) * occ[:, here]
+        resp[:, here] = value
+        for p in range(window // LANES):
+            total = total + value[:, p * LANES : (p + 1) * LANES]
+        return total
+
+    zero = jnp.zeros((channels, LANES), F32)
+    total = lax.fori_loop(0, tile_rows // window, convolve_window, zero)
+    total = jnp.sum(total, axis=1, keepdims=True)
+    number = jnp.sum(occ[...], axis=1, keepdims=True)
+    mean = total / jnp.maximum(number, 1.0)
+
+    def spread(p, squares):
+        at = pl.ds(pl.multiple_of(p * LANES, LANES), LANES)
+        centred = (resp[:, at] - mean) * occ[:, at]
+        return squares + centred * centred
+
+    squares = lax.fori_loop(0, tile_rows // LANES, spread, zero, unroll=4)
+    squares = jnp.sum(squares, axis=1, keepdims=True)
+    columns = jnp.where(lane == 0, total, jnp.where(lane == 1, squares, jnp.broadcast_to(number, (channels, LANES))))
+    stats[...] = columns.T[: stats.shape[0], :]
+
+
+def convolve(source, kmap, xt_local, rims, weights_t, occ, block):
+    offsets, _, tile_rows = kmap.shape
+    local_blocks, channels, _ = xt_local.shape
     window = min(1024, tile_rows)
-    ext_blocks = (tile_rows + sum(rim.shape[0] for rim in rims)) // block
+    ext_blocks = local_blocks + sum(rim.shape[0] for rim in rims) // block
     whole = pl.BlockSpec(memory_space=pltpu.VMEM)
     return pl.pallas_call(
-        functools.partial(conv_kernel, block),
-        grid=(tile_rows // window,),
-        in_specs=[
-            pl.BlockSpec(memory_space=pltpu.SMEM),
-            pl.BlockSpec((offsets, window), lambda q: (0, q)),
-            *[whole] * 6,
-        ],
-        out_specs=[whole, whole, whole],
+        functools.partial(conv_kernel, block, window),
+        in_specs=[pl.BlockSpec(memory_space=pltpu.SMEM), *[whole] * 8],
+        out_specs=[whole, whole],
         out_shape=[
             jax.ShapeDtypeStruct((channels, tile_rows), F32),
-            jax.ShapeDtypeStruct((1, tile_rows), F32),
             jax.ShapeDtypeStruct((4, channels), F32),
         ],
         scratch_shapes=[
             pltpu.VMEM((ext_blocks, channels, LANES), BF16),
             pltpu.VMEM((offsets * channels, window), BF16),
         ],
-        compiler_params=pltpu.CompilerParams(vmem_limit_bytes=56 * MIB),
+        compiler_params=pltpu.CompilerParams(vmem_limit_bytes=40 * MIB),
         name="convolve",
-    )(source, kmap, arrival, *rims, weights_t)
+    )(source, kmap, xt_local, *rims, weights_t, occ)
 
 
 def finish_kernel(population, stats, gain, bias, resp, occ, out, affine):
@@ -282,11 +335,10 @@
     def swap(value):
         return lax.all_to_all(value, AXES, split_axis=0, concat_axis=0, tiled=True)
 
-    outgoing = place(voxels, owner_tile[:, 0], tile_rows, pair_rows)
+    outgoing = place(voxels, owner_tile, tile_rows, pair_rows)
     arrival = swap(outgoing.reshape(devices, pair_rows, channels)).reshape(tile_rows, channels)
-    kmap = kernel_map[0]
+    kmap = kernel_map.transpose(1, 0, 2)
     source = source_blocks(kmap, block)
-    weights_t = weights.transpose(2, 0, 1).reshape(weights.shape[2], offsets * channels)
     picked = pick(arrival, rim_blocks[0], block)
     rims = (
         from_behind(picked[0], "tx", 1),
@@ -294,7 +346,8 @@
         from_behind(picked[2], "ty", 1),
         from_behind(picked[3], "ty", -1),
     )
-    resp, occ, stats = convolve(source, kmap, arrival, rims, weights_t, block)
+    xt, occ, weights_t = turn_local(arrival, weights, block)
+    resp, stats = convolve(source, kmap, xt, rims, weights_t, occ, block)
     gathered = swap(jnp.broadcast_to(stats[None], (devices, *stats.shape)))
     return finish(gathered, norm_gain, shift_bias, resp, occ, float(voxels.shape[0] * devices))
 

time: 144 us -> 127 us (0.88)
  Pallas kernels: 59.7 us -> 49.7 us
  local copies, waits for them, and re-layouts: 9.96 us -> 1.81 us
    pallas_call x1 -> x2, Pallas kernels: 41.4 us -> 31.1 us  [the longest x1 27.9 us: convolve(): pl.pallas_call(functools.partial(conv_kernel, block, window), in_specs=[p...]
    unnamed x22 -> x13, local copies, waits for them, and re-layouts: 6.99 us -> 1.75 us
    reshape x1, local copies, waits for them, and re-layouts: 2.28 us -> 0.01 us  [place(): owner.reshape(runs, rows // runs)]
  transfers between devices with their start and end apart: 4 -> 4, of which waited for: 1 -> 1; matrix products, arithmetic and copies ran while one was open for 3% -> 0% of each run, Pallas kernels for 1% -> 4%
where the time goes in v3:
time: 127 us; the launch traced here: 126 us
  blocking collectives  61.4 us (48%)
  Pallas kernels  49.7 us (39%)
  starting transfers between devices  9.19 us (7%)
  waiting for transfers between devices  2.87 us (2%)
  local copies, waits for them, and re-layouts  1.81 us (1%)
  other arithmetic  1.4 us (1%)
    all_to_all x2, blocking collectives, swap(): return lax.all_to_all(value, AXES, split_axis=0, concat_axis=0, tiled=True)  61.4 us
    pallas_call x1, Pallas kernels, convolve(): pl.pallas_call(functools.partial(conv_kernel, block, window), in_specs=[p...  27.9 us
    pallas_call x1, Pallas kernels, place(): pl.pallas_call(functools.partial(place_kernel, pair_rows), out_shape=jax....  11.6 us
    ppermute x4, starting transfers between devices, from_behind(): lax.ppermute(value, axis, [(source, source + steps) for source in range(l...  9.19 us
    pallas_call x1, Pallas kernels, finish(): pl.pallas_call(functools.partial(finish_kernel, population), grid=(tile_r...  4.7 us
    pallas_call x1, Pallas kernels, turn_local(): pl.pallas_call(functools.partial(turn_kernel, block), out_shape=[jax.Shap...  3.16 us
    ppermute x4, waiting for transfers between devices, from_behind(): lax.ppermute(value, axis, [(source, source + steps) for source in range(l...  2.87 us
  transfers between devices with their start and end apart: 4, of which 1 were waited for; matrix products, arithmetic and copies ran while one was open for 0% of the time, Pallas kernels for 4%

profile of v3, /device:TPU:1, one launch (start us, length us, event | category | flops | bytes accessed | tf_op | source)
XLA Modules:
  0.0 126.4 jit_solution(8848911123889831284)
XLA Ops:
  0.0 0.5 broadcast.4
  0.5 1.4 %reduce.3 = s32[4096]{0:T(1024)S(1)} reduce(s32[4096,1]{0,1:T(1,128)} %param.8, s32[]{:T(128)} %broadcast.4), dimensions={1}, to_apply=%param.8.reduce_sub_computation.3 | reduce | bytes 32772 | tf_op args[1]
  1.9 0.0 copy-start.1
  1.9 1.2 copy-done.1
  3.2 11.6 %place.1 = bf16[8192,128]{1,0:T(8,128)(2,1)S(1)} custom-call(s32[8,512]{1,0:T(8,128)S(1)} %reshape.16.owner, bf16[4096,128]{1,0:T(8,128)(2,1)S(1)} %copy-done.1), custom_call_target="tpu_custom_call" | custom-call | tf_op jit(solution)/shard_map/place/pallas_call | solution.py:71
  14.8 0.0 copy-start.3
  14.8 41.1 %all_to_all.10 = bf16[128,64,128]{2,1,0:T(8,128)(2,1)S(1)} all-to-all(bf16[128,64,128]{2,1,0:T(8,128)(2,1)S(1)} %bitcast.9), channel_id=1, replica_groups=mesh['tx'=8,'ty'=16] {'tx','ty'}, dimensions={0} | all-to-all | bytes 4194304 | tf_op jit(solution)/shard_map/all_to_all | solution.py:336
  55.9 0.0 copy-start
  55.9 0.0 copy-start.2
  55.9 0.0 copy-done.3
  55.9 0.7 pick_rims.1
  56.5 3.4 %collective-permute-start = (bf16[1024,128]{1,0:T(8,128)(2,1)S(1)}, bf16[1024,128]{1,0:T(8,128)(2,1)S(1)}, u32[]{:S(2)}, u32[]{:S(2)}) collective-permute-start(bf16[1024,128]{1,0:T(8,128)(2,1)S(1)} %get-tuple-element.15), channel_id=1, source_target_pairs={{0,16},{16,32},{32,48},{48,64},{64,80},{80,96},{96,112},{1,17},{17... | collective-permute-start | bytes 786440 | tf_op jit(solution)/shard_map/ppermute | solution.py:20
  59.9 1.9 %collective-permute-start.1 = (bf16[1024,128]{1,0:T(8,128)(2,1)S(1)}, bf16[1024,128]{1,0:T(8,128)(2,1)S(1)}, u32[]{:S(2)}, u32[]{:S(2)}) collective-permute-start(bf16[1024,128]{1,0:T(8,128)(2,1)S(1)} %get-tuple-element.16), channel_id=1, source_target_pairs={{16,0},{32,16},{48,32},{64,48},{80,64},{96,80},{112,96},{17,1},{33... | collective-permute-start | bytes 786440 | tf_op jit(solution)/shard_map/ppermute | solution.py:20
  61.8 2.6 %collective-permute-start.2 = (bf16[1024,128]{1,0:T(8,128)(2,1)S(1)}, bf16[1024,128]{1,0:T(8,128)(2,1)S(1)}, u32[]{:S(2)}, u32[]{:S(2)}) collective-permute-start(bf16[1024,128]{1,0:T(8,128)(2,1)S(1)} %get-tuple-element.17), channel_id=1, source_target_pairs={{0,1},{1,2},{2,3},{3,4},{4,5},{5,6},{6,7},{7,8},{8,9},{9,10},{10,1... | collective-permute-start | bytes 786440 | tf_op jit(solution)/shard_map/ppermute | solution.py:20
  64.5 1.3 %collective-permute-start.3 = (bf16[1024,128]{1,0:T(8,128)(2,1)S(1)}, bf16[1024,128]{1,0:T(8,128)(2,1)S(1)}, u32[]{:S(2)}, u32[]{:S(2)}) collective-permute-start(bf16[1024,128]{1,0:T(8,128)(2,1)S(1)} %get-tuple-element.18), channel_id=1, source_target_pairs={{1,0},{2,1},{3,2},{4,3},{5,4},{6,5},{7,6},{8,7},{9,8},{10,9},{11,1... | collective-permute-start | bytes 786440 | tf_op jit(solution)/shard_map/ppermute | solution.py:20
  65.8 0.0 copy-done
  65.8 1.6 %source_blocks.1.source = s32[27,128]{1,0:T(8,128)S(1)} custom-call(s32[27,1,8192]{2,1,0:T(1,128)S(1)} %bitcast.10), custom_call_target="tpu_custom_call" | custom-call | tf_op jit(solution)/shard_map/source_blocks/pallas_call | solution.py:125
  67.4 0.0 copy-done.2
  67.4 3.2 %turn_local.1 = (bf16[128,128,128]{2,1,0:T(8,128)(2,1)S(1)}, f32[1,8192]{1,0:T(1,128)S(1)}, bf16[128,3456]{1,0:T(8,128)(2,1)S(1)}) custom-call(bf16[8192,128]{1,0:T(8,128)(2,1)S(1)} %bitcast.8, bf16[27,128,128]{2,1,0:T(8,128)(2,1)S(1)} %copy-done.2), custom_call_target="tpu_custom_call" | custom-call | tf_op jit(solution)/shard_map/turn_local/pallas_call | solution.py:169
  70.6 0.0 collective-permute-done.rim0
  70.6 0.0 collective-permute-done.1.rim1
  70.6 0.0 collective-permute-done.2.rim2
  70.6 2.9 %collective-permute-done.3.rim3 = bf16[1024,128]{1,0:T(8,128)(2,1)S(1)} collective-permute-done((bf16[1024,128]{1,0:T(8,128)(2,1)S(1)}, bf16[1024,128]{1,0:T(8,128)(2,1)S(1)}, u32[]{:S(2)}, u32[]{:S(2)}) %collective-permute-start.3) | collective-permute-done | bytes 262176 | tf_op jit(solution)/shard_map/ppermute | solution.py:20
  73.5 0.0 copy-start.4
  73.5 0.0 copy-start.5
  73.5 27.9 %convolve.1 = (f32[128,8192]{1,0:T(8,128)S(1)}, f32[4,128]{1,0:T(4,128)S(1)}) custom-call(s32[27,128]{1,0:T(8,128)S(1)} %source_blocks.1.source, s32[27,1,8192]{2,1,0:T(1,128)S(1)} %bitcast.11, bf16[128,128,128]{2,1,0:T(8,128)(2,1)S(1)} %get-tuple-element.14.xt_local, bf16[1024,128]{1,0:T(8,128)(2,1)S(1)} %collective-permute-done.rim0, ...), custom_call_target="tpu_custom_call" | custom-call | tf_op jit(solution)/shard_map/convolve/pallas_call | solution.py:271
  101.4 0.1 broadcast_in_dim.2
  101.4 20.3 %all_to_all.11.stats = f32[128,4,128]{2,1,0:T(4,128)S(1)} all-to-all(f32[128,4,128]{2,1,0:T(4,128)S(1)} %broadcast_in_dim.2), channel_id=1, replica_groups=mesh['tx'=8,'ty'=16] {'tx','ty'}, dimensions={0} | all-to-all | bytes 524288 | tf_op jit(solution)/shard_map/all_to_all | solution.py:336
  121.7 0.0 copy-done.4
  121.7 0.0 copy-done.5
  121.7 4.7 %finish.1 = bf16[8192,128]{1,0:T(8,128)(2,1)} custom-call(f32[128,4,128]{2,1,0:T(4,128)S(1)} %all_to_all.11.stats, f32[1,128]{1,0:T(1,128)S(1)} %bitcast.13, f32[1,128]{1,0:T(1,128)S(1)} %bitcast.14, f32[128,8192]{1,0:T(8,128)S(1)} %get-tuple-element.22.resp, f32[1,8192]{1,0:T(1,128)S(1)} %get-tuple-element.20.occ), custom_call_target="tpu_custom_call" | custom-call | tf_op jit(solution)/shard_map/finish/pallas_call | solution.py:310
  (1 shorter events, 0.0 us)
Async XLA Ops:
  1.9 1.2 copy-start.1
  14.8 41.1 %copy-start.3 = (s32[1,4,16]{2,1,0:T(4,128)S(1)}, s32[1,4,16]{2,1,0:T(4,128)}, u32[]{:S(2)}) copy-start(s32[1,4,16]{2,1,0:T(4,128)} %param.9) | copy-start | bytes 772
  55.9 9.9 %copy-start = (s32[1,27,8192]{2,0,1:T(1,128)S(1)}, s32[1,27,8192]{2,0,1:T(1,128)}, u32[]{:S(2)}) copy-start(s32[1,27,8192]{2,0,1:T(1,128)} %param.10) | copy-start | bytes 2654212
  55.9 11.5 %copy-start.2 = (bf16[27,128,128]{2,1,0:T(8,128)(2,1)S(1)}, bf16[27,128,128]{2,1,0:T(8,128)(2,1)}, u32[]{:S(2)}) copy-start(bf16[27,128,128]{2,1,0:T(8,128)(2,1)} %weights.1) | copy-start | bytes 2654212
  56.5 14.0 %collective-permute-start = (bf16[1024,128]{1,0:T(8,128)(2,1)S(1)}, bf16[1024,128]{1,0:T(8,128)(2,1)S(1)}, u32[]{:S(2)}, u32[]{:S(2)}) collective-permute-start(bf16[1024,128]{1,0:T(8,128)(2,1)S(1)} %get-tuple-element.15), channel_id=1, source_target_pairs={{0,16},{16,32},{32,48},{48,64},{64,80},{80,96},{96,112},{1,17},{17... | collective-permute-start | bytes 786440 | tf_op jit(solution)/shard_map/ppermute | solution.py:20
  59.9 10.7 %collective-permute-start.1 = (bf16[1024,128]{1,0:T(8,128)(2,1)S(1)}, bf16[1024,128]{1,0:T(8,128)(2,1)S(1)}, u32[]{:S(2)}, u32[]{:S(2)}) collective-permute-start(bf16[1024,128]{1,0:T(8,128)(2,1)S(1)} %get-tuple-element.16), channel_id=1, source_target_pairs={{16,0},{32,16},{48,32},{64,48},{80,64},{96,80},{112,96},{17,1},{33... | collective-permute-start | bytes 786440 | tf_op jit(solution)/shard_map/ppermute | solution.py:20
  61.8 8.8 %collective-permute-start.2 = (bf16[1024,128]{1,0:T(8,128)(2,1)S(1)}, bf16[1024,128]{1,0:T(8,128)(2,1)S(1)}, u32[]{:S(2)}, u32[]{:S(2)}) collective-permute-start(bf16[1024,128]{1,0:T(8,128)(2,1)S(1)} %get-tuple-element.17), channel_id=1, source_target_pairs={{0,1},{1,2},{2,3},{3,4},{4,5},{5,6},{6,7},{7,8},{8,9},{9,10},{10,1... | collective-permute-start | bytes 786440 | tf_op jit(solution)/shard_map/ppermute | solution.py:20
  64.5 9.0 %collective-permute-start.3 = (bf16[1024,128]{1,0:T(8,128)(2,1)S(1)}, bf16[1024,128]{1,0:T(8,128)(2,1)S(1)}, u32[]{:S(2)}, u32[]{:S(2)}) collective-permute-start(bf16[1024,128]{1,0:T(8,128)(2,1)S(1)} %get-tuple-element.18), channel_id=1, source_target_pairs={{1,0},{2,1},{3,2},{4,3},{5,4},{6,5},{7,6},{8,7},{9,8},{10,9},{11,1... | collective-permute-start | bytes 786440 | tf_op jit(solution)/shard_map/ppermute | solution.py:20
  73.5 48.3 %copy-start.4 = (f32[128]{0:T(128)S(1)}, f32[128]{0:T(128)}, u32[]{:S(2)}) copy-start(f32[128]{0:T(128)} %param.12) | copy-start | bytes 1540
  73.5 48.3 %copy-start.5 = (f32[128]{0:T(128)S(1)}, f32[128]{0:T(128)}, u32[]{:S(2)}) copy-start(f32[128]{0:T(128)} %param.13) | copy-start | bytes 1540

commit v4 on v3

--- a/solution.py
+++ b/solution.py
@@ -20,67 +20,74 @@
     return lax.ppermute(value, axis, [(source, source + steps) for source in range(leading, last)])
 
 
-def place_kernel(pair_rows, owner, voxels, out, addr_v, addr_s, wide, slots, sem):
-    runs, run_len = owner.shape
+def place_kernel(pair_rows, owner, voxels, out, held, addr_v, addr_s, wide, slots, sems):
+    rows = voxels.shape[0]
     tiles = out.shape[0] // pair_rows
+    fetch = pltpu.make_async_copy(voxels, held, sems.at[0])
+    fetch.start()
+    run_len = min(512, rows)
     earlier = lax.broadcasted_iota(I32, (run_len, run_len), 0)
     later = lax.broadcasted_iota(I32, (run_len, run_len), 1)
     upto = (earlier <= later).astype(BF16)
     tile_ids = lax.broadcasted_iota(I32, (tiles, run_len), 0)
     before = jnp.zeros((tiles, 1), F32)
-    for run in range(runs):
-        target = owner[run : run + 1, :]
+    for first in range(0, rows, run_len):
+        target = owner[:, first : first + run_len]
         member = tile_ids == target
         inside = jnp.dot(member.astype(BF16), upto, preferred_element_type=F32) + before
         rank = jnp.sum(jnp.where(member, inside, 0.0), axis=0, keepdims=True)
-        addr_v[run : run + 1, :] = target * pair_rows + rank.astype(I32) - 1
+        address = target * pair_rows + rank.astype(I32) - 1
+        for j in range(0, run_len, LANES):
+            line = (first + j) // LANES
+            addr_v[line : line + 1, :] = address[:, j : j + LANES]
         before = inside[:, run_len - 1 : run_len]
-    copy = pltpu.make_async_copy(addr_v, addr_s, sem)
+    copy = pltpu.make_async_copy(addr_v, addr_s, sems.at[1])
     copy.start()
     chunk = 256
 
-    @pl.loop(0, voxels.shape[0] // chunk)
-    def _(i):
-        rows = pl.ds(pl.multiple_of(i * chunk, chunk), chunk)
-        wide[rows, :] = voxels[rows, :].astype(F32)
-
     @pl.loop(0, out.shape[0] // chunk)
     def _(i):
-        rows = pl.ds(pl.multiple_of(i * chunk, chunk), chunk)
-        slots[rows, :] = jnp.full((chunk, slots.shape[1]), EMPTY, F32)
+        here = pl.ds(pl.multiple_of(i * chunk, chunk), chunk)
+        slots[here, :] = jnp.full((chunk, slots.shape[1]), EMPTY, F32)
+
+    fetch.wait()
+
+    @pl.loop(0, rows // chunk)
+    def _(i):
+        here = pl.ds(pl.multiple_of(i * chunk, chunk), chunk)
+        wide[here, :] = held[here, :].astype(F32)
 
     copy.wait()
-    unroll = 16
-    for run in range(runs):
-
-        @pl.loop(0, run_len // unroll)
-        def _(i):
-            for u in range(unroll):
-                place = addr_s[run, i * unroll + u]
-                slots[pl.ds(place, 1), :] = wide[pl.ds(run * run_len + i * unroll + u, 1), :]
+
+    @pl.loop(0, rows // LANES)
+    def _(line):
+        for u in range(LANES):
+            slots[pl.ds(addr_s[line, u], 1), :] = wide[pl.ds(line * LANES + u, 1), :]
 
     @pl.loop(0, out.shape[0] // chunk)
     def _(i):
-        rows = pl.ds(pl.multiple_of(i * chunk, chunk), chunk)
-        out[rows, :] = slots[rows, :].astype(BF16)
-
-
-def place(voxels, owner, tile_rows, pair_rows):
+        here = pl.ds(pl.multiple_of(i * chunk, chunk), chunk)
+        out[here, :] = slots[here, :].astype(BF16)
+
+
+def place(voxels, owner_tile, tile_rows, pair_rows):
     rows, channels = voxels.shape
-    runs = 8
     return pl.pallas_call(
         functools.partial(place_kernel, pair_rows),
+        in_specs=[pl.BlockSpec(memory_space=pltpu.VMEM), pl.BlockSpec(memory_space=pl.ANY)],
+        out_specs=pl.BlockSpec(memory_space=pltpu.VMEM),
         out_shape=jax.ShapeDtypeStruct((tile_rows, channels), BF16),
         scratch_shapes=[
-            pltpu.VMEM((runs, rows // runs), I32),
-            pltpu.SMEM((runs, rows // runs), I32),
+            pltpu.VMEM((rows, channels), BF16),
+            pltpu.VMEM((rows // LANES, LANES), I32),
+            pltpu.SMEM((rows // LANES, LANES), I32),
             pltpu.VMEM((rows, channels), F32),
             pltpu.VMEM((tile_rows, channels), F32),
-            pltpu.SemaphoreType.DMA,
+            pltpu.SemaphoreType.DMA((2,)),
         ],
         compiler_params=pltpu.CompilerParams(vmem_limit_bytes=32 * MIB),
         name="place",
-    )(owner.reshape(runs, rows // runs), voxels)
+    )(owner_tile.T, voxels)
 
 
 def pick_kernel(block, listed, arrival, *outs):
@@ -259,7 +266,14 @@
     squares = lax.fori_loop(0, tile_rows // LANES, spread, zero, unroll=4)
     squares = jnp.sum(squares, axis=1, keepdims=True)
     columns = jnp.where(lane == 0, total, jnp.where(lane == 1, squares, jnp.broadcast_to(number, (channels, LANES))))
-    stats[...] = columns.T[: stats.shape[0], :]
+    lines = columns.T
+    line = jnp.concatenate((lines[0:1], lines[1:2], lines[2:3]), axis=1)
+
+    def tell(i, carry):
+        stats[i] = line
+        return carry
+
+    lax.fori_loop(0, stats.shape[0], tell, 0, unroll=8)
 
 
 def convolve(source, kmap, xt_local, rims, weights_t, occ, block):
@@ -274,7 +288,7 @@
         out_specs=[whole, whole],
         out_shape=[
             jax.ShapeDtypeStruct((channels, tile_rows), F32),
-            jax.ShapeDtypeStruct((4, channels), F32),
+            jax.ShapeDtypeStruct((tile_rows // block, 1, 3 * channels), F32),
         ],
         scratch_shapes=[
             pltpu.VMEM((ext_blocks, channels, LANES), BF16),
@@ -285,42 +299,47 @@
     )(source, kmap, xt_local, *rims, weights_t, occ)
 
 
-def finish_kernel(population, stats, gain, bias, resp, occ, out, affine):
-    @pl.when(pl.program_id(0) == 0)
-    def _():
-        total, squares, number = stats[:, 0, :], stats[:, 1, :], stats[:, 2, :]
-        average = jnp.sum(total, axis=0, keepdims=True) / population
-        apart = total / jnp.maximum(number, 1.0) - average
-        spread = jnp.sum(squares + number * apart * apart, axis=0, keepdims=True)
-        scale = gain[...] / jnp.sqrt(spread / population + 1e-05)
-        row = lax.broadcasted_iota(I32, affine.shape, 0)
-        rows = jnp.where(row == 0, average, jnp.where(row == 1, scale, bias[...]))
-        affine[...] = rows.T
-
+def finish_kernel(population, stats, gain, bias, resp, occ, out, stage, sems):
+    channels, tile_rows = resp.shape
+    total = stats[:, 0, :channels]
+    squares = stats[:, 0, channels : 2 * channels]
+    number = stats[:, 0, 2 * channels :]
+    average = jnp.sum(total, axis=0, keepdims=True) / population
+    apart = total / jnp.maximum(number, 1.0) - average
+    spread = jnp.sum(squares + number * apart * apart, axis=0, keepdims=True)
+    scale = gain[...] / jnp.sqrt(spread / population + 1e-05)
+    row = lax.broadcasted_iota(I32, (LANES, channels), 0)
+    affine = jnp.where(row == 0, average, jnp.where(row == 1, scale, bias[...])).T
     average, scale, shift = affine[:, 0:1], affine[:, 1:2], affine[:, 2:3]
-    for p in range(resp.shape[1] // LANES):
-        at = slice(p * LANES, (p + 1) * LANES)
-        value = jnp.maximum((resp[:, at] - average) * scale + shift, 0.0) * occ[:, at]
-        out[at, :] = value.T.astype(BF16)
+    count = sems.shape[0]
+    part = tile_rows // count
+    copies = []
+    for c in range(count):
+
+        def turn(p, carry, c=c):
+            at = pl.ds(pl.multiple_of(c * part + p * LANES, LANES), LANES)
+            value = jnp.maximum((resp[:, at] - average) * scale + shift, 0.0) * occ[:, at]
+            stage[at, :] = value.T.astype(BF16)
+            return carry
+
+        lax.fori_loop(0, part // LANES, turn, 0, unroll=8)
+        here = slice(c * part, (c + 1) * part)
+        copies.append(pltpu.make_async_copy(stage.at[here, :], out.at[here, :], sems.at[c]))
+        copies[-1].start()
+    for copy in copies:
+        copy.wait()
 
 
 def finish(stats, gain, bias, resp, occ, population):
     channels, tile_rows = resp.shape
-    window = min(1024, tile_rows)
+    whole = pl.BlockSpec(memory_space=pltpu.VMEM)
     return pl.pallas_call(
         functools.partial(finish_kernel, population),
-        grid=(tile_rows // window,),
-        in_specs=[
-            pl.BlockSpec(memory_space=pltpu.VMEM),
-            pl.BlockSpec(memory_space=pltpu.VMEM),
-            pl.BlockSpec(memory_space=pltpu.VMEM),
-            pl.BlockSpec((channels, window), lambda q: (0, q)),
-            pl.BlockSpec((1, window), lambda q: (0, q)),
-        ],
-        out_specs=pl.BlockSpec((window, channels), lambda q: (q, 0)),
+        in_specs=[whole] * 5,
+        out_specs=pl.BlockSpec(memory_space=pl.ANY),
         out_shape=jax.ShapeDtypeStruct((tile_rows, channels), BF16),
-        scratch_shapes=[pltpu.VMEM((channels, LANES), F32)],
-        compiler_params=pltpu.CompilerParams(vmem_limit_bytes=32 * MIB),
+        scratch_shapes=[pltpu.VMEM((tile_rows, channels), BF16), pltpu.SemaphoreType.DMA((8,))],
+        compiler_params=pltpu.CompilerParams(vmem_limit_bytes=16 * MIB),
         name="finish",
     )(stats, gain.reshape(1, channels), bias.reshape(1, channels), resp, occ)
 
@@ -348,7 +367,7 @@
     )
     xt, occ, weights_t = turn_local(arrival, weights, block)
     resp, stats = convolve(source, kmap, xt, rims, weights_t, occ, block)
-    gathered = swap(jnp.broadcast_to(stats[None], (devices, *stats.shape)))
+    gathered = swap(stats)
     return finish(gathered, norm_gain, shift_bias, resp, occ, float(voxels.shape[0] * devices))
 
 

time: 127 us -> 116 us (0.913)
  Pallas kernels: 49.7 us -> 41 us
  other arithmetic: 1.4 us -> 0 us
    pallas_call x2, Pallas kernels: 16.3 us -> 7.6 us  [the longest x1 5.42 us: place(): pl.pallas_call(functools.partial(place_kernel, pair_rows), in_specs=[pl.B...]
    unnamed x1 -> x0, other arithmetic: 1.4 us -> none
where the time goes in v4:
time: 116 us
  blocking collectives  60.8 us (52%)
  Pallas kernels  41 us (35%)
  starting transfers between devices  9.19 us (8%)
  waiting for transfers between devices  2.99 us (3%)
  local copies, waits for them, and re-layouts  1.96 us (2%)
    all_to_all x2, blocking collectives, swap(): return lax.all_to_all(value, AXES, split_axis=0, concat_axis=0, tiled=True)  60.8 us
    pallas_call x1, Pallas kernels, convolve(): pl.pallas_call(functools.partial(conv_kernel, block, window), in_specs=[p...  28.1 us
    ppermute x4, starting transfers between devices, from_behind(): lax.ppermute(value, axis, [(source, source + steps) for source in range(l...  9.19 us
    pallas_call x1, Pallas kernels, place(): pl.pallas_call(functools.partial(place_kernel, pair_rows), in_specs=[pl.B...  5.42 us
    pallas_call x1, Pallas kernels, turn_local(): pl.pallas_call(functools.partial(turn_kernel, block), out_shape=[jax.Shap...  3.16 us
    ppermute x4, waiting for transfers between devices, from_behind(): lax.ppermute(value, axis, [(source, source + steps) for source in range(l...  2.99 us
  transfers between devices with their start and end apart: 4, of which 1 were waited for; matrix products, arithmetic and copies ran while one was open for 0% of the time, Pallas kernels for 4%

profile of v4, /device:TPU:1, one launch (start us, length us, event | category | flops | bytes accessed | tf_op | source)
XLA Modules:
  0.0 116.0 jit_solution(4196343027138593346)
XLA Ops:
  0.0 0.0 copy-start.1
  0.0 1.2 %copy-done.1 = bf16[4096,128]{1,0:T(8,128)(2,1)S(1)} copy-done((bf16[4096,128]{1,0:T(8,128)(2,1)S(1)}, bf16[4096,128]{1,0:T(8,128)(2,1)}, u32[]{:S(2)}) %copy-start.1) | copy-done | bytes 1048600
  1.2 0.0 copy-start.3
  1.2 0.7 copy-done.3
  1.9 5.4 %place.1 = bf16[8192,128]{1,0:T(8,128)(2,1)S(1)} custom-call(s32[1,4096]{1,0:T(1,128)S(1)} %bitcast.12, bf16[4096,128]{1,0:T(8,128)(2,1)S(1)} %copy-done.1), custom_call_target="tpu_custom_call" | custom-call | tf_op jit(solution)/shard_map/place/pallas_call | solution.py:75
  7.4 0.0 copy-start.4
  7.4 41.1 %all_to_all.10 = bf16[128,64,128]{2,1,0:T(8,128)(2,1)S(1)} all-to-all(bf16[128,64,128]{2,1,0:T(8,128)(2,1)S(1)} %bitcast.9), channel_id=1, replica_groups=mesh['tx'=8,'ty'=16] {'tx','ty'}, dimensions={0} | all-to-all | bytes 4194304 | tf_op jit(solution)/shard_map/all_to_all | solution.py:355
  48.4 0.0 copy-start
  48.5 0.0 copy-start.2
  48.5 0.0 copy-done.4
  48.5 0.7 pick_rims.1
  49.1 3.4 %collective-permute-start = (bf16[1024,128]{1,0:T(8,128)(2,1)S(1)}, bf16[1024,128]{1,0:T(8,128)(2,1)S(1)}, u32[]{:S(2)}, u32[]{:S(2)}) collective-permute-start(bf16[1024,128]{1,0:T(8,128)(2,1)S(1)} %get-tuple-element.15), channel_id=1, source_target_pairs={{0,16},{16,32},{32,48},{48,64},{64,80},{80,96},{96,112},{1,17},{17... | collective-permute-start | bytes 786440 | tf_op jit(solution)/shard_map/ppermute | solution.py:20
  52.5 1.9 %collective-permute-start.1 = (bf16[1024,128]{1,0:T(8,128)(2,1)S(1)}, bf16[1024,128]{1,0:T(8,128)(2,1)S(1)}, u32[]{:S(2)}, u32[]{:S(2)}) collective-permute-start(bf16[1024,128]{1,0:T(8,128)(2,1)S(1)} %get-tuple-element.16), channel_id=1, source_target_pairs={{16,0},{32,16},{48,32},{64,48},{80,64},{96,80},{112,96},{17,1},{33... | collective-permute-start | bytes 786440 | tf_op jit(solution)/shard_map/ppermute | solution.py:20
  54.4 2.6 %collective-permute-start.2 = (bf16[1024,128]{1,0:T(8,128)(2,1)S(1)}, bf16[1024,128]{1,0:T(8,128)(2,1)S(1)}, u32[]{:S(2)}, u32[]{:S(2)}) collective-permute-start(bf16[1024,128]{1,0:T(8,128)(2,1)S(1)} %get-tuple-element.17), channel_id=1, source_target_pairs={{0,1},{1,2},{2,3},{3,4},{4,5},{5,6},{6,7},{7,8},{8,9},{9,10},{10,1... | collective-permute-start | bytes 786440 | tf_op jit(solution)/shard_map/ppermute | solution.py:20
  57.0 1.3 %collective-permute-start.3 = (bf16[1024,128]{1,0:T(8,128)(2,1)S(1)}, bf16[1024,128]{1,0:T(8,128)(2,1)S(1)}, u32[]{:S(2)}, u32[]{:S(2)}) collective-permute-start(bf16[1024,128]{1,0:T(8,128)(2,1)S(1)} %get-tuple-element.18), channel_id=1, source_target_pairs={{1,0},{2,1},{3,2},{4,3},{5,4},{6,5},{7,6},{8,7},{9,8},{10,9},{11,1... | collective-permute-start | bytes 786440 | tf_op jit(solution)/shard_map/ppermute | solution.py:20
  58.3 0.0 copy-done
  58.4 1.5 %source_blocks.1.source = s32[27,128]{1,0:T(8,128)S(1)} custom-call(s32[27,1,8192]{2,1,0:T(1,128)S(1)} %bitcast.10), custom_call_target="tpu_custom_call" | custom-call | tf_op jit(solution)/shard_map/source_blocks/pallas_call | solution.py:132
  59.8 0.0 copy-done.2
  59.9 3.2 %turn_local.1 = (bf16[128,128,128]{2,1,0:T(8,128)(2,1)S(1)}, f32[1,8192]{1,0:T(1,128)S(1)}, bf16[128,3456]{1,0:T(8,128)(2,1)S(1)}) custom-call(bf16[8192,128]{1,0:T(8,128)(2,1)S(1)} %bitcast.8, bf16[27,128,128]{2,1,0:T(8,128)(2,1)S(1)} %copy-done.2), custom_call_target="tpu_custom_call" | custom-call | tf_op jit(solution)/shard_map/turn_local/pallas_call | solution.py:176
  63.0 0.0 collective-permute-done.rim0
  63.0 0.0 collective-permute-done.1.rim1
  63.0 0.0 collective-permute-done.2.rim2
  63.1 3.0 %collective-permute-done.3.rim3 = bf16[1024,128]{1,0:T(8,128)(2,1)S(1)} collective-permute-done((bf16[1024,128]{1,0:T(8,128)(2,1)S(1)}, bf16[1024,128]{1,0:T(8,128)(2,1)S(1)}, u32[]{:S(2)}, u32[]{:S(2)}) %collective-permute-start.3) | collective-permute-done | bytes 262176 | tf_op jit(solution)/shard_map/ppermute | solution.py:20
  66.0 0.0 copy-start.5
  66.0 0.0 copy-start.6
  66.0 28.1 %convolve.1 = (f32[128,8192]{1,0:T(8,128)S(1)}, f32[128,1,384]{2,1,0:T(1,128)S(1)}) custom-call(s32[27,128]{1,0:T(8,128)S(1)} %source_blocks.1.source, s32[27,1,8192]{2,1,0:T(1,128)S(1)} %bitcast.11, bf16[128,128,128]{2,1,0:T(8,128)(2,1)S(1)} %get-tuple-element.14.xt_local, bf16[1024,128]{1,0:T(8,128)(2,1)S(1)} %collective-permute-done.rim0, ...), custom_call_target="tpu_custom_call" | custom-call | tf_op jit(solution)/shard_map/convolve/pallas_call | solution.py:285
  94.1 19.7 %all_to_all.11.stats = f32[128,1,384]{2,1,0:T(1,128)S(1)} all-to-all(f32[128,1,384]{2,1,0:T(1,128)S(1)} %get-tuple-element.21), channel_id=1, replica_groups=mesh['tx'=8,'ty'=16] {'tx','ty'}, dimensions={0} | all-to-all | bytes 393216 | tf_op jit(solution)/shard_map/all_to_all | solution.py:355
  113.8 0.0 copy-done.5
  113.8 0.0 copy-done.6
  113.8 2.2 %finish.1 = bf16[8192,128]{1,0:T(8,128)(2,1)} custom-call(f32[128,1,384]{2,1,0:T(1,128)S(1)} %all_to_all.11.stats, f32[1,128]{1,0:T(1,128)S(1)} %bitcast.14, f32[1,128]{1,0:T(1,128)S(1)} %bitcast.15, f32[128,8192]{1,0:T(8,128)S(1)} %get-tuple-element.22.resp, f32[1,8192]{1,0:T(1,128)S(1)} %get-tuple-element.20.occ), custom_call_target="tpu_custom_call" | custom-call | tf_op jit(solution)/shard_map/finish/pallas_call | solution.py:336
Async XLA Ops:
  0.0 1.2 %copy-start.1 = (bf16[4096,128]{1,0:T(8,128)(2,1)S(1)}, bf16[4096,128]{1,0:T(8,128)(2,1)}, u32[]{:S(2)}) copy-start(bf16[4096,128]{1,0:T(8,128)(2,1)} %voxels.1) | copy-start | bytes 3145732
  1.2 0.7 copy-start.3
  7.4 41.1 %copy-start.4 = (s32[1,4,16]{2,1,0:T(4,128)S(1)}, s32[1,4,16]{2,1,0:T(4,128)}, u32[]{:S(2)}) copy-start(s32[1,4,16]{2,1,0:T(4,128)} %param.9) | copy-start | bytes 772
  48.4 9.9 %copy-start = (s32[1,27,8192]{2,0,1:T(1,128)S(1)}, s32[1,27,8192]{2,0,1:T(1,128)}, u32[]{:S(2)}) copy-start(s32[1,27,8192]{2,0,1:T(1,128)} %param.10) | copy-start | bytes 2654212
  48.5 11.4 %copy-start.2 = (bf16[27,128,128]{2,1,0:T(8,128)(2,1)S(1)}, bf16[27,128,128]{2,1,0:T(8,128)(2,1)}, u32[]{:S(2)}) copy-start(bf16[27,128,128]{2,1,0:T(8,128)(2,1)} %weights.1) | copy-start | bytes 2654212
  49.1 13.9 %collective-permute-start = (bf16[1024,128]{1,0:T(8,128)(2,1)S(1)}, bf16[1024,128]{1,0:T(8,128)(2,1)S(1)}, u32[]{:S(2)}, u32[]{:S(2)}) collective-permute-start(bf16[1024,128]{1,0:T(8,128)(2,1)S(1)} %get-tuple-element.15), channel_id=1, source_target_pairs={{0,16},{16,32},{32,48},{48,64},{64,80},{80,96},{96,112},{1,17},{17... | collective-permute-start | bytes 786440 | tf_op jit(solution)/shard_map/ppermute | solution.py:20
  52.5 10.5 %collective-permute-start.1 = (bf16[1024,128]{1,0:T(8,128)(2,1)S(1)}, bf16[1024,128]{1,0:T(8,128)(2,1)S(1)}, u32[]{:S(2)}, u32[]{:S(2)}) collective-permute-start(bf16[1024,128]{1,0:T(8,128)(2,1)S(1)} %get-tuple-element.16), channel_id=1, source_target_pairs={{16,0},{32,16},{48,32},{64,48},{80,64},{96,80},{112,96},{17,1},{33... | collective-permute-start | bytes 786440 | tf_op jit(solution)/shard_map/ppermute | solution.py:20
  54.4 8.6 %collective-permute-start.2 = (bf16[1024,128]{1,0:T(8,128)(2,1)S(1)}, bf16[1024,128]{1,0:T(8,128)(2,1)S(1)}, u32[]{:S(2)}, u32[]{:S(2)}) collective-permute-start(bf16[1024,128]{1,0:T(8,128)(2,1)S(1)} %get-tuple-element.17), channel_id=1, source_target_pairs={{0,1},{1,2},{2,3},{3,4},{4,5},{5,6},{6,7},{7,8},{8,9},{9,10},{10,1... | collective-permute-start | bytes 786440 | tf_op jit(solution)/shard_map/ppermute | solution.py:20
  57.0 9.0 %collective-permute-start.3 = (bf16[1024,128]{1,0:T(8,128)(2,1)S(1)}, bf16[1024,128]{1,0:T(8,128)(2,1)S(1)}, u32[]{:S(2)}, u32[]{:S(2)}) collective-permute-start(bf16[1024,128]{1,0:T(8,128)(2,1)S(1)} %get-tuple-element.18), channel_id=1, source_target_pairs={{1,0},{2,1},{3,2},{4,3},{5,4},{6,5},{7,6},{8,7},{9,8},{10,9},{11,1... | collective-permute-start | bytes 786440 | tf_op jit(solution)/shard_map/ppermute | solution.py:20
  66.0 47.8 %copy-start.5 = (f32[128]{0:T(128)S(1)}, f32[128]{0:T(128)}, u32[]{:S(2)}) copy-start(f32[128]{0:T(128)} %param.12) | copy-start | bytes 1540
  66.0 47.8 %copy-start.6 = (f32[128]{0:T(128)S(1)}, f32[128]{0:T(128)}, u32[]{:S(2)}) copy-start(f32[128]{0:T(128)} %param.13) | copy-start | bytes 1540

commit v5 on v4

--- a/solution.py
+++ b/solution.py
@@ -14,10 +14,9 @@
 MIB = 1 << 20
 
 
-def from_behind(value, axis, steps):
-    count = lax.axis_size(axis)
-    leading, last = (max(0, -steps), min(count, count - steps))
-    return lax.ppermute(value, axis, [(source, source + steps) for source in range(leading, last)])
+def exchanged(value, axis, first):
+    pairs = range(first, lax.axis_size(axis) - 1, 2)
+    return lax.ppermute(value, axis, [way for i in pairs for way in ((i, i + 1), (i + 1, i))])
 
 
 def place_kernel(pair_rows, owner, voxels, out, held, addr_v, addr_s, wide, slots, sems):
@@ -90,20 +89,21 @@
     )(owner_tile.T, voxels)
 
 
-def pick_kernel(block, listed, arrival, *outs):
+def pick_kernel(block, listed, ways, arrival, *outs):
     count = outs[0].shape[0] // block
     for d, out in enumerate(outs):
         for i in range(count):
-            at = pl.multiple_of(listed[d, i] * block, block)
+            at = pl.multiple_of(listed[ways[d], i] * block, block)
             out[i * block : (i + 1) * block, :] = arrival[pl.ds(at, block), :]
 
 
-def pick(arrival, listed, block):
+def pick(arrival, listed, ways, block):
     directions, count = listed.shape
     shape = jax.ShapeDtypeStruct((count * block, arrival.shape[1]), arrival.dtype)
     return pl.pallas_call(
         functools.partial(pick_kernel, block),
         in_specs=[
+            pl.BlockSpec(memory_space=pltpu.SMEM),
             pl.BlockSpec(memory_space=pltpu.SMEM),
             pl.BlockSpec(memory_space=pltpu.VMEM),
         ],
@@ -111,7 +111,7 @@
         out_shape=[shape] * directions,
         compiler_params=pltpu.CompilerParams(vmem_limit_bytes=16 * MIB),
         name="pick_rims",
-    )(listed, arrival)
+    )(listed, ways, arrival)
 
 
 def source_kernel(block, kmap, out):
@@ -185,7 +185,7 @@
     )(arrival, weights)
 
 
-def conv_kernel(block, window, source, kmap, xt_local, rim0, rim1, rim2, rim3, weights_t, occ, resp, stats, xt, g):
+def conv_kernel(block, window, source, ways, kmap, xt_local, rim0, rim1, rim2, rim3, weights_t, occ, resp, stats, xt, g):
     offsets, tile_rows = kmap.shape[0], kmap.shape[2]
     channels = xt_local.shape[1]
     same = same_of(channels)
@@ -199,10 +199,10 @@
         xt[i] = xt_local[i]
         return carry
 
-    first = xt_local.shape[0]
-    lax.fori_loop(0, first, keep, 0, unroll=8)
-    for part in (rim0, rim1, rim2, rim3):
-        pairs = part.shape[0] // LANES
+    local_blocks = xt_local.shape[0]
+    lax.fori_loop(0, local_blocks, keep, 0, unroll=8)
+    for d, part in enumerate((rim0, rim1, rim2, rim3)):
+        first = local_blocks + (ways[d] ^ 1) * (part.shape[0] // block)
 
         def turn(p, carry, part=part, first=first):
             both = jnp.maximum(turn_pair(same, part, p, block), 0.0).astype(BF16)
@@ -210,8 +210,7 @@
             xt[first + 2 * p + 1] = both[:, LANES:]
             return carry
 
-        lax.fori_loop(0, pairs, turn, 0, unroll=8)
-        first += 2 * pairs
+        lax.fori_loop(0, part.shape[0] // LANES, turn, 0, unroll=8)
 
     blocks = window // block
 
@@ -276,7 +275,7 @@
     lax.fori_loop(0, stats.shape[0], tell, 0, unroll=8)
 
 
-def convolve(source, kmap, xt_local, rims, weights_t, occ, block):
+def convolve(source, ways, kmap, xt_local, rims, weights_t, occ, block):
     offsets, _, tile_rows = kmap.shape
     local_blocks, channels, _ = xt_local.shape
     window = min(1024, tile_rows)
@@ -284,7 +283,7 @@
     whole = pl.BlockSpec(memory_space=pltpu.VMEM)
     return pl.pallas_call(
         functools.partial(conv_kernel, block, window),
-        in_specs=[pl.BlockSpec(memory_space=pltpu.SMEM), *[whole] * 8],
+        in_specs=[pl.BlockSpec(memory_space=pltpu.SMEM)] * 2 + [whole] * 8,
         out_specs=[whole, whole],
         out_shape=[
             jax.ShapeDtypeStruct((channels, tile_rows), F32),
@@ -296,7 +295,7 @@
         ],
         compiler_params=pltpu.CompilerParams(vmem_limit_bytes=40 * MIB),
         name="convolve",
-    )(source, kmap, xt_local, *rims, weights_t, occ)
+    )(source, ways, kmap, xt_local, *rims, weights_t, occ)
 
 
 def finish_kernel(population, stats, gain, bias, resp, occ, out, stage, sems):
@@ -358,15 +357,17 @@
     arrival = swap(outgoing.reshape(devices, pair_rows, channels)).reshape(tile_rows, channels)
     kmap = kernel_map.transpose(1, 0, 2)
     source = source_blocks(kmap, block)
-    picked = pick(arrival, rim_blocks[0], block)
+    odd_row, odd_col = lax.axis_index("tx") % 2, lax.axis_index("ty") % 2
+    ways = jnp.stack((odd_row, 1 - odd_row, 2 + odd_col, 3 - odd_col)).astype(I32)
+    picked = pick(arrival, rim_blocks[0], ways, block)
     rims = (
-        from_behind(picked[0], "tx", 1),
-        from_behind(picked[1], "tx", -1),
-        from_behind(picked[2], "ty", 1),
-        from_behind(picked[3], "ty", -1),
+        exchanged(picked[0], "tx", 0),
+        exchanged(picked[1], "tx", 1),
+        exchanged(picked[2], "ty", 0),
+        exchanged(picked[3], "ty", 1),
     )
     xt, occ, weights_t = turn_local(arrival, weights, block)
-    resp, stats = convolve(source, kmap, xt, rims, weights_t, occ, block)
+    resp, stats = convolve(source, ways, kmap, xt, rims, weights_t, occ, block)
     gathered = swap(stats)
     return finish(gathered, norm_gain, shift_bias, resp, occ, float(voxels.shape[0] * devices))
 

time: 116 us -> 112 us (0.966)
  blocking collectives: 60.8 us -> 20.2 us
  waiting for transfers between devices: 2.99 us -> 30.4 us
  starting transfers between devices: 9.19 us -> 16.4 us
  local copies, waits for them, and re-layouts: 1.96 us -> 3.28 us
    all_to_all x2 -> x1, blocking collectives: 60.8 us -> 20.2 us  [swap(): return lax.all_to_all(value, AXES, split_axis=0, concat_axis=0, tiled=True)]
    all_to_all x0 -> x1, waiting for transfers between devices: none -> 29.7 us  [swap(): return lax.all_to_all(value, AXES, split_axis=0, concat_axis=0, tiled=True)]
    all_to_all x0 -> x1, starting transfers between devices: none -> 11.5 us  [swap(): return lax.all_to_all(value, AXES, split_axis=0, concat_axis=0, tiled=True)]
    ppermute x4, starting transfers between devices: 9.19 us -> 4.9 us  [exchanged(): lax.ppermute(value, axis, [way for i in pairs for way in ((i, i + 1), (i...]
    ppermute x4, waiting for transfers between devices: 2.99 us -> 0.76 us  [exchanged(): lax.ppermute(value, axis, [way for i in pairs for way in ((i, i + 1), (i...]
    unnamed x14 -> x16, local copies, waits for them, and re-layouts: 1.96 us -> 3.28 us
  transfers between devices with their start and end apart: 4 -> 5, of which waited for: 1 -> 2; matrix products, arithmetic and copies ran while one was open for 0% -> 0% of each run, Pallas kernels for 4% -> 4%
where the time goes in v5:
time: 112 us; the launch traced here: 111 us
  Pallas kernels  41 us (37%)
  waiting for transfers between devices  30.4 us (27%)
  blocking collectives  20.2 us (18%)
  starting transfers between devices  16.4 us (15%)
  local copies, waits for them, and re-layouts  3.28 us (3%)
    all_to_all x1, waiting for transfers between devices, swap(): return lax.all_to_all(value, AXES, split_axis=0, concat_axis=0, tiled=True)  29.7 us
    pallas_call x1, Pallas kernels, convolve(): pl.pallas_call(functools.partial(conv_kernel, block, window), in_specs=[p...  28.1 us
    all_to_all x1, blocking collectives, swap(): return lax.all_to_all(value, AXES, split_axis=0, concat_axis=0, tiled=True)  20.2 us
    all_to_all x1, starting transfers between devices, swap(): return lax.all_to_all(value, AXES, split_axis=0, concat_axis=0, tiled=True)  11.5 us
    pallas_call x1, Pallas kernels, place(): pl.pallas_call(functools.partial(place_kernel, pair_rows), in_specs=[pl.B...  5.42 us
    ppermute x4, starting transfers between devices, exchanged(): lax.ppermute(value, axis, [way for i in pairs for way in ((i, i + 1), (i...  4.9 us
    unnamed x16, local copies, waits for them, and re-layouts  3.28 us
    pallas_call x1, Pallas kernels, turn_local(): pl.pallas_call(functools.partial(turn_kernel, block), out_shape=[jax.Shap...  3.16 us
  transfers between devices with their start and end apart: 5, of which 2 were waited for; matrix products, arithmetic and copies ran while one was open for 0% of the time, Pallas kernels for 4%

profile of v5, /device:TPU:1, one launch (start us, length us, event | category | flops | bytes accessed | tf_op | source)
XLA Modules:
  0.0 111.5 jit_solution(3745576993105874299)
XLA Ops:
  0.0 0.0 copy-start.2
  0.0 1.2 %copy-done.2 = bf16[4096,128]{1,0:T(8,128)(2,1)S(1)} copy-done((bf16[4096,128]{1,0:T(8,128)(2,1)S(1)}, bf16[4096,128]{1,0:T(8,128)(2,1)}, u32[]{:S(2)}) %copy-start.2) | copy-done | bytes 1048600
  1.2 0.0 copy-start.4
  1.2 0.7 copy-done.4
  1.9 5.4 %place.1 = bf16[8192,128]{1,0:T(8,128)(2,1)S(1)} custom-call(s32[1,4096]{1,0:T(1,128)S(1)} %bitcast.16, bf16[4096,128]{1,0:T(8,128)(2,1)S(1)} %copy-done.2), custom_call_target="tpu_custom_call" | custom-call | tf_op jit(solution)/shard_map/place/pallas_call | solution.py:74
  7.4 0.0 copy-start
  7.4 1.3 %copy-done = bf16[8192,128]{1,0:T(8,128)(2,1)} copy-done((bf16[8192,128]{1,0:T(8,128)(2,1)}, bf16[8192,128]{1,0:T(8,128)(2,1)S(1)}, u32[]{:S(2)}) %copy-start) | copy-done | bytes 2097176
  8.7 0.0 copy-start.5
  8.7 11.5 %all-to-all-start = ((bf16[128,64,128]{2,1,0:T(8,128)(2,1)}), bf16[128,64,128]{2,1,0:T(8,128)(2,1)S(1)}, u32[]{:S(2)}, u32[]{:S(2)}) async-start(bf16[128,64,128]{2,1,0:T(8,128)(2,1)} %bitcast.13), calls=%async_computation | async-start | bytes 4194304 | tf_op jit(solution)/shard_map/all_to_all | solution.py:354
  20.2 0.0 copy-start.1
  20.2 0.1 pad_add_fusion.ways
  20.3 29.7 %all-to-all-done = bf16[128,64,128]{2,1,0:T(8,128)(2,1)S(1)} async-done(((bf16[128,64,128]{2,1,0:T(8,128)(2,1)}), bf16[128,64,128]{2,1,0:T(8,128)(2,1)S(1)}, u32[]{:S(2)}, u32[]{:S(2)}) %all-to-all-start) | async-done | bytes 2097184 | tf_op jit(solution)/shard_map/all_to_all | solution.py:354
  50.0 0.0 copy-start.3
  50.0 0.0 copy-done.5
  50.0 0.7 pick_rims.1
  50.7 1.1 collective-permute-start
  51.7 2.4 %collective-permute-start.1 = (bf16[1024,128]{1,0:T(8,128)(2,1)S(1)}, bf16[1024,128]{1,0:T(8,128)(2,1)S(1)}, u32[]{:S(2)}, u32[]{:S(2)}) collective-permute-start(bf16[1024,128]{1,0:T(8,128)(2,1)S(1)} %get-tuple-element.16), channel_id=1, source_target_pairs={{16,32},{32,16},{48,64},{64,48},{80,96},{96,80},{17,33},{33,17},{4... | collective-permute-start | bytes 786440 | tf_op jit(solution)/shard_map/ppermute | solution.py:19
  54.1 0.8 collective-permute-start.2
  54.9 0.7 collective-permute-start.3
  55.6 0.0 copy-done.1
  55.6 1.5 %source_blocks.1.source = s32[27,128]{1,0:T(8,128)S(1)} custom-call(s32[27,1,8192]{2,1,0:T(1,128)S(1)} %bitcast.14), custom_call_target="tpu_custom_call" | custom-call | tf_op jit(solution)/shard_map/source_blocks/pallas_call | solution.py:132
  57.1 0.0 copy-done.3
  57.1 3.2 %turn_local.1 = (bf16[128,128,128]{2,1,0:T(8,128)(2,1)S(1)}, f32[1,8192]{1,0:T(1,128)S(1)}, bf16[128,3456]{1,0:T(8,128)(2,1)S(1)}) custom-call(bf16[8192,128]{1,0:T(8,128)(2,1)S(1)} %bitcast.12, bf16[27,128,128]{2,1,0:T(8,128)(2,1)S(1)} %copy-done.3), custom_call_target="tpu_custom_call" | custom-call | tf_op jit(solution)/shard_map/turn_local/pallas_call | solution.py:176
  60.2 0.0 collective-permute-done.rim0
  60.3 0.0 collective-permute-done.1.rim1
  60.3 0.8 collective-permute-done.2.rim2
  61.0 0.0 collective-permute-done.3.rim3
  61.0 0.0 copy-start.6
  61.0 0.0 copy-start.7
  61.0 28.1 %convolve.1 = (f32[128,8192]{1,0:T(8,128)S(1)}, f32[128,1,384]{2,1,0:T(1,128)S(1)}) custom-call(s32[27,128]{1,0:T(8,128)S(1)} %source_blocks.1.source, s32[4]{0:T(128)S(1)} %pad_add_fusion.ways, s32[27,1,8192]{2,1,0:T(1,128)S(1)} %bitcast.15, bf16[128,128,128]{2,1,0:T(8,128)(2,1)S(1)} %get-tuple-element.14.xt_local, ...), custom_call_target="tpu_custom_call" | custom-call | tf_op jit(solution)/shard_map/convolve/pallas_call | solution.py:284
  89.1 20.2 %all_to_all.10.stats = f32[128,1,384]{2,1,0:T(1,128)S(1)} all-to-all(f32[128,1,384]{2,1,0:T(1,128)S(1)} %get-tuple-element.21), channel_id=1, replica_groups=mesh['tx'=8,'ty'=16] {'tx','ty'}, dimensions={0} | all-to-all | bytes 393216 | tf_op jit(solution)/shard_map/all_to_all | solution.py:354
  109.3 0.0 copy-done.6
  109.3 0.0 copy-done.7
  109.3 2.2 %finish.1 = bf16[8192,128]{1,0:T(8,128)(2,1)} custom-call(f32[128,1,384]{2,1,0:T(1,128)S(1)} %all_to_all.10.stats, f32[1,128]{1,0:T(1,128)S(1)} %bitcast.18, f32[1,128]{1,0:T(1,128)S(1)} %bitcast.19, f32[128,8192]{1,0:T(8,128)S(1)} %get-tuple-element.22.resp, f32[1,8192]{1,0:T(1,128)S(1)} %get-tuple-element.20.occ), custom_call_target="tpu_custom_call" | custom-call | tf_op jit(solution)/shard_map/finish/pallas_call | solution.py:335
Async XLA Ops:
  0.0 1.2 %copy-start.2 = (bf16[4096,128]{1,0:T(8,128)(2,1)S(1)}, bf16[4096,128]{1,0:T(8,128)(2,1)}, u32[]{:S(2)}) copy-start(bf16[4096,128]{1,0:T(8,128)(2,1)} %voxels.1) | copy-start | bytes 3145732
  1.2 0.7 copy-start.4
  7.4 1.3 %copy-start = (bf16[8192,128]{1,0:T(8,128)(2,1)}, bf16[8192,128]{1,0:T(8,128)(2,1)S(1)}, u32[]{:S(2)}) copy-start(bf16[8192,128]{1,0:T(8,128)(2,1)S(1)} %place.1) | copy-start | bytes 6291460
  8.7 41.3 %copy-start.5 = (s32[1,4,16]{2,1,0:T(4,128)S(1)}, s32[1,4,16]{2,1,0:T(4,128)}, u32[]{:S(2)}) copy-start(s32[1,4,16]{2,1,0:T(4,128)} %param.9) | copy-start | bytes 772
  8.7 41.3 %all-to-all-start = ((bf16[128,64,128]{2,1,0:T(8,128)(2,1)}), bf16[128,64,128]{2,1,0:T(8,128)(2,1)S(1)}, u32[]{:S(2)}, u32[]{:S(2)}) async-start(bf16[128,64,128]{2,1,0:T(8,128)(2,1)} %bitcast.13), calls=%async_computation | async-start | bytes 4194304 | tf_op jit(solution)/shard_map/all_to_all | solution.py:354
  20.2 35.4 %copy-start.1 = (s32[1,27,8192]{2,0,1:T(1,128)S(1)}, s32[1,27,8192]{2,0,1:T(1,128)}, u32[]{:S(2)}) copy-start(s32[1,27,8192]{2,0,1:T(1,128)} %param.10) | copy-start | bytes 2654212
  50.0 7.1 %copy-start.3 = (bf16[27,128,128]{2,1,0:T(8,128)(2,1)S(1)}, bf16[27,128,128]{2,1,0:T(8,128)(2,1)}, u32[]{:S(2)}) copy-start(bf16[27,128,128]{2,1,0:T(8,128)(2,1)} %weights.1) | copy-start | bytes 2654212
  50.7 9.6 %collective-permute-start = (bf16[1024,128]{1,0:T(8,128)(2,1)S(1)}, bf16[1024,128]{1,0:T(8,128)(2,1)S(1)}, u32[]{:S(2)}, u32[]{:S(2)}) collective-permute-start(bf16[1024,128]{1,0:T(8,128)(2,1)S(1)} %get-tuple-element.15), channel_id=1, source_target_pairs={{0,16},{16,0},{32,48},{48,32},{64,80},{80,64},{96,112},{112,96},{1... | collective-permute-start | bytes 786440 | tf_op jit(solution)/shard_map/ppermute | solution.py:19
  51.7 8.5 %collective-permute-start.1 = (bf16[1024,128]{1,0:T(8,128)(2,1)S(1)}, bf16[1024,128]{1,0:T(8,128)(2,1)S(1)}, u32[]{:S(2)}, u32[]{:S(2)}) collective-permute-start(bf16[1024,128]{1,0:T(8,128)(2,1)S(1)} %get-tuple-element.16), channel_id=1, source_target_pairs={{16,32},{32,16},{48,64},{64,48},{80,96},{96,80},{17,33},{33,17},{4... | collective-permute-start | bytes 786440 | tf_op jit(solution)/shard_map/ppermute | solution.py:19
  54.1 6.9 %collective-permute-start.2 = (bf16[1024,128]{1,0:T(8,128)(2,1)S(1)}, bf16[1024,128]{1,0:T(8,128)(2,1)S(1)}, u32[]{:S(2)}, u32[]{:S(2)}) collective-permute-start(bf16[1024,128]{1,0:T(8,128)(2,1)S(1)} %get-tuple-element.17), channel_id=1, source_target_pairs={{0,1},{1,0},{2,3},{3,2},{4,5},{5,4},{6,7},{7,6},{8,9},{9,8},{10,11... | collective-permute-start | bytes 786440 | tf_op jit(solution)/shard_map/ppermute | solution.py:19
  54.9 6.1 %collective-permute-start.3 = (bf16[1024,128]{1,0:T(8,128)(2,1)S(1)}, bf16[1024,128]{1,0:T(8,128)(2,1)S(1)}, u32[]{:S(2)}, u32[]{:S(2)}) collective-permute-start(bf16[1024,128]{1,0:T(8,128)(2,1)S(1)} %get-tuple-element.18), channel_id=1, source_target_pairs={{1,2},{2,1},{3,4},{4,3},{5,6},{6,5},{7,8},{8,7},{9,10},{10,9},{11,... | collective-permute-start | bytes 786440 | tf_op jit(solution)/shard_map/ppermute | solution.py:19
  61.0 48.3 %copy-start.6 = (f32[128]{0:T(128)S(1)}, f32[128]{0:T(128)}, u32[]{:S(2)}) copy-start(f32[128]{0:T(128)} %param.12) | copy-start | bytes 1540
  61.0 48.3 %copy-start.7 = (f32[128]{0:T(128)S(1)}, f32[128]{0:T(128)}, u32[]{:S(2)}) copy-start(f32[128]{0:T(128)} %param.13) | copy-start | bytes 1540

commit v6 on v5

--- a/solution.py
+++ b/solution.py
@@ -9,9 +9,10 @@
 
 AXES = ("tx", "ty")
 LANES = 128
-BF16, F32, I32 = jnp.bfloat16, jnp.float32, jnp.int32
+BF16, F32, I32, I16 = jnp.bfloat16, jnp.float32, jnp.int32, jnp.int16
 EMPTY = -1.0
 MIB = 1 << 20
+LANE_TURN = 4
 
 
 def exchanged(value, axis, first):
@@ -137,6 +138,18 @@
     )(kmap)
 
 
+def lane_gather(value, index):
+    numbers = lax.GatherDimensionNumbers(
+        offset_dims=(),
+        collapsed_slice_dims=(1,),
+        start_index_map=(1,),
+        operand_batching_dims=(0,),
+        start_indices_batching_dims=(0,),
+    )
+    mode = lax.GatherScatterMode.PROMISE_IN_BOUNDS
+    return lax.gather(value, index[..., None], numbers, (1, 1), mode=mode)
+
+
 def same_of(channels):
     row = lax.broadcasted_iota(I32, (channels, channels), 0)
     lane = lax.broadcasted_iota(I32, (channels, channels), 1)
@@ -192,7 +205,7 @@
     lane = lax.broadcasted_iota(I32, (channels, LANES), 1)
     right = lane >= block
     half = jnp.where(lax.broadcasted_iota(I32, (1, LANES), 1) >= block, block, 0)
-    rows16 = lax.broadcasted_iota(I32, (LANES, LANES), 0).astype(jnp.int16)
+    rows16 = lax.broadcasted_iota(I32, (LANES, LANES), 0).astype(I16)
     none = jnp.zeros((LANES, LANES), BF16)
 
     def keep(i, carry):
@@ -224,7 +237,7 @@
             at = pl.ds(pl.multiple_of(step * window, window) + p * LANES, LANES)
             listed = kmap[k, :, at]
             local = jnp.where(listed < 0, -1, (listed & (block - 1)) + half)
-            local = jnp.broadcast_to(local, (LANES, LANES)).astype(jnp.int16)
+            local = jnp.broadcast_to(local, (LANES, LANES)).astype(I16)
             return jnp.where(rows16 == local, jnp.ones((), BF16), jnp.zeros((), BF16))
 
         for k in range(offsets):
@@ -233,6 +246,15 @@
                 if k == offsets // 2:
                     for q in (p, p + 1):
                         g[to, q * LANES : (q + 1) * LANES] = xt[blocks * step + 2 * q]
+                    continue
+                if k % LANE_TURN == 0:
+                    for q in (p, p + 1):
+                        at = pl.ds(pl.multiple_of(step * window, window) + q * LANES, LANES)
+                        listed = kmap[k, :, at]
+                        index = jnp.broadcast_to((listed & (block - 1)) + half, (channels, LANES)).astype(I16)
+                        there = jnp.broadcast_to(listed, (channels, LANES)).astype(I16) >= 0
+                        chosen = jnp.where(there, lane_gather(pair_of(k, q), index), jnp.zeros((), BF16))
+                        g[to, q * LANES : (q + 1) * LANES] = chosen
                     continue
                 pairs = jnp.concatenate((pair_of(k, p), pair_of(k, p + 1)), axis=1)
                 chooser = jnp.concatenate(
@@ -353,12 +375,13 @@
     def swap(value):
         return lax.all_to_all(value, AXES, split_axis=0, concat_axis=0, tiled=True)
 
+    odd_row, odd_col = lax.axis_index("tx") % 2, lax.axis_index("ty") % 2
+    ways = jnp.stack((odd_row, 1 - odd_row, 2 + odd_col, 3 - odd_col)).astype(I32)
     outgoing = place(voxels, owner_tile, tile_rows, pair_rows)
+    ways, outgoing = lax.optimization_barrier((ways, outgoing))
     arrival = swap(outgoing.reshape(devices, pair_rows, channels)).reshape(tile_rows, channels)
     kmap = kernel_map.transpose(1, 0, 2)
     source = source_blocks(kmap, block)
-    odd_row, odd_col = lax.axis_index("tx") % 2, lax.axis_index("ty") % 2
-    ways = jnp.stack((odd_row, 1 - odd_row, 2 + odd_col, 3 - odd_col)).astype(I32)
     picked = pick(arrival, rim_blocks[0], ways, block)
     rims = (
         exchanged(picked[0], "tx", 0),

time: 112 us -> 109 us (0.973)
  blocking collectives: 20.2 us -> 61.2 us
  waiting for transfers between devices: 30.4 us -> 0.63 us
  starting transfers between devices: 16.4 us -> 4.9 us
  local copies, waits for them, and re-layouts: 3.28 us -> 1.96 us
  Pallas kernels: 41 us -> 39.8 us
    all_to_all x1 -> x2, blocking collectives: 20.2 us -> 61.2 us  [swap(): return lax.all_to_all(value, AXES, split_axis=0, concat_axis=0, tiled=True)]
    all_to_all x1 -> x0, waiting for transfers between devices: 29.7 us -> none  [swap(): return lax.all_to_all(value, AXES, split_axis=0, concat_axis=0, tiled=True)]
    all_to_all x1 -> x0, starting transfers between devices: 11.5 us -> none  [swap(): return lax.all_to_all(value, AXES, split_axis=0, concat_axis=0, tiled=True)]
    unnamed x16 -> x14, local copies, waits for them, and re-layouts: 3.28 us -> 1.96 us
    pallas_call x1, Pallas kernels: 28.1 us -> 26.8 us  [convolve(): pl.pallas_call(functools.partial(conv_kernel, block, window), in_specs=[p...]
  transfers between devices with their start and end apart: 5 -> 4, of which waited for: 2 -> 1; matrix products, arithmetic and copies ran while one was open for 0% -> 0% of each run, Pallas kernels for 4% -> 4%
where the time goes in v6:
time: 109 us
  blocking collectives  61.2 us (56%)
  Pallas kernels  39.8 us (37%)
  starting transfers between devices  4.9 us (4%)
  local copies, waits for them, and re-layouts  1.96 us (2%)
    all_to_all x2, blocking collectives, swap(): return lax.all_to_all(value, AXES, split_axis=0, concat_axis=0, tiled=True)  61.2 us
    pallas_call x1, Pallas kernels, convolve(): pl.pallas_call(functools.partial(conv_kernel, block, window), in_specs=[p...  26.8 us
    pallas_call x1, Pallas kernels, place(): pl.pallas_call(functools.partial(place_kernel, pair_rows), in_specs=[pl.B...  5.42 us
    ppermute x4, starting transfers between devices, exchanged(): lax.ppermute(value, axis, [way for i in pairs for way in ((i, i + 1), (i...  4.9 us
    pallas_call x1, Pallas kernels, turn_local(): pl.pallas_call(functools.partial(turn_kernel, block), out_shape=[jax.Shap...  3.16 us
    pallas_call x1, Pallas kernels, finish(): pl.pallas_call(functools.partial(finish_kernel, population), in_specs=[wh...  2.2 us
  transfers between devices with their start and end apart: 4, of which 1 were waited for; matrix products, arithmetic and copies ran while one was open for 0% of the time, Pallas kernels for 4%

profile of v6, /device:TPU:1, one launch (start us, length us, event | category | flops | bytes accessed | tf_op | source)
XLA Modules:
  0.0 108.7 jit_solution(17365485900731563454)
XLA Ops:
  0.0 0.0 copy-start.1
  0.0 1.2 %copy-done.1 = bf16[4096,128]{1,0:T(8,128)(2,1)S(1)} copy-done((bf16[4096,128]{1,0:T(8,128)(2,1)S(1)}, bf16[4096,128]{1,0:T(8,128)(2,1)}, u32[]{:S(2)}) %copy-start.1) | copy-done | bytes 1048600
  1.2 0.0 copy-start.3
  1.2 0.7 copy-done.3
  1.9 5.4 %place.1 = bf16[8192,128]{1,0:T(8,128)(2,1)S(1)} custom-call(s32[1,4096]{1,0:T(1,128)S(1)} %bitcast.16, bf16[4096,128]{1,0:T(8,128)(2,1)S(1)} %copy-done.1), custom_call_target="tpu_custom_call" | custom-call | tf_op jit(solution)/shard_map/place/pallas_call | solution.py:75
  7.4 0.1 pad_add_fusion.ways
  7.4 0.0 copy-start.4
  7.5 41.1 %all_to_all.10 = bf16[128,64,128]{2,1,0:T(8,128)(2,1)S(1)} all-to-all(bf16[128,64,128]{2,1,0:T(8,128)(2,1)S(1)} %bitcast.13), channel_id=1, replica_groups=mesh['tx'=8,'ty'=16] {'tx','ty'}, dimensions={0} | all-to-all | bytes 4194304 | tf_op jit(solution)/shard_map/all_to_all | solution.py:376
  48.5 0.0 copy-start
  48.5 0.0 copy-start.2
  48.5 0.0 copy-done.4
  48.5 0.7 pick_rims.1
  49.2 1.1 %collective-permute-start = (bf16[1024,128]{1,0:T(8,128)(2,1)S(1)}, bf16[1024,128]{1,0:T(8,128)(2,1)S(1)}, u32[]{:S(2)}, u32[]{:S(2)}) collective-permute-start(bf16[1024,128]{1,0:T(8,128)(2,1)S(1)} %get-tuple-element.19), channel_id=1, source_target_pairs={{0,16},{16,0},{32,48},{48,32},{64,80},{80,64},{96,112},{112,96},{1... | collective-permute-start | bytes 786440 | tf_op jit(solution)/shard_map/ppermute | solution.py:20
  50.3 2.4 %collective-permute-start.1 = (bf16[1024,128]{1,0:T(8,128)(2,1)S(1)}, bf16[1024,128]{1,0:T(8,128)(2,1)S(1)}, u32[]{:S(2)}, u32[]{:S(2)}) collective-permute-start(bf16[1024,128]{1,0:T(8,128)(2,1)S(1)} %get-tuple-element.20), channel_id=1, source_target_pairs={{16,32},{32,16},{48,64},{64,48},{80,96},{96,80},{17,33},{33,17},{4... | collective-permute-start | bytes 786440 | tf_op jit(solution)/shard_map/ppermute | solution.py:20
  52.7 0.8 collective-permute-start.2
  53.4 0.7 collective-permute-start.3
  54.1 0.0 copy-done
  54.1 1.6 %source_blocks.1.source = s32[27,128]{1,0:T(8,128)S(1)} custom-call(s32[27,1,8192]{2,1,0:T(1,128)S(1)} %bitcast.14), custom_call_target="tpu_custom_call" | custom-call | tf_op jit(solution)/shard_map/source_blocks/pallas_call | solution.py:133
  55.7 0.0 copy-done.2
  55.8 3.2 %turn_local.1 = (bf16[128,128,128]{2,1,0:T(8,128)(2,1)S(1)}, f32[1,8192]{1,0:T(1,128)S(1)}, bf16[128,3456]{1,0:T(8,128)(2,1)S(1)}) custom-call(bf16[8192,128]{1,0:T(8,128)(2,1)S(1)} %bitcast.12, bf16[27,128,128]{2,1,0:T(8,128)(2,1)S(1)} %copy-done.2), custom_call_target="tpu_custom_call" | custom-call | tf_op jit(solution)/shard_map/turn_local/pallas_call | solution.py:189
  58.9 0.0 collective-permute-done.rim0
  58.9 0.0 collective-permute-done.1.rim1
  58.9 0.6 collective-permute-done.2.rim2
  59.6 0.0 collective-permute-done.3.rim3
  59.6 0.0 copy-start.5
  59.6 0.0 copy-start.6
  59.6 26.8 %convolve.1 = (f32[128,8192]{1,0:T(8,128)S(1)}, f32[128,1,384]{2,1,0:T(1,128)S(1)}) custom-call(s32[27,128]{1,0:T(8,128)S(1)} %source_blocks.1.source, s32[4]{0:T(128)S(1)} %pad_add_fusion.ways, s32[27,1,8192]{2,1,0:T(1,128)S(1)} %bitcast.15, bf16[128,128,128]{2,1,0:T(8,128)(2,1)S(1)} %get-tuple-element.18.xt_local, ...), custom_call_target="tpu_custom_call" | custom-call | tf_op jit(solution)/shard_map/convolve/pallas_call | solution.py:306
  86.4 20.2 %all_to_all.11.stats = f32[128,1,384]{2,1,0:T(1,128)S(1)} all-to-all(f32[128,1,384]{2,1,0:T(1,128)S(1)} %get-tuple-element.25), channel_id=1, replica_groups=mesh['tx'=8,'ty'=16] {'tx','ty'}, dimensions={0} | all-to-all | bytes 393216 | tf_op jit(solution)/shard_map/all_to_all | solution.py:376
  106.5 0.0 copy-done.5
  106.5 0.0 copy-done.6
  106.5 2.2 %finish.1 = bf16[8192,128]{1,0:T(8,128)(2,1)} custom-call(f32[128,1,384]{2,1,0:T(1,128)S(1)} %all_to_all.11.stats, f32[1,128]{1,0:T(1,128)S(1)} %bitcast.18, f32[1,128]{1,0:T(1,128)S(1)} %bitcast.19, f32[128,8192]{1,0:T(8,128)S(1)} %get-tuple-element.26.resp, f32[1,8192]{1,0:T(1,128)S(1)} %get-tuple-element.24.occ), custom_call_target="tpu_custom_call" | custom-call | tf_op jit(solution)/shard_map/finish/pallas_call | solution.py:357
Async XLA Ops:
  0.0 1.2 %copy-start.1 = (bf16[4096,128]{1,0:T(8,128)(2,1)S(1)}, bf16[4096,128]{1,0:T(8,128)(2,1)}, u32[]{:S(2)}) copy-start(bf16[4096,128]{1,0:T(8,128)(2,1)} %voxels.1) | copy-start | bytes 3145732
  1.2 0.7 copy-start.3
  7.4 41.1 %copy-start.4 = (s32[1,4,16]{2,1,0:T(4,128)S(1)}, s32[1,4,16]{2,1,0:T(4,128)}, u32[]{:S(2)}) copy-start(s32[1,4,16]{2,1,0:T(4,128)} %param.9) | copy-start | bytes 772
  48.5 5.6 %copy-start = (s32[1,27,8192]{2,0,1:T(1,128)S(1)}, s32[1,27,8192]{2,0,1:T(1,128)}, u32[]{:S(2)}) copy-start(s32[1,27,8192]{2,0,1:T(1,128)} %param.10) | copy-start | bytes 2654212
  48.5 7.2 %copy-start.2 = (bf16[27,128,128]{2,1,0:T(8,128)(2,1)S(1)}, bf16[27,128,128]{2,1,0:T(8,128)(2,1)}, u32[]{:S(2)}) copy-start(bf16[27,128,128]{2,1,0:T(8,128)(2,1)} %weights.1) | copy-start | bytes 2654212
  49.2 9.7 %collective-permute-start = (bf16[1024,128]{1,0:T(8,128)(2,1)S(1)}, bf16[1024,128]{1,0:T(8,128)(2,1)S(1)}, u32[]{:S(2)}, u32[]{:S(2)}) collective-permute-start(bf16[1024,128]{1,0:T(8,128)(2,1)S(1)} %get-tuple-element.19), channel_id=1, source_target_pairs={{0,16},{16,0},{32,48},{48,32},{64,80},{80,64},{96,112},{112,96},{1... | collective-permute-start | bytes 786440 | tf_op jit(solution)/shard_map/ppermute | solution.py:20
  50.3 8.6 %collective-permute-start.1 = (bf16[1024,128]{1,0:T(8,128)(2,1)S(1)}, bf16[1024,128]{1,0:T(8,128)(2,1)S(1)}, u32[]{:S(2)}, u32[]{:S(2)}) collective-permute-start(bf16[1024,128]{1,0:T(8,128)(2,1)S(1)} %get-tuple-element.20), channel_id=1, source_target_pairs={{16,32},{32,16},{48,64},{64,48},{80,96},{96,80},{17,33},{33,17},{4... | collective-permute-start | bytes 786440 | tf_op jit(solution)/shard_map/ppermute | solution.py:20
  52.7 6.9 %collective-permute-start.2 = (bf16[1024,128]{1,0:T(8,128)(2,1)S(1)}, bf16[1024,128]{1,0:T(8,128)(2,1)S(1)}, u32[]{:S(2)}, u32[]{:S(2)}) collective-permute-start(bf16[1024,128]{1,0:T(8,128)(2,1)S(1)} %get-tuple-element.21), channel_id=1, source_target_pairs={{0,1},{1,0},{2,3},{3,2},{4,5},{5,4},{6,7},{7,6},{8,9},{9,8},{10,11... | collective-permute-start | bytes 786440 | tf_op jit(solution)/shard_map/ppermute | solution.py:20
  53.4 6.1 %collective-permute-start.3 = (bf16[1024,128]{1,0:T(8,128)(2,1)S(1)}, bf16[1024,128]{1,0:T(8,128)(2,1)S(1)}, u32[]{:S(2)}, u32[]{:S(2)}) collective-permute-start(bf16[1024,128]{1,0:T(8,128)(2,1)S(1)} %get-tuple-element.22), channel_id=1, source_target_pairs={{1,2},{2,1},{3,4},{4,3},{5,6},{6,5},{7,8},{8,7},{9,10},{10,9},{11,... | collective-permute-start | bytes 786440 | tf_op jit(solution)/shard_map/ppermute | solution.py:20
  59.6 47.0 %copy-start.5 = (f32[128]{0:T(128)S(1)}, f32[128]{0:T(128)}, u32[]{:S(2)}) copy-start(f32[128]{0:T(128)} %param.12) | copy-start | bytes 1540
  59.6 47.0 %copy-start.6 = (f32[128]{0:T(128)S(1)}, f32[128]{0:T(128)}, u32[]{:S(2)}) copy-start(f32[128]{0:T(128)} %param.13) | copy-start | bytes 1540

commit v7 on v6

--- a/solution.py
+++ b/solution.py
@@ -12,7 +12,8 @@
 BF16, F32, I32, I16 = jnp.bfloat16, jnp.float32, jnp.int32, jnp.int16
 EMPTY = -1.0
 MIB = 1 << 20
-LANE_TURN = 4
+REGION = 8
+LANE_TURN = 6
 
 
 def exchanged(value, axis, first):
@@ -59,10 +60,15 @@
 
     copy.wait()
 
-    @pl.loop(0, rows // LANES)
-    def _(line):
-        for u in range(LANES):
-            slots[pl.ds(addr_s[line, u], 1), :] = wide[pl.ds(line * LANES + u, 1), :]
+    lines = rows // LANES
+    for first in range(0, lines, REGION):
+
+        @pl.when(addr_s[first, 0] >= 0)
+        def _():
+            for line in range(first, min(first + REGION, lines)):
+                for u in range(LANES):
+                    row = line * LANES + u
+                    slots[pl.ds(addr_s[line, u], 1), :] = wide[row : row + 1, :]
 
     @pl.loop(0, out.shape[0] // chunk)
     def _(i):

time: 109 us -> 107 us (0.982)
  Pallas kernels: 39.8 us -> 38.2 us
    pallas_call x1, Pallas kernels: 5.42 us -> 4.22 us  [place(): pl.pallas_call(functools.partial(place_kernel, pair_rows), in_specs=[pl.B...]
where the time goes in v7:
time: 107 us
  blocking collectives  61.2 us (57%)
  Pallas kernels  38.2 us (36%)
  starting transfers between devices  4.9 us (5%)
  local copies, waits for them, and re-layouts  1.96 us (2%)
    all_to_all x2, blocking collectives, swap(): return lax.all_to_all(value, AXES, split_axis=0, concat_axis=0, tiled=True)  61.2 us
    pallas_call x1, Pallas kernels, convolve(): pl.pallas_call(functools.partial(conv_kernel, block, window), in_specs=[p...  26.3 us
    ppermute x4, starting transfers between devices, exchanged(): lax.ppermute(value, axis, [way for i in pairs for way in ((i, i + 1), (i...  4.9 us
    pallas_call x1, Pallas kernels, place(): pl.pallas_call(functools.partial(place_kernel, pair_rows), in_specs=[pl.B...  4.22 us
    pallas_call x1, Pallas kernels, turn_local(): pl.pallas_call(functools.partial(turn_kernel, block), out_shape=[jax.Shap...  3.16 us
    pallas_call x1, Pallas kernels, finish(): pl.pallas_call(functools.partial(finish_kernel, population), in_specs=[wh...  2.2 us
  transfers between devices with their start and end apart: 4, of which 1 were waited for; matrix products, arithmetic and copies ran while one was open for 0% of the time, Pallas kernels for 4%

profile of v7, /device:TPU:1, one launch (start us, length us, event | category | flops | bytes accessed | tf_op | source)
XLA Modules:
  0.0 107.1 jit_solution(9488675147989043260)
XLA Ops:
  0.0 0.0 copy-start.1
  0.0 1.2 %copy-done.1 = bf16[4096,128]{1,0:T(8,128)(2,1)S(1)} copy-done((bf16[4096,128]{1,0:T(8,128)(2,1)S(1)}, bf16[4096,128]{1,0:T(8,128)(2,1)}, u32[]{:S(2)}) %copy-start.1) | copy-done | bytes 1048600
  1.2 0.0 copy-start.3
  1.2 0.7 copy-done.3
  1.9 4.2 %place.1 = bf16[8192,128]{1,0:T(8,128)(2,1)S(1)} custom-call(s32[1,4096]{1,0:T(1,128)S(1)} %bitcast.16, bf16[4096,128]{1,0:T(8,128)(2,1)S(1)} %copy-done.1), custom_call_target="tpu_custom_call" | custom-call | tf_op jit(solution)/shard_map/place/pallas_call | solution.py:81
  6.2 0.1 pad_add_fusion.ways
  6.3 0.0 copy-start.4
  6.3 41.1 %all_to_all.10 = bf16[128,64,128]{2,1,0:T(8,128)(2,1)S(1)} all-to-all(bf16[128,64,128]{2,1,0:T(8,128)(2,1)S(1)} %bitcast.13), channel_id=1, replica_groups=mesh['tx'=8,'ty'=16] {'tx','ty'}, dimensions={0} | all-to-all | bytes 4194304 | tf_op jit(solution)/shard_map/all_to_all | solution.py:382
  47.3 0.0 copy-start
  47.3 0.0 copy-start.2
  47.3 0.0 copy-done.4
  47.3 0.7 pick_rims.1
  48.0 1.1 %collective-permute-start = (bf16[1024,128]{1,0:T(8,128)(2,1)S(1)}, bf16[1024,128]{1,0:T(8,128)(2,1)S(1)}, u32[]{:S(2)}, u32[]{:S(2)}) collective-permute-start(bf16[1024,128]{1,0:T(8,128)(2,1)S(1)} %get-tuple-element.19), channel_id=1, source_target_pairs={{0,16},{16,0},{32,48},{48,32},{64,80},{80,64},{96,112},{112,96},{1... | collective-permute-start | bytes 786440 | tf_op jit(solution)/shard_map/ppermute | solution.py:21
  49.1 2.4 %collective-permute-start.1 = (bf16[1024,128]{1,0:T(8,128)(2,1)S(1)}, bf16[1024,128]{1,0:T(8,128)(2,1)S(1)}, u32[]{:S(2)}, u32[]{:S(2)}) collective-permute-start(bf16[1024,128]{1,0:T(8,128)(2,1)S(1)} %get-tuple-element.20), channel_id=1, source_target_pairs={{16,32},{32,16},{48,64},{64,48},{80,96},{96,80},{17,33},{33,17},{4... | collective-permute-start | bytes 786440 | tf_op jit(solution)/shard_map/ppermute | solution.py:21
  51.5 0.8 collective-permute-start.2
  52.2 0.7 collective-permute-start.3
  52.9 0.0 copy-done
  52.9 1.6 %source_blocks.1.source = s32[27,128]{1,0:T(8,128)S(1)} custom-call(s32[27,1,8192]{2,1,0:T(1,128)S(1)} %bitcast.14), custom_call_target="tpu_custom_call" | custom-call | tf_op jit(solution)/shard_map/source_blocks/pallas_call | solution.py:139
  54.5 0.0 copy-done.2
  54.6 3.2 %turn_local.1 = (bf16[128,128,128]{2,1,0:T(8,128)(2,1)S(1)}, f32[1,8192]{1,0:T(1,128)S(1)}, bf16[128,3456]{1,0:T(8,128)(2,1)S(1)}) custom-call(bf16[8192,128]{1,0:T(8,128)(2,1)S(1)} %bitcast.12, bf16[27,128,128]{2,1,0:T(8,128)(2,1)S(1)} %copy-done.2), custom_call_target="tpu_custom_call" | custom-call | tf_op jit(solution)/shard_map/turn_local/pallas_call | solution.py:195
  57.7 0.0 collective-permute-done.rim0
  57.7 0.0 collective-permute-done.1.rim1
  57.7 0.6 collective-permute-done.2.rim2
  58.4 0.0 collective-permute-done.3.rim3
  58.4 0.0 copy-start.5
  58.4 0.0 copy-start.6
  58.4 26.3 %convolve.1 = (f32[128,8192]{1,0:T(8,128)S(1)}, f32[128,1,384]{2,1,0:T(1,128)S(1)}) custom-call(s32[27,128]{1,0:T(8,128)S(1)} %source_blocks.1.source, s32[4]{0:T(128)S(1)} %pad_add_fusion.ways, s32[27,1,8192]{2,1,0:T(1,128)S(1)} %bitcast.15, bf16[128,128,128]{2,1,0:T(8,128)(2,1)S(1)} %get-tuple-element.18.xt_local, ...), custom_call_target="tpu_custom_call" | custom-call | tf_op jit(solution)/shard_map/convolve/pallas_call | solution.py:312
  84.7 20.2 %all_to_all.11.stats = f32[128,1,384]{2,1,0:T(1,128)S(1)} all-to-all(f32[128,1,384]{2,1,0:T(1,128)S(1)} %get-tuple-element.25), channel_id=1, replica_groups=mesh['tx'=8,'ty'=16] {'tx','ty'}, dimensions={0} | all-to-all | bytes 393216 | tf_op jit(solution)/shard_map/all_to_all | solution.py:382
  104.9 0.0 copy-done.5
  104.9 0.0 copy-done.6
  104.9 2.2 %finish.1 = bf16[8192,128]{1,0:T(8,128)(2,1)} custom-call(f32[128,1,384]{2,1,0:T(1,128)S(1)} %all_to_all.11.stats, f32[1,128]{1,0:T(1,128)S(1)} %bitcast.18, f32[1,128]{1,0:T(1,128)S(1)} %bitcast.19, f32[128,8192]{1,0:T(8,128)S(1)} %get-tuple-element.26.resp, f32[1,8192]{1,0:T(1,128)S(1)} %get-tuple-element.24.occ), custom_call_target="tpu_custom_call" | custom-call | tf_op jit(solution)/shard_map/finish/pallas_call | solution.py:363
Async XLA Ops:
  0.0 1.2 %copy-start.1 = (bf16[4096,128]{1,0:T(8,128)(2,1)S(1)}, bf16[4096,128]{1,0:T(8,128)(2,1)}, u32[]{:S(2)}) copy-start(bf16[4096,128]{1,0:T(8,128)(2,1)} %voxels.1) | copy-start | bytes 3145732
  1.2 0.7 copy-start.3
  6.3 41.1 %copy-start.4 = (s32[1,4,16]{2,1,0:T(4,128)S(1)}, s32[1,4,16]{2,1,0:T(4,128)}, u32[]{:S(2)}) copy-start(s32[1,4,16]{2,1,0:T(4,128)} %param.9) | copy-start | bytes 772
  47.3 5.6 %copy-start = (s32[1,27,8192]{2,0,1:T(1,128)S(1)}, s32[1,27,8192]{2,0,1:T(1,128)}, u32[]{:S(2)}) copy-start(s32[1,27,8192]{2,0,1:T(1,128)} %param.10) | copy-start | bytes 2654212
  47.3 7.2 %copy-start.2 = (bf16[27,128,128]{2,1,0:T(8,128)(2,1)S(1)}, bf16[27,128,128]{2,1,0:T(8,128)(2,1)}, u32[]{:S(2)}) copy-start(bf16[27,128,128]{2,1,0:T(8,128)(2,1)} %weights.1) | copy-start | bytes 2654212
  48.0 9.7 %collective-permute-start = (bf16[1024,128]{1,0:T(8,128)(2,1)S(1)}, bf16[1024,128]{1,0:T(8,128)(2,1)S(1)}, u32[]{:S(2)}, u32[]{:S(2)}) collective-permute-start(bf16[1024,128]{1,0:T(8,128)(2,1)S(1)} %get-tuple-element.19), channel_id=1, source_target_pairs={{0,16},{16,0},{32,48},{48,32},{64,80},{80,64},{96,112},{112,96},{1... | collective-permute-start | bytes 786440 | tf_op jit(solution)/shard_map/ppermute | solution.py:21
  49.1 8.6 %collective-permute-start.1 = (bf16[1024,128]{1,0:T(8,128)(2,1)S(1)}, bf16[1024,128]{1,0:T(8,128)(2,1)S(1)}, u32[]{:S(2)}, u32[]{:S(2)}) collective-permute-start(bf16[1024,128]{1,0:T(8,128)(2,1)S(1)} %get-tuple-element.20), channel_id=1, source_target_pairs={{16,32},{32,16},{48,64},{64,48},{80,96},{96,80},{17,33},{33,17},{4... | collective-permute-start | bytes 786440 | tf_op jit(solution)/shard_map/ppermute | solution.py:21
  51.5 6.9 %collective-permute-start.2 = (bf16[1024,128]{1,0:T(8,128)(2,1)S(1)}, bf16[1024,128]{1,0:T(8,128)(2,1)S(1)}, u32[]{:S(2)}, u32[]{:S(2)}) collective-permute-start(bf16[1024,128]{1,0:T(8,128)(2,1)S(1)} %get-tuple-element.21), channel_id=1, source_target_pairs={{0,1},{1,0},{2,3},{3,2},{4,5},{5,4},{6,7},{7,6},{8,9},{9,8},{10,11... | collective-permute-start | bytes 786440 | tf_op jit(solution)/shard_map/ppermute | solution.py:21
  52.2 6.1 %collective-permute-start.3 = (bf16[1024,128]{1,0:T(8,128)(2,1)S(1)}, bf16[1024,128]{1,0:T(8,128)(2,1)S(1)}, u32[]{:S(2)}, u32[]{:S(2)}) collective-permute-start(bf16[1024,128]{1,0:T(8,128)(2,1)S(1)} %get-tuple-element.22), channel_id=1, source_target_pairs={{1,2},{2,1},{3,4},{4,3},{5,6},{6,5},{7,8},{8,7},{9,10},{10,9},{11,... | collective-permute-start | bytes 786440 | tf_op jit(solution)/shard_map/ppermute | solution.py:21
  58.4 46.5 %copy-start.5 = (f32[128]{0:T(128)S(1)}, f32[128]{0:T(128)}, u32[]{:S(2)}) copy-start(f32[128]{0:T(128)} %param.12) | copy-start | bytes 1540
  58.4 46.5 %copy-start.6 = (f32[128]{0:T(128)S(1)}, f32[128]{0:T(128)}, u32[]{:S(2)}) copy-start(f32[128]{0:T(128)} %param.13) | copy-start | bytes 1540

commit v8 on v7

--- a/solution.py
+++ b/solution.py
@@ -122,26 +122,27 @@
 
 
 def source_kernel(block, kmap, out):
-    offsets, tile_rows = kmap.shape[0], kmap.shape[2]
-    lane = lax.broadcasted_iota(I32, (offsets, LANES), 1)
+    offsets, pairs, _ = kmap.shape
+    lane = lax.broadcasted_iota(I32, (pairs, LANES), 1)
     right = lane >= block
-    found = jnp.zeros((offsets, LANES), I32)
-    for p in range(tile_rows // LANES):
-        listed = kmap[:, 0, p * LANES : (p + 1) * LANES]
+    found = jnp.zeros((pairs, LANES), I32)
+    for k in range(offsets):
+        listed = kmap[k]
         for half, mine in enumerate((jnp.logical_not(right), right)):
             top = jnp.max(jnp.where(mine, listed, 0), axis=1, keepdims=True)
-            found = jnp.where(lane == 2 * p + half, top, found)
+            found = jnp.where(lane == 2 * k + half, top, found)
     out[...] = found // block
 
 
 def source_blocks(kmap, block):
     offsets, _, tile_rows = kmap.shape
+    pairs = tile_rows // LANES
     return pl.pallas_call(
         functools.partial(source_kernel, block),
-        out_shape=jax.ShapeDtypeStruct((offsets, tile_rows // block), I32),
+        out_shape=jax.ShapeDtypeStruct((pairs, LANES), I32),
         compiler_params=pltpu.CompilerParams(vmem_limit_bytes=16 * MIB),
         name="source_blocks",
-    )(kmap)
+    )(kmap.reshape(offsets, pairs, LANES))
 
 
 def lane_gather(value, index):
@@ -184,7 +185,7 @@
         xt[2 * p + 1] = both[:, LANES:]
         return carry
 
-    lax.fori_loop(0, arrival.shape[0] // LANES, turn, 0, unroll=8)
+    lax.fori_loop(0, arrival.shape[0] // LANES, turn, 0, unroll=16)
     for k in range(weights.shape[0]):
         weights_t[:, k * channels : (k + 1) * channels] = turned(same, weights[k]).astype(BF16)
 
@@ -235,8 +236,9 @@
 
     def convolve_window(step, total):
         def pair_of(k, p):
-            left_block = source[k, blocks * step + 2 * p]
-            right_block = source[k, blocks * step + 2 * p + 1]
+            line = blocks // 2 * step + p
+            left_block = source[line, 2 * k]
+            right_block = source[line, 2 * k + 1]
             return jnp.where(right, xt[right_block ^ 1], xt[left_block])
 
         def chooser_of(k, p):

time: 107 us -> 107 us (level)
  Pallas kernels: 38.2 us -> 36.7 us
  waiting for transfers between devices: 0.63 us -> 1.77 us
    ppermute x4, waiting for transfers between devices: 0.63 us -> 1.77 us  [exchanged(): lax.ppermute(value, axis, [way for i in pairs for way in ((i, i + 1), (i...]
  transfers between devices with their start and end apart: 4 -> 4, of which waited for: 1 -> 2; matrix products, arithmetic and copies ran while one was open for 0% -> 0% of each run, Pallas kernels for 4% -> 3%
where the time goes in v8:
time: 107 us
  blocking collectives  61.2 us (57%)
  Pallas kernels  36.7 us (34%)
  starting transfers between devices  4.9 us (5%)
  local copies, waits for them, and re-layouts  1.96 us (2%)
  waiting for transfers between devices  1.77 us (2%)
    all_to_all x2, blocking collectives, swap(): return lax.all_to_all(value, AXES, split_axis=0, concat_axis=0, tiled=True)  61.2 us
    pallas_call x1, Pallas kernels, convolve(): pl.pallas_call(functools.partial(conv_kernel, block, window), in_specs=[p...  25.9 us
    ppermute x4, starting transfers between devices, exchanged(): lax.ppermute(value, axis, [way for i in pairs for way in ((i, i + 1), (i...  4.9 us
    pallas_call x1, Pallas kernels, place(): pl.pallas_call(functools.partial(place_kernel, pair_rows), in_specs=[pl.B...  4.22 us
    pallas_call x1, Pallas kernels, turn_local(): pl.pallas_call(functools.partial(turn_kernel, block), out_shape=[jax.Shap...  2.5 us
    pallas_call x1, Pallas kernels, finish(): pl.pallas_call(functools.partial(finish_kernel, population), in_specs=[wh...  2.2 us
  transfers between devices with their start and end apart: 4, of which 2 were waited for; matrix products, arithmetic and copies ran while one was open for 0% of the time, Pallas kernels for 3%

profile of v8, /device:TPU:1, one launch (start us, length us, event | category | flops | bytes accessed | tf_op | source)
XLA Modules:
  0.0 106.7 jit_solution(437950775447488235)
XLA Ops:
  0.0 0.0 copy-start.1
  0.0 1.2 %copy-done.1 = bf16[4096,128]{1,0:T(8,128)(2,1)S(1)} copy-done((bf16[4096,128]{1,0:T(8,128)(2,1)S(1)}, bf16[4096,128]{1,0:T(8,128)(2,1)}, u32[]{:S(2)}) %copy-start.1) | copy-done | bytes 1048600
  1.2 0.0 copy-start.3
  1.2 0.7 copy-done.3
  1.9 4.2 %place.1 = bf16[8192,128]{1,0:T(8,128)(2,1)S(1)} custom-call(s32[1,4096]{1,0:T(1,128)S(1)} %bitcast.17, bf16[4096,128]{1,0:T(8,128)(2,1)S(1)} %copy-done.1), custom_call_target="tpu_custom_call" | custom-call | tf_op jit(solution)/shard_map/place/pallas_call | solution.py:81
  6.2 0.1 pad_add_fusion.ways
  6.3 0.0 copy-start.4
  6.3 41.1 %all_to_all.10 = bf16[128,64,128]{2,1,0:T(8,128)(2,1)S(1)} all-to-all(bf16[128,64,128]{2,1,0:T(8,128)(2,1)S(1)} %bitcast.14), channel_id=1, replica_groups=mesh['tx'=8,'ty'=16] {'tx','ty'}, dimensions={0} | all-to-all | bytes 4194304 | tf_op jit(solution)/shard_map/all_to_all | solution.py:384
  47.3 0.0 copy-start
  47.3 0.0 copy-start.2
  47.3 0.0 copy-done.4
  47.3 0.7 pick_rims.1
  48.0 1.1 %collective-permute-start = (bf16[1024,128]{1,0:T(8,128)(2,1)S(1)}, bf16[1024,128]{1,0:T(8,128)(2,1)S(1)}, u32[]{:S(2)}, u32[]{:S(2)}) collective-permute-start(bf16[1024,128]{1,0:T(8,128)(2,1)S(1)} %get-tuple-element.19), channel_id=1, source_target_pairs={{0,16},{16,0},{32,48},{48,32},{64,80},{80,64},{96,112},{112,96},{1... | collective-permute-start | bytes 786440 | tf_op jit(solution)/shard_map/ppermute | solution.py:21
  49.1 2.4 %collective-permute-start.1 = (bf16[1024,128]{1,0:T(8,128)(2,1)S(1)}, bf16[1024,128]{1,0:T(8,128)(2,1)S(1)}, u32[]{:S(2)}, u32[]{:S(2)}) collective-permute-start(bf16[1024,128]{1,0:T(8,128)(2,1)S(1)} %get-tuple-element.20), channel_id=1, source_target_pairs={{16,32},{32,16},{48,64},{64,48},{80,96},{96,80},{17,33},{33,17},{4... | collective-permute-start | bytes 786440 | tf_op jit(solution)/shard_map/ppermute | solution.py:21
  51.5 0.8 collective-permute-start.2
  52.2 0.7 collective-permute-start.3
  52.9 0.0 copy-done
  52.9 1.1 %source_blocks.1.source = s32[64,128]{1,0:T(8,128)S(1)} custom-call(s32[27,64,128]{2,1,0:T(8,128)S(1)} %bitcast.15), custom_call_target="tpu_custom_call" | custom-call | tf_op jit(solution)/shard_map/source_blocks/pallas_call | solution.py:140
  54.1 0.0 copy-done.2
  54.1 2.5 %turn_local.1 = (bf16[128,128,128]{2,1,0:T(8,128)(2,1)S(1)}, f32[1,8192]{1,0:T(1,128)S(1)}, bf16[128,3456]{1,0:T(8,128)(2,1)S(1)}) custom-call(bf16[8192,128]{1,0:T(8,128)(2,1)S(1)} %bitcast.13, bf16[27,128,128]{2,1,0:T(8,128)(2,1)S(1)} %copy-done.2), custom_call_target="tpu_custom_call" | custom-call | tf_op jit(solution)/shard_map/turn_local/pallas_call | solution.py:196
  56.6 0.0 collective-permute-done.rim0
  56.6 0.5 collective-permute-done.1.rim1
  57.1 1.3 %collective-permute-done.2.rim2 = bf16[1024,128]{1,0:T(8,128)(2,1)S(1)} collective-permute-done((bf16[1024,128]{1,0:T(8,128)(2,1)S(1)}, bf16[1024,128]{1,0:T(8,128)(2,1)S(1)}, u32[]{:S(2)}, u32[]{:S(2)}) %collective-permute-start.2) | collective-permute-done | bytes 262176 | tf_op jit(solution)/shard_map/ppermute | solution.py:21
  58.4 0.0 collective-permute-done.3.rim3
  58.4 0.0 copy-start.5
  58.4 0.0 copy-start.6
  58.4 25.9 %convolve.1 = (f32[128,8192]{1,0:T(8,128)S(1)}, f32[128,1,384]{2,1,0:T(1,128)S(1)}) custom-call(s32[64,128]{1,0:T(8,128)S(1)} %source_blocks.1.source, s32[4]{0:T(128)S(1)} %pad_add_fusion.ways, s32[27,1,8192]{2,1,0:T(1,128)S(1)} %bitcast.16, bf16[128,128,128]{2,1,0:T(8,128)(2,1)S(1)} %get-tuple-element.18.xt_local, ...), custom_call_target="tpu_custom_call" | custom-call | tf_op jit(solution)/shard_map/convolve/pallas_call | solution.py:314
  84.3 20.2 %all_to_all.11.stats = f32[128,1,384]{2,1,0:T(1,128)S(1)} all-to-all(f32[128,1,384]{2,1,0:T(1,128)S(1)} %get-tuple-element.25), channel_id=1, replica_groups=mesh['tx'=8,'ty'=16] {'tx','ty'}, dimensions={0} | all-to-all | bytes 393216 | tf_op jit(solution)/shard_map/all_to_all | solution.py:384
  104.5 0.0 copy-done.5
  104.5 0.0 copy-done.6
  104.5 2.2 %finish.1 = bf16[8192,128]{1,0:T(8,128)(2,1)} custom-call(f32[128,1,384]{2,1,0:T(1,128)S(1)} %all_to_all.11.stats, f32[1,128]{1,0:T(1,128)S(1)} %bitcast.19, f32[1,128]{1,0:T(1,128)S(1)} %bitcast.20, f32[128,8192]{1,0:T(8,128)S(1)} %get-tuple-element.26.resp, f32[1,8192]{1,0:T(1,128)S(1)} %get-tuple-element.24.occ), custom_call_target="tpu_custom_call" | custom-call | tf_op jit(solution)/shard_map/finish/pallas_call | solution.py:365
Async XLA Ops:
  0.0 1.2 %copy-start.1 = (bf16[4096,128]{1,0:T(8,128)(2,1)S(1)}, bf16[4096,128]{1,0:T(8,128)(2,1)}, u32[]{:S(2)}) copy-start(bf16[4096,128]{1,0:T(8,128)(2,1)} %voxels.1) | copy-start | bytes 3145732
  1.2 0.7 copy-start.3
  6.3 41.1 %copy-start.4 = (s32[1,4,16]{2,1,0:T(4,128)S(1)}, s32[1,4,16]{2,1,0:T(4,128)}, u32[]{:S(2)}) copy-start(s32[1,4,16]{2,1,0:T(4,128)} %param.9) | copy-start | bytes 772
  47.3 5.6 %copy-start = (s32[1,27,8192]{2,0,1:T(1,128)S(1)}, s32[1,27,8192]{2,0,1:T(1,128)}, u32[]{:S(2)}) copy-start(s32[1,27,8192]{2,0,1:T(1,128)} %param.10) | copy-start | bytes 2654212
  47.3 6.8 %copy-start.2 = (bf16[27,128,128]{2,1,0:T(8,128)(2,1)S(1)}, bf16[27,128,128]{2,1,0:T(8,128)(2,1)}, u32[]{:S(2)}) copy-start(bf16[27,128,128]{2,1,0:T(8,128)(2,1)} %weights.1) | copy-start | bytes 2654212
  48.0 8.6 %collective-permute-start = (bf16[1024,128]{1,0:T(8,128)(2,1)S(1)}, bf16[1024,128]{1,0:T(8,128)(2,1)S(1)}, u32[]{:S(2)}, u32[]{:S(2)}) collective-permute-start(bf16[1024,128]{1,0:T(8,128)(2,1)S(1)} %get-tuple-element.19), channel_id=1, source_target_pairs={{0,16},{16,0},{32,48},{48,32},{64,80},{80,64},{96,112},{112,96},{1... | collective-permute-start | bytes 786440 | tf_op jit(solution)/shard_map/ppermute | solution.py:21
  49.1 8.0 %collective-permute-start.1 = (bf16[1024,128]{1,0:T(8,128)(2,1)S(1)}, bf16[1024,128]{1,0:T(8,128)(2,1)S(1)}, u32[]{:S(2)}, u32[]{:S(2)}) collective-permute-start(bf16[1024,128]{1,0:T(8,128)(2,1)S(1)} %get-tuple-element.20), channel_id=1, source_target_pairs={{16,32},{32,16},{48,64},{64,48},{80,96},{96,80},{17,33},{33,17},{4... | collective-permute-start | bytes 786440 | tf_op jit(solution)/shard_map/ppermute | solution.py:21
  51.5 6.9 %collective-permute-start.2 = (bf16[1024,128]{1,0:T(8,128)(2,1)S(1)}, bf16[1024,128]{1,0:T(8,128)(2,1)S(1)}, u32[]{:S(2)}, u32[]{:S(2)}) collective-permute-start(bf16[1024,128]{1,0:T(8,128)(2,1)S(1)} %get-tuple-element.21), channel_id=1, source_target_pairs={{0,1},{1,0},{2,3},{3,2},{4,5},{5,4},{6,7},{7,6},{8,9},{9,8},{10,11... | collective-permute-start | bytes 786440 | tf_op jit(solution)/shard_map/ppermute | solution.py:21
  52.2 6.1 %collective-permute-start.3 = (bf16[1024,128]{1,0:T(8,128)(2,1)S(1)}, bf16[1024,128]{1,0:T(8,128)(2,1)S(1)}, u32[]{:S(2)}, u32[]{:S(2)}) collective-permute-start(bf16[1024,128]{1,0:T(8,128)(2,1)S(1)} %get-tuple-element.22), channel_id=1, source_target_pairs={{1,2},{2,1},{3,4},{4,3},{5,6},{6,5},{7,8},{8,7},{9,10},{10,9},{11,... | collective-permute-start | bytes 786440 | tf_op jit(solution)/shard_map/ppermute | solution.py:21
  58.4 46.1 %copy-start.5 = (f32[128]{0:T(128)S(1)}, f32[128]{0:T(128)}, u32[]{:S(2)}) copy-start(f32[128]{0:T(128)} %param.12) | copy-start | bytes 1540
  58.4 46.1 %copy-start.6 = (f32[128]{0:T(128)S(1)}, f32[128]{0:T(128)}, u32[]{:S(2)}) copy-start(f32[128]{0:T(128)} %param.13) | copy-start | bytes 1540

commit v9 on v8

--- a/solution.py
+++ b/solution.py
@@ -391,12 +391,9 @@
     kmap = kernel_map.transpose(1, 0, 2)
     source = source_blocks(kmap, block)
     picked = pick(arrival, rim_blocks[0], ways, block)
-    rims = (
-        exchanged(picked[0], "tx", 0),
-        exchanged(picked[1], "tx", 1),
-        exchanged(picked[2], "ty", 0),
-        exchanged(picked[3], "ty", 1),
-    )
+    rims = [None] * len(picked)
+    for d, axis, first in ((3, "ty", 1), (1, "tx", 1), (2, "ty", 0), (0, "tx", 0)):
+        rims[d] = exchanged(picked[d], axis, first)
     xt, occ, weights_t = turn_local(arrival, weights, block)
     resp, stats = convolve(source, ways, kmap, xt, rims, weights_t, occ, block)
     gathered = swap(stats)

time: 107 us -> 107 us (level)
  no operation moved by 1% of the time
where the time goes in v9:
time: 107 us
  blocking collectives  61.2 us (57%)
  Pallas kernels  36.7 us (34%)
  starting transfers between devices  4.9 us (5%)
  local copies, waits for them, and re-layouts  1.96 us (2%)
  waiting for transfers between devices  1.77 us (2%)
    all_to_all x2, blocking collectives, swap(): return lax.all_to_all(value, AXES, split_axis=0, concat_axis=0, tiled=True)  61.2 us
    pallas_call x1, Pallas kernels, convolve(): pl.pallas_call(functools.partial(conv_kernel, block, window), in_specs=[p...  25.9 us
    ppermute x4, starting transfers between devices, exchanged(): lax.ppermute(value, axis, [way for i in pairs for way in ((i, i + 1), (i...  4.9 us
    pallas_call x1, Pallas kernels, place(): pl.pallas_call(functools.partial(place_kernel, pair_rows), in_specs=[pl.B...  4.22 us
    pallas_call x1, Pallas kernels, turn_local(): pl.pallas_call(functools.partial(turn_kernel, block), out_shape=[jax.Shap...  2.5 us
    pallas_call x1, Pallas kernels, finish(): pl.pallas_call(functools.partial(finish_kernel, population), in_specs=[wh...  2.2 us
  transfers between devices with their start and end apart: 4, of which 2 were waited for; matrix products, arithmetic and copies ran while one was open for 0% of the time, Pallas kernels for 3%

profile of v9, /device:TPU:1, one launch (start us, length us, event | category | flops | bytes accessed | tf_op | source)
XLA Modules:
  0.0 106.7 jit_solution(437950775447488235)
XLA Ops:
  0.0 0.0 copy-start.1
  0.0 1.2 %copy-done.1 = bf16[4096,128]{1,0:T(8,128)(2,1)S(1)} copy-done((bf16[4096,128]{1,0:T(8,128)(2,1)S(1)}, bf16[4096,128]{1,0:T(8,128)(2,1)}, u32[]{:S(2)}) %copy-start.1) | copy-done | bytes 1048600
  1.2 0.0 copy-start.3
  1.2 0.7 copy-done.3
  1.9 4.2 %place.1 = bf16[8192,128]{1,0:T(8,128)(2,1)S(1)} custom-call(s32[1,4096]{1,0:T(1,128)S(1)} %bitcast.17, bf16[4096,128]{1,0:T(8,128)(2,1)S(1)} %copy-done.1), custom_call_target="tpu_custom_call" | custom-call | tf_op jit(solution)/shard_map/place/pallas_call | solution.py:81
  6.2 0.1 pad_add_fusion.ways
  6.3 0.0 copy-start.4
  6.3 41.1 %all_to_all.10 = bf16[128,64,128]{2,1,0:T(8,128)(2,1)S(1)} all-to-all(bf16[128,64,128]{2,1,0:T(8,128)(2,1)S(1)} %bitcast.14), channel_id=1, replica_groups=mesh['tx'=8,'ty'=16] {'tx','ty'}, dimensions={0} | all-to-all | bytes 4194304 | tf_op jit(solution)/shard_map/all_to_all | solution.py:384
  47.3 0.0 copy-start
  47.3 0.0 copy-start.2
  47.3 0.0 copy-done.4
  47.3 0.7 pick_rims.1
  48.0 1.1 %collective-permute-start = (bf16[1024,128]{1,0:T(8,128)(2,1)S(1)}, bf16[1024,128]{1,0:T(8,128)(2,1)S(1)}, u32[]{:S(2)}, u32[]{:S(2)}) collective-permute-start(bf16[1024,128]{1,0:T(8,128)(2,1)S(1)} %get-tuple-element.19), channel_id=1, source_target_pairs={{0,16},{16,0},{32,48},{48,32},{64,80},{80,64},{96,112},{112,96},{1... | collective-permute-start | bytes 786440 | tf_op jit(solution)/shard_map/ppermute | solution.py:21
  49.1 2.4 %collective-permute-start.1 = (bf16[1024,128]{1,0:T(8,128)(2,1)S(1)}, bf16[1024,128]{1,0:T(8,128)(2,1)S(1)}, u32[]{:S(2)}, u32[]{:S(2)}) collective-permute-start(bf16[1024,128]{1,0:T(8,128)(2,1)S(1)} %get-tuple-element.20), channel_id=1, source_target_pairs={{16,32},{32,16},{48,64},{64,48},{80,96},{96,80},{17,33},{33,17},{4... | collective-permute-start | bytes 786440 | tf_op jit(solution)/shard_map/ppermute | solution.py:21
  51.5 0.8 collective-permute-start.2
  52.2 0.7 collective-permute-start.3
  52.9 0.0 copy-done
  52.9 1.1 %source_blocks.1.source = s32[64,128]{1,0:T(8,128)S(1)} custom-call(s32[27,64,128]{2,1,0:T(8,128)S(1)} %bitcast.15), custom_call_target="tpu_custom_call" | custom-call | tf_op jit(solution)/shard_map/source_blocks/pallas_call | solution.py:140
  54.1 0.0 copy-done.2
  54.1 2.5 %turn_local.1 = (bf16[128,128,128]{2,1,0:T(8,128)(2,1)S(1)}, f32[1,8192]{1,0:T(1,128)S(1)}, bf16[128,3456]{1,0:T(8,128)(2,1)S(1)}) custom-call(bf16[8192,128]{1,0:T(8,128)(2,1)S(1)} %bitcast.13, bf16[27,128,128]{2,1,0:T(8,128)(2,1)S(1)} %copy-done.2), custom_call_target="tpu_custom_call" | custom-call | tf_op jit(solution)/shard_map/turn_local/pallas_call | solution.py:196
  56.6 0.0 collective-permute-done.rim0
  56.6 0.5 collective-permute-done.1.rim1
  57.1 1.3 %collective-permute-done.2.rim2 = bf16[1024,128]{1,0:T(8,128)(2,1)S(1)} collective-permute-done((bf16[1024,128]{1,0:T(8,128)(2,1)S(1)}, bf16[1024,128]{1,0:T(8,128)(2,1)S(1)}, u32[]{:S(2)}, u32[]{:S(2)}) %collective-permute-start.2) | collective-permute-done | bytes 262176 | tf_op jit(solution)/shard_map/ppermute | solution.py:21
  58.4 0.0 collective-permute-done.3.rim3
  58.4 0.0 copy-start.5
  58.4 0.0 copy-start.6
  58.4 25.9 %convolve.1 = (f32[128,8192]{1,0:T(8,128)S(1)}, f32[128,1,384]{2,1,0:T(1,128)S(1)}) custom-call(s32[64,128]{1,0:T(8,128)S(1)} %source_blocks.1.source, s32[4]{0:T(128)S(1)} %pad_add_fusion.ways, s32[27,1,8192]{2,1,0:T(1,128)S(1)} %bitcast.16, bf16[128,128,128]{2,1,0:T(8,128)(2,1)S(1)} %get-tuple-element.18.xt_local, ...), custom_call_target="tpu_custom_call" | custom-call | tf_op jit(solution)/shard_map/convolve/pallas_call | solution.py:314
  84.3 20.2 %all_to_all.11.stats = f32[128,1,384]{2,1,0:T(1,128)S(1)} all-to-all(f32[128,1,384]{2,1,0:T(1,128)S(1)} %get-tuple-element.25), channel_id=1, replica_groups=mesh['tx'=8,'ty'=16] {'tx','ty'}, dimensions={0} | all-to-all | bytes 393216 | tf_op jit(solution)/shard_map/all_to_all | solution.py:384
  104.5 0.0 copy-done.5
  104.5 0.0 copy-done.6
  104.5 2.2 %finish.1 = bf16[8192,128]{1,0:T(8,128)(2,1)} custom-call(f32[128,1,384]{2,1,0:T(1,128)S(1)} %all_to_all.11.stats, f32[1,128]{1,0:T(1,128)S(1)} %bitcast.19, f32[1,128]{1,0:T(1,128)S(1)} %bitcast.20, f32[128,8192]{1,0:T(8,128)S(1)} %get-tuple-element.26.resp, f32[1,8192]{1,0:T(1,128)S(1)} %get-tuple-element.24.occ), custom_call_target="tpu_custom_call" | custom-call | tf_op jit(solution)/shard_map/finish/pallas_call | solution.py:365
Async XLA Ops:
  0.0 1.2 %copy-start.1 = (bf16[4096,128]{1,0:T(8,128)(2,1)S(1)}, bf16[4096,128]{1,0:T(8,128)(2,1)}, u32[]{:S(2)}) copy-start(bf16[4096,128]{1,0:T(8,128)(2,1)} %voxels.1) | copy-start | bytes 3145732
  1.2 0.7 copy-start.3
  6.3 41.1 %copy-start.4 = (s32[1,4,16]{2,1,0:T(4,128)S(1)}, s32[1,4,16]{2,1,0:T(4,128)}, u32[]{:S(2)}) copy-start(s32[1,4,16]{2,1,0:T(4,128)} %param.9) | copy-start | bytes 772
  47.3 5.6 %copy-start = (s32[1,27,8192]{2,0,1:T(1,128)S(1)}, s32[1,27,8192]{2,0,1:T(1,128)}, u32[]{:S(2)}) copy-start(s32[1,27,8192]{2,0,1:T(1,128)} %param.10) | copy-start | bytes 2654212
  47.3 6.8 %copy-start.2 = (bf16[27,128,128]{2,1,0:T(8,128)(2,1)S(1)}, bf16[27,128,128]{2,1,0:T(8,128)(2,1)}, u32[]{:S(2)}) copy-start(bf16[27,128,128]{2,1,0:T(8,128)(2,1)} %weights.1) | copy-start | bytes 2654212
  48.0 8.6 %collective-permute-start = (bf16[1024,128]{1,0:T(8,128)(2,1)S(1)}, bf16[1024,128]{1,0:T(8,128)(2,1)S(1)}, u32[]{:S(2)}, u32[]{:S(2)}) collective-permute-start(bf16[1024,128]{1,0:T(8,128)(2,1)S(1)} %get-tuple-element.19), channel_id=1, source_target_pairs={{0,16},{16,0},{32,48},{48,32},{64,80},{80,64},{96,112},{112,96},{1... | collective-permute-start | bytes 786440 | tf_op jit(solution)/shard_map/ppermute | solution.py:21
  49.1 8.0 %collective-permute-start.1 = (bf16[1024,128]{1,0:T(8,128)(2,1)S(1)}, bf16[1024,128]{1,0:T(8,128)(2,1)S(1)}, u32[]{:S(2)}, u32[]{:S(2)}) collective-permute-start(bf16[1024,128]{1,0:T(8,128)(2,1)S(1)} %get-tuple-element.20), channel_id=1, source_target_pairs={{16,32},{32,16},{48,64},{64,48},{80,96},{96,80},{17,33},{33,17},{4... | collective-permute-start | bytes 786440 | tf_op jit(solution)/shard_map/ppermute | solution.py:21
  51.5 6.9 %collective-permute-start.2 = (bf16[1024,128]{1,0:T(8,128)(2,1)S(1)}, bf16[1024,128]{1,0:T(8,128)(2,1)S(1)}, u32[]{:S(2)}, u32[]{:S(2)}) collective-permute-start(bf16[1024,128]{1,0:T(8,128)(2,1)S(1)} %get-tuple-element.21), channel_id=1, source_target_pairs={{0,1},{1,0},{2,3},{3,2},{4,5},{5,4},{6,7},{7,6},{8,9},{9,8},{10,11... | collective-permute-start | bytes 786440 | tf_op jit(solution)/shard_map/ppermute | solution.py:21
  52.2 6.1 %collective-permute-start.3 = (bf16[1024,128]{1,0:T(8,128)(2,1)S(1)}, bf16[1024,128]{1,0:T(8,128)(2,1)S(1)}, u32[]{:S(2)}, u32[]{:S(2)}) collective-permute-start(bf16[1024,128]{1,0:T(8,128)(2,1)S(1)} %get-tuple-element.22), channel_id=1, source_target_pairs={{1,2},{2,1},{3,4},{4,3},{5,6},{6,5},{7,8},{8,7},{9,10},{10,9},{11,... | collective-permute-start | bytes 786440 | tf_op jit(solution)/shard_map/ppermute | solution.py:21
  58.4 46.1 %copy-start.5 = (f32[128]{0:T(128)S(1)}, f32[128]{0:T(128)}, u32[]{:S(2)}) copy-start(f32[128]{0:T(128)} %param.12) | copy-start | bytes 1540
  58.4 46.1 %copy-start.6 = (f32[128]{0:T(128)S(1)}, f32[128]{0:T(128)}, u32[]{:S(2)}) copy-start(f32[128]{0:T(128)} %param.13) | copy-start | bytes 1540
